TPU v7x, 32 devices: a whole 2x2x4 slice. The times are simulated.
32 devices in a mesh: dp: 8 (over z, x), tensor: 4 (over y, core).
Axes of the slice: x: 2, y: 2, z: 4, core: 2. Of those that a mesh axis runs over, the one named last changes fastest.
Arguments:
- embeddings: bfloat16 [4096, 768], P('dp'), may hold values from -4 to 4
- replace_table: bfloat16 [32, 768], replicated, may hold values from -4 to 4
- replace_ids: int32 [4096], P('dp'), may hold values from 0 to 31
- masked: int32 [4096], P('dp'), may hold values 0 or 1
- padding: int32 [4096], P('dp'), may hold values from 0 to 1, as said below
- w_qkv: bfloat16 [2, 768, 2304], P(None, None, 'tensor'), may hold values from -4 to 4
- b_qv: bfloat16 [2, 1536], P(None, 'tensor'), may hold values from -2 to 2
- w_out: bfloat16 [2, 768, 768], P(None, 'tensor'), may hold values from -3.5 to 3.5
- b_out: bfloat16 [2, 768], replicated, may hold values from -3 to 3
- first_gain: bfloat16 [2, 768], replicated, may hold values from 0.25 to 1.75
- first_shift: bfloat16 [2, 768], replicated, may hold values from -3 to 3
- w_in: bfloat16 [2, 768, 3072], P(None, None, 'tensor'), may hold values from -0.21875 to 0.21875
- b_in: bfloat16 [2, 3072], P(None, 'tensor'), may hold values from -3 to 3
- w_down: bfloat16 [2, 3072, 768], P(None, 'tensor'), may hold values from -0.109375 to 0.109375
- b_down: bfloat16 [2, 768], replicated, may hold values from -3 to 3
- second_gain: bfloat16 [2, 768], replicated, may hold values from 0.25 to 1.75
- second_shift: bfloat16 [2, 768], replicated, may hold values from -3 to 3
- cotangent: bfloat16 [4096, 768], P('dp'), may hold values from -6 to 6
Outputs:
- hidden_out: bfloat16 [4096, 768], P('dp')
- grad_embeddings: bfloat16 [4096, 768], P('dp')
- grad_table: float32 [32, 768], replicated
- grad_w_qkv: float32 [2, 768, 2304], P(None, None, 'tensor')
- grad_b_qv: float32 [2, 1536], P(None, 'tensor')
- grad_w_out: float32 [2, 768, 768], P(None, 'tensor')
- grad_b_out: float32 [2, 768], replicated
- grad_first_gain: float32 [2, 768], replicated
- grad_first_shift: float32 [2, 768], replicated
- grad_w_in: float32 [2, 768, 3072], P(None, None, 'tensor')
- grad_b_in: float32 [2, 3072], P(None, 'tensor')
- grad_w_down: float32 [2, 3072, 768], P(None, 'tensor')
- grad_b_down: float32 [2, 768], replicated
- grad_second_gain: float32 [2, 768], replicated
- grad_second_shift: float32 [2, 768], replicated
Inputs may be any that keep to these rules, and one draw needn't show every extreme that they name: `padding`: on each of the 8 pages of 512 tokens the real tokens come first and number 512 // 2 or more.
All inputs are finite; a program needn't handle non-finite values. No bound on the sum of `masked` on one device may be relied on, other than what follows from the above.
Results may differ from a plain program's by a relative error of at most 0.015.
Values sent between devices are 32-bit elements; how exact they have to be, the bound alone decides.
A program may use at most 128 MiB of HBM per device.

v0:
```python
import jax
import jax.numpy as jnp
from jax import lax
from jax.sharding import PartitionSpec as P

HEAD_DIM = 64
LAYERS = 2
PAGE_LEN = 512
REPL = 32


EPSILON = 1e-12


def layer_norm(values, gain, shift):
    average = jnp.mean(values, axis=-1, keepdims=True)
    centered = values - average
    variance = jnp.mean(centered * centered, axis=-1, keepdims=True)
    return centered * lax.rsqrt(variance + EPSILON) * gain + shift


def exact_gelu(values):
    return jax.nn.gelu(values, approximate=False)


def contract_rows(left, right):
    return lax.dot_general(
        left, right, (((0,), (0,)), ((), ())), preferred_element_type=jnp.float32
    )


def contract_cols(left, right):
    return lax.dot_general(
        left, right, (((1,), (1,)), ((), ())), preferred_element_type=jnp.float32
    )


def score_page(page_block, bias_row):
    scores = jnp.einsum(
        "qhd,khd->hqk", page_block[:, :, 0], page_block[:, :, 1], preferred_element_type=jnp.float32
    )
    return scores * HEAD_DIM ** (-0.5) + bias_row[None, None, :]


def page_forward(operands):
    page_block, bias_row = operands
    scores = score_page(page_block, bias_row)
    largest = jnp.max(scores, axis=-1, keepdims=True)
    weights = jnp.exp(scores - largest)
    totals = jnp.sum(weights, axis=-1, keepdims=True)
    probabilities = (weights / totals).astype(jnp.bfloat16)
    attended = jnp.einsum(
        "hqk,khd->qhd", probabilities, page_block[:, :, 2], preferred_element_type=jnp.float32
    )
    return (attended.astype(jnp.bfloat16), (largest + jnp.log(totals))[:, :, 0])


def page_backward(operands):
    page_block, bias_row, log_total, grad_heads = operands
    scores = score_page(page_block, bias_row)
    probabilities = jnp.exp(scores - log_total[:, :, None])
    grad_probs = jnp.einsum(
        "qhd,khd->hqk", grad_heads, page_block[:, :, 2], preferred_element_type=jnp.float32
    )
    grad_values = jnp.einsum(
        "hqk,qhd->khd",
        probabilities.astype(jnp.bfloat16),
        grad_heads,
        preferred_element_type=jnp.float32,
    )
    inner_sum = jnp.sum(probabilities * grad_probs, axis=-1, keepdims=True)
    grad_scores = (probabilities * (grad_probs - inner_sum)).astype(jnp.bfloat16)
    score_scale = HEAD_DIM ** (-0.5)
    grad_queries = (
        jnp.einsum(
            "hqk,khd->qhd", grad_scores, page_block[:, :, 1], preferred_element_type=jnp.float32
        )
        * score_scale
    )
    grad_keys = (
        jnp.einsum(
            "hqk,qhd->khd", grad_scores, page_block[:, :, 0], preferred_element_type=jnp.float32
        )
        * score_scale
    )
    return jnp.stack([grad_queries, grad_keys, grad_values], axis=2)


def forward_layer(inputs_low, bias_rows, params):
    (
        w_qkv,
        b_qv,
        w_out,
        b_out,
        gain_one,
        shift_one,
        w_in,
        b_in,
        w_down,
        b_down,
        gain_two,
        shift_two,
    ) = params
    row_count = inputs_low.shape[0]
    page_count = bias_rows.shape[0]
    local_heads = w_qkv.shape[1] // (3 * HEAD_DIM)
    projected = jnp.dot(inputs_low, w_qkv, preferred_element_type=jnp.float32).reshape(
        row_count, local_heads, 3, HEAD_DIM
    )
    bias_pair = b_qv.astype(jnp.float32).reshape(local_heads, 2, HEAD_DIM)
    bias_full = jnp.stack(
        [bias_pair[:, 0], jnp.zeros_like(bias_pair[:, 0]), bias_pair[:, 1]], axis=1
    )
    packed = (projected + bias_full).astype(jnp.bfloat16)
    attended_heads, log_total = lax.map(
        page_forward, (packed.reshape(page_count, PAGE_LEN, local_heads, 3, HEAD_DIM), bias_rows)
    )
    attended_heads = attended_heads.reshape(row_count, local_heads * HEAD_DIM)
    attended = lax.psum(
        jnp.dot(attended_heads, w_out, preferred_element_type=jnp.float32), "tensor"
    )
    before_one = inputs_low.astype(jnp.float32) + attended + b_out.astype(jnp.float32)
    normed_one = layer_norm(before_one, gain_one.astype(jnp.float32), shift_one.astype(jnp.float32))
    normed_low = normed_one.astype(jnp.bfloat16)
    hidden = jnp.dot(normed_low, w_in, preferred_element_type=jnp.float32) + b_in.astype(
        jnp.float32
    )
    active = exact_gelu(hidden).astype(jnp.bfloat16)
    lowered = lax.psum(jnp.dot(active, w_down, preferred_element_type=jnp.float32), "tensor")
    before_two = normed_one + lowered + b_down.astype(jnp.float32)
    result = layer_norm(before_two, gain_two.astype(jnp.float32), shift_two.astype(jnp.float32))
    return (
        result,
        (packed, attended_heads, log_total, before_one, normed_low, hidden, active, before_two),
    )


def backward_layer(inputs_low, bias_rows, params, saved, grad_result):
    (
        w_qkv,
        b_qv,
        w_out,
        b_out,
        gain_one,
        shift_one,
        w_in,
        b_in,
        w_down,
        b_down,
        gain_two,
        shift_two,
    ) = params
    packed, attended_heads, log_total, before_one, normed_low, hidden, active, before_two = saved
    row_count, local_heads = (packed.shape[0], packed.shape[1])
    page_count = bias_rows.shape[0]
    norm_values, norm_pull = jax.vjp(
        layer_norm, before_two, gain_two.astype(jnp.float32), shift_two.astype(jnp.float32)
    )
    grad_two, grad_gain_two, grad_shift_two = norm_pull(grad_result)
    grad_two_low = grad_two.astype(jnp.bfloat16)
    grad_w_down = contract_rows(active, grad_two_low)
    grad_active = contract_cols(grad_two_low, w_down)
    gelu_values, gelu_pull = jax.vjp(exact_gelu, hidden)
    grad_hidden = gelu_pull(grad_active)[0]
    grad_hidden_low = grad_hidden.astype(jnp.bfloat16)
    grad_w_in = contract_rows(normed_low, grad_hidden_low)
    grad_normed = grad_two + lax.psum(contract_cols(grad_hidden_low, w_in), "tensor")
    first_values, first_pull = jax.vjp(
        layer_norm, before_one, gain_one.astype(jnp.float32), shift_one.astype(jnp.float32)
    )
    grad_one, grad_gain_one, grad_shift_one = first_pull(grad_normed)
    grad_one_low = grad_one.astype(jnp.bfloat16)
    grad_w_out = contract_rows(attended_heads, grad_one_low)
    grad_heads = (
        contract_cols(grad_one_low, w_out)
        .astype(jnp.bfloat16)
        .reshape(page_count, PAGE_LEN, local_heads, HEAD_DIM)
    )
    grad_packed = lax.map(
        page_backward,
        (
            packed.reshape(page_count, PAGE_LEN, local_heads, 3, HEAD_DIM),
            bias_rows,
            log_total,
            grad_heads,
        ),
    )
    grad_packed = grad_packed.reshape(row_count, local_heads, 3, HEAD_DIM)
    grad_b_qv = jnp.sum(grad_packed[:, :, 0::2], axis=0).reshape(-1)
    grad_proj_low = grad_packed.reshape(row_count, -1).astype(jnp.bfloat16)
    grad_w_qkv = contract_rows(inputs_low, grad_proj_low)
    grad_inputs = grad_one + lax.psum(contract_cols(grad_proj_low, w_qkv), "tensor")
    gradients = (
        grad_w_qkv,
        grad_b_qv,
        grad_w_out,
        jnp.sum(grad_one, axis=0),
        grad_gain_one,
        grad_shift_one,
        grad_w_in,
        jnp.sum(grad_hidden, axis=0),
        grad_w_down,
        jnp.sum(grad_two, axis=0),
        grad_gain_two,
        grad_shift_two,
    )
    return (grad_inputs, gradients)


def sum_every(stacked_terms, table_term):
    shared = (
        lax.psum_scatter(stacked_terms[0], "dp", scatter_dimension=1, tiled=True),
        lax.psum_scatter(stacked_terms[1], "dp", scatter_dimension=1, tiled=True),
        lax.psum_scatter(stacked_terms[2], "dp", scatter_dimension=2, tiled=True),
        lax.psum_scatter(stacked_terms[3], "dp", scatter_dimension=1, tiled=True),
        lax.psum_scatter(stacked_terms[4], "dp", scatter_dimension=1, tiled=True),
        lax.psum_scatter(stacked_terms[5], "dp", scatter_dimension=1, tiled=True),
        lax.psum_scatter(stacked_terms[6], "dp", scatter_dimension=1, tiled=True),
        lax.psum_scatter(stacked_terms[7], "dp", scatter_dimension=1, tiled=True),
        lax.psum_scatter(stacked_terms[8], "dp", scatter_dimension=2, tiled=True),
        lax.psum_scatter(stacked_terms[9], "dp", scatter_dimension=1, tiled=True),
        lax.psum_scatter(stacked_terms[10], "dp", scatter_dimension=1, tiled=True),
        lax.psum_scatter(stacked_terms[11], "dp", scatter_dimension=1, tiled=True),
        lax.psum_scatter(table_term, "dp", scatter_dimension=1, tiled=True),
    )
    return (
        lax.all_gather(shared[0], "dp", axis=1, tiled=True),
        lax.all_gather(shared[1], "dp", axis=1, tiled=True),
        lax.all_gather(shared[2], "dp", axis=2, tiled=True),
        lax.all_gather(shared[3], "dp", axis=1, tiled=True),
        lax.all_gather(shared[4], "dp", axis=1, tiled=True),
        lax.all_gather(shared[5], "dp", axis=1, tiled=True),
        lax.all_gather(shared[6], "dp", axis=1, tiled=True),
        lax.all_gather(shared[7], "dp", axis=1, tiled=True),
        lax.all_gather(shared[8], "dp", axis=2, tiled=True),
        lax.all_gather(shared[9], "dp", axis=1, tiled=True),
        lax.all_gather(shared[10], "dp", axis=1, tiled=True),
        lax.all_gather(shared[11], "dp", axis=1, tiled=True),
        lax.all_gather(shared[12], "dp", axis=1, tiled=True),
    )


def on_device(
    embeddings,
    replace_table,
    replace_ids,
    masked,
    padding,
    w_qkv,
    b_qv,
    w_out,
    b_out,
    first_gain,
    first_shift,
    w_in,
    b_in,
    w_down,
    b_down,
    second_gain,
    second_shift,
    cotangent,
):
    live_rows = (masked * padding).astype(jnp.float32)
    choose = (replace_ids[:, None] == jnp.arange(REPL, dtype=jnp.int32)[None, :]).astype(
        jnp.float32
    )
    picked = jnp.dot(
        choose.astype(jnp.bfloat16), replace_table, preferred_element_type=jnp.float32
    ).astype(jnp.bfloat16)
    layer_zero = jnp.where(live_rows[:, None] > 0, picked, embeddings)
    bias_rows = ((padding.astype(jnp.float32) - 1.0) * 10000.0).reshape(-1, PAGE_LEN)
    stacks = (
        w_qkv,
        b_qv,
        w_out,
        b_out,
        first_gain,
        first_shift,
        w_in,
        b_in,
        w_down,
        b_down,
        second_gain,
        second_shift,
    )
    inputs_list = [layer_zero]
    saved_list = []
    for layer_index in range(LAYERS):
        params = tuple((stacked[layer_index] for stacked in stacks))
        result, saved = forward_layer(inputs_list[-1], bias_rows, params)
        saved_list.append(saved)
        inputs_list.append(result.astype(jnp.bfloat16))
    hidden_out = inputs_list[-1]
    grad_inputs = cotangent.astype(jnp.float32) * live_rows[:, None]
    per_layer = [None] * LAYERS
    for layer_index in reversed(range(LAYERS)):
        params = tuple((stacked[layer_index] for stacked in stacks))
        saved = forward_layer(inputs_list[layer_index], bias_rows, params)[1]
        grad_inputs, gradients = backward_layer(
            inputs_list[layer_index], bias_rows, params, saved, grad_inputs
        )
        per_layer[layer_index] = gradients
    grad_embeddings = (grad_inputs * (1.0 - live_rows[:, None])).astype(jnp.bfloat16)
    table_term = lax.dot_general(
        choose,
        grad_inputs * live_rows[:, None],
        (((0,), (0,)), ((), ())),
        precision=lax.Precision.HIGHEST,
        preferred_element_type=jnp.float32,
    )
    stacked_terms = tuple(
        (
            jnp.stack([per_layer[layer_index][member] for layer_index in range(LAYERS)])
            for member in range(12)
        )
    )
    every_result = sum_every(stacked_terms, table_term)
    merged = every_result[:12]
    grad_table = every_result[12]
    return (
        hidden_out,
        grad_embeddings,
        grad_table,
        merged[0],
        merged[1],
        merged[2],
        merged[3],
        merged[4],
        merged[5],
        merged[6],
        merged[7],
        merged[8],
        merged[9],
        merged[10],
        merged[11],
    )


def solution(mesh):
    placed = (
        P("dp", None),
        P(),
        P("dp"),
        P("dp"),
        P("dp"),
        P(None, None, "tensor"),
        P(None, "tensor"),
        P(None, "tensor", None),
        P(),
        P(),
        P(),
        P(None, None, "tensor"),
        P(None, "tensor"),
        P(None, "tensor", None),
        P(),
        P(),
        P(),
        P("dp", None),
    )
    return jax.shard_map(
        on_device,
        mesh=mesh,
        in_specs=placed,
        out_specs=(
            P("dp", None),
            P("dp", None),
            P(),
            P(None, None, "tensor"),
            P(None, "tensor"),
            P(None, "tensor", None),
            P(),
            P(),
            P(),
            P(None, None, "tensor"),
            P(None, "tensor"),
            P(None, "tensor", None),
            P(),
            P(),
            P(),
        ),
        check_vma=False,
    )
```

profile of v0, /device:TPU:0, one launch (start us, length us, event | category | flops | bytes accessed | tf_op | source)
XLA Modules:
  0.0 1759.3 jit_solution(13340556419361851524)
XLA Ops:
  9.0 2.5 fusion.121
  16.9 45.5 %all-reduce.13.cloned.1.call-done = f32[512,768]{1,0:T(8,128)} async-done(((f32[512,768]{1,0:T(8,128)}), f32[512,768]{1,0:T(8,128)}) %all-reduce.13.cloned.1.call-update) | async-done | bytes 1572880 | tf_op jit(solution)/shard_map/psum | solution.py:119
  62.4 2.0 fusion.120
  64.8 5.4 multiply_convert_fusion.4
  73.9 42.3 %all-reduce.15.cloned.1.call-done = f32[512,768]{1,0:T(8,128)} async-done(((f32[512,768]{1,0:T(8,128)}), f32[512,768]{1,0:T(8,128)}) %all-reduce.15.cloned.1.call-update) | async-done | bytes 1572880 | tf_op jit(solution)/shard_map/psum | solution.py:129
  116.2 2.4 fusion.118
  126.6 42.8 %all-reduce.17.cloned.1.call-done = f32[512,768]{1,0:T(8,128)} async-done(((f32[512,768]{1,0:T(8,128)}), f32[512,768]{1,0:T(8,128)}) %all-reduce.17.cloned.1.call-update) | async-done | bytes 1572880 | tf_op jit(solution)/shard_map/psum | solution.py:119
  169.4 2.6 fusion.117
  172.4 5.4 multiply_convert_fusion.3
  178.7 1.9 fusion.48
  180.7 43.0 %all-reduce.19.cloned.1.call-done = f32[512,768]{1,0:T(8,128)} async-done(((f32[512,768]{1,0:T(8,128)}), f32[512,768]{1,0:T(8,128)}) %all-reduce.19.cloned.1.call-update) | async-done | bytes 1572880 | tf_op jit(solution)/shard_map/psum | solution.py:129
  223.8 2.4 fusion.115
  232.8 2.0 fusion.52
  235.3 42.6 %all-reduce.21.cloned.1.call-done = f32[512,768]{1,0:T(8,128)} async-done(((f32[512,768]{1,0:T(8,128)}), f32[512,768]{1,0:T(8,128)}) %all-reduce.21.cloned.1.call-update) | async-done | bytes 1572880 | tf_op jit(solution)/shard_map/psum | solution.py:167
  277.9 3.4 multiply_reduce_fusion.4
  289.8 2.0 fusion.74
  291.9 43.0 %all-reduce.23.cloned.1.call-done = f32[512,768]{1,0:T(8,128)} async-done(((f32[512,768]{1,0:T(8,128)}), f32[512,768]{1,0:T(8,128)}) %all-reduce.23.cloned.1.call-update) | async-done | bytes 1572880 | tf_op jit(solution)/shard_map/psum | solution.py:192
  334.9 3.4 multiply_reduce_fusion.3
  343.1 2.0 fusion.61
  345.3 42.8 %all-reduce.25.cloned.1.call-done = f32[512,768]{1,0:T(8,128)} async-done(((f32[512,768]{1,0:T(8,128)}), f32[512,768]{1,0:T(8,128)}) %all-reduce.25.cloned.1.call-update) | async-done | bytes 1572880 | tf_op jit(solution)/shard_map/psum | solution.py:167
  388.2 3.4 multiply_reduce_fusion.5
  398.8 2.0 fusion.76
  402.9 2.1 copy.112
  404.9 3.4 reshape.323
  408.4 2.1 convolution_bitcast_fusion
  413.0 2.5 pad_maximum_fusion.1
  415.5 8.2 copy.91
  423.7 1.9 convolution_bitcast_fusion.5
  425.6 2.0 pad_maximum_fusion.2
  427.7 7.4 copy.82
  435.4 2.8 convolution_bitcast_fusion.2
  439.2 2.5 pad_maximum_fusion
  451.0 2.7 add_reduce_fusion
  454.8 2.4 fusion.33
  457.2 54.9 %reduce-scatter.38.cloned.1.call-done = f32[96,384]{1,0:T(8,128)} async-done(((f32[768,384]{1,0:T(8,128)}), f32[96,384]{1,0:T(8,128)}) %reduce-scatter.38.cloned.1.call-update) | async-done | bytes 147472
  515.2 277.8 %all-reduce.29.cloned.1.call-done = (f32[2,768,576]{2,0,1:T(2,128)}, f32[2,768,768]{1,0,2:T(2,128)}) async-done(((f32[2,768,576]{2,0,1:T(2,128)}, f32[2,768,768]{1,0,2:T(2,128)}), (f32[2,768,576]{2,0,1:T(2,128)}, f32[2,768,768]{1,0,2:T(2,128)})) %all-reduce.29.cloned.1.call-update) | async-done | bytes 8257552
  794.9 1.9 constant_dynamic-slice_fusion
  796.9 95.0 %reduce-scatter.32.cloned.1.call-done = f32[2,96,768]{2,1,0:T(8,128)} async-done(((f32[2,768,768]{2,1,0:T(8,128)}), f32[2,96,768]{2,1,0:T(8,128)}) %reduce-scatter.32.cloned.1.call-update) | async-done | bytes 589840 | tf_op jit(solution)/shard_map/reduce_scatter | solution.py:218
  892.0 64.6 %reduce-scatter.46.cloned.1.call-done = f32[96,2]{1,0:T(8,128)} async-done(((f32[768,2]{1,0:T(8,128)}), f32[96,2]{1,0:T(8,128)}) %reduce-scatter.46.cloned.1.call-update) | async-done | bytes 784
  957.4 18.6 %all-gather.5 = f32[8,96,2]{1,2,0:T(2,128)S(1)} all-gather(f32[1,96,2]{1,2,0:T(2,128)S(1)} %bitcast.300), channel_id=1, replica_groups=mesh['dp'=8,'tensor'=4] {'dp'}, dimensions={0}, use_global_device_ids=true | all-gather | bytes 6912 | tf_op jit(solution)/shard_map/all_gather | solution.py:234
  976.7 43.9 %reduce-scatter.50.cloned.1.call-done = f32[96,2]{1,0:T(8,128)} async-done(((f32[768,2]{1,0:T(8,128)}), f32[96,2]{1,0:T(8,128)}) %reduce-scatter.50.cloned.1.call-update) | async-done | bytes 784
  1021.5 18.6 %all-gather.7 = f32[8,96,2]{1,2,0:T(2,128)S(1)} all-gather(f32[1,96,2]{1,2,0:T(2,128)S(1)} %bitcast.301), channel_id=1, replica_groups=mesh['dp'=8,'tensor'=4] {'dp'}, dimensions={0}, use_global_device_ids=true | all-gather | bytes 6912 | tf_op jit(solution)/shard_map/all_gather | solution.py:237
  1040.8 43.7 %reduce-scatter.52.cloned.1.call-done = f32[96,2]{1,0:T(8,128)} async-done(((f32[768,2]{1,0:T(8,128)}), f32[96,2]{1,0:T(8,128)}) %reduce-scatter.52.cloned.1.call-update) | async-done | bytes 784
  1085.4 18.6 %all-gather.8 = f32[8,96,2]{1,2,0:T(2,128)S(1)} all-gather(f32[1,96,2]{1,2,0:T(2,128)S(1)} %bitcast.302), channel_id=1, replica_groups=mesh['dp'=8,'tensor'=4] {'dp'}, dimensions={0}, use_global_device_ids=true | all-gather | bytes 6912 | tf_op jit(solution)/shard_map/all_gather | solution.py:238
  1104.6 43.4 %reduce-scatter.36.cloned.1.call-done = f32[48,2]{1,0:T(8,128)} async-done(((f32[384,2]{1,0:T(8,128)}), f32[48,2]{1,0:T(8,128)}) %reduce-scatter.36.cloned.1.call-update) | async-done | bytes 400
  1148.9 18.6 %all-gather.1 = f32[8,48,2]{1,2,0:T(2,128)S(1)} all-gather(f32[1,48,2]{1,2,0:T(2,128)S(1)} %bitcast.303), channel_id=1, replica_groups=mesh['dp'=8,'tensor'=4] {'dp'}, dimensions={0}, use_global_device_ids=true | all-gather | bytes 3456 | tf_op jit(solution)/shard_map/all_gather | solution.py:228
  1168.1 43.8 %reduce-scatter.42.cloned.1.call-done = f32[96,2]{1,0:T(8,128)} async-done(((f32[768,2]{1,0:T(8,128)}), f32[96,2]{1,0:T(8,128)}) %reduce-scatter.42.cloned.1.call-update) | async-done | bytes 784
  1212.8 18.6 %all-gather.3 = f32[8,96,2]{1,2,0:T(2,128)S(1)} all-gather(f32[1,96,2]{1,2,0:T(2,128)S(1)} %bitcast.304), channel_id=1, replica_groups=mesh['dp'=8,'tensor'=4] {'dp'}, dimensions={0}, use_global_device_ids=true | all-gather | bytes 6912 | tf_op jit(solution)/shard_map/all_gather | solution.py:231
  1232.1 43.7 %reduce-scatter.44.cloned.1.call-done = f32[96,2]{1,0:T(8,128)} async-done(((f32[768,2]{1,0:T(8,128)}), f32[96,2]{1,0:T(8,128)}) %reduce-scatter.44.cloned.1.call-update) | async-done | bytes 784
  1276.7 18.6 %all-gather.4 = f32[8,96,2]{1,2,0:T(2,128)S(1)} all-gather(f32[1,96,2]{1,2,0:T(2,128)S(1)} %bitcast.305), channel_id=1, replica_groups=mesh['dp'=8,'tensor'=4] {'dp'}, dimensions={0}, use_global_device_ids=true | all-gather | bytes 6912 | tf_op jit(solution)/shard_map/all_gather | solution.py:232
  1296.0 43.8 %reduce-scatter.48.cloned.1.call-done = f32[96,2]{1,0:T(8,128)} async-done(((f32[768,2]{1,0:T(8,128)}), f32[96,2]{1,0:T(8,128)}) %reduce-scatter.48.cloned.1.call-update) | async-done | bytes 784
  1340.7 18.6 %all-gather.6 = f32[8,96,2]{1,2,0:T(2,128)S(1)} all-gather(f32[1,96,2]{1,2,0:T(2,128)S(1)} %bitcast.306), channel_id=1, replica_groups=mesh['dp'=8,'tensor'=4] {'dp'}, dimensions={0}, use_global_device_ids=true | all-gather | bytes 6912 | tf_op jit(solution)/shard_map/all_gather | solution.py:236
  1359.9 43.9 %reduce-scatter.40.cloned.1.call-done = f32[96,2]{1,0:T(8,128)} async-done(((f32[768,2]{1,0:T(8,128)}), f32[96,2]{1,0:T(8,128)}) %reduce-scatter.40.cloned.1.call-update) | async-done | bytes 784
  1404.7 18.6 %all-gather.2 = f32[8,96,2]{1,2,0:T(2,128)S(1)} all-gather(f32[1,96,2]{1,2,0:T(2,128)S(1)} %bitcast.307), channel_id=1, replica_groups=mesh['dp'=8,'tensor'=4] {'dp'}, dimensions={0}, use_global_device_ids=true | all-gather | bytes 6912 | tf_op jit(solution)/shard_map/all_gather | solution.py:230
  1424.0 43.8 %reduce-scatter.34.cloned.1.call-done = f32[96,32]{1,0:T(8,128)} async-done(((f32[768,32]{1,0:T(8,128)}), f32[96,32]{1,0:T(8,128)}) %reduce-scatter.34.cloned.1.call-update) | async-done | bytes 12304
  1468.6 30.8 %all-gather = f32[8,96,32]{1,2,0:T(8,128)S(1)} all-gather(f32[1,96,32]{1,2,0:T(8,128)S(1)} %bitcast.283), channel_id=1, replica_groups=mesh['dp'=8,'tensor'=4] {'dp'}, dimensions={0}, use_global_device_ids=true | all-gather | bytes 110592 | tf_op jit(solution)/shard_map/all_gather | solution.py:239
  1500.2 13.6 all-gather.16.cloned.1.call-done
  1513.7 3.5 copy.96
  1517.2 68.5 %all-gather.14.cloned.1.call-done = f32[2,768,576]{2,0,1:T(2,128)} async-done(((f32[2,96,576]{2,0,1:T(2,128)}), f32[2,768,576]{2,0,1:T(2,128)}) %all-gather.14.cloned.1.call-update) | async-done | bytes 3538960 | tf_op jit(solution)/shard_map/all_gather | solution.py:227
  1585.8 7.6 copy.95
  1593.4 73.6 %all-gather.20.cloned.1.call-done = f32[2,768,768]{1,0,2:T(2,128)} async-done(((f32[2,768,96]{1,0,2:T(2,128)}), f32[2,768,768]{1,0,2:T(2,128)}) %all-gather.20.cloned.1.call-update) | async-done | bytes 4718608 | tf_op jit(solution)/shard_map/all_gather | solution.py:235
  1667.0 8.1 copy.97
  1675.1 72.2 %all-gather.18.cloned.1.call-done = f32[2,768,768]{2,1,0:T(8,128)} async-done(((f32[2,96,768]{2,1,0:T(8,128)}), f32[2,768,768]{2,1,0:T(8,128)}) %all-gather.18.cloned.1.call-update) | async-done | bytes 4718608 | tf_op jit(solution)/shard_map/all_gather | solution.py:233
  1747.4 4.8 copy.139
  (352 shorter events, 81.9 us)
Async XLA Ops:
  7.2 4.4 copy-start
  7.2 55.2 %all-reduce.13.cloned.1.call-start = ((), (), s32[]{:S(2)}) async-start(), calls=%async_computation.11 | async-start | bytes 3145728 | tf_op jit(solution)/shard_map/psum | solution.py:119
  9.0 2.6 copy-start.50
  9.0 2.6 copy-start.62
  15.1 1.7 copy-start.57
  15.1 1.7 copy-start.58
  16.7 99.5 %all-reduce.15.cloned.1.call-start = ((), (), s32[]{:S(2)}) async-start(), calls=%async_computation.12 | async-start | bytes 3145728 | tf_op jit(solution)/shard_map/psum | solution.py:129
  62.4 2.4 copy-start.67
  64.5 5.8 copy-start.6
  64.8 6.4 copy-start.63
  73.2 96.3 %all-reduce.17.cloned.1.call-start = ((), (), s32[]{:S(2)}) async-start(), calls=%async_computation.13 | async-start | bytes 3145728 | tf_op jit(solution)/shard_map/psum | solution.py:119
  126.4 97.4 %all-reduce.19.cloned.1.call-start = ((), (), s32[]{:S(2)}) async-start(), calls=%async_computation.14 | async-start | bytes 3145728 | tf_op jit(solution)/shard_map/psum | solution.py:129
  169.4 2.9 copy-start.68
  172.0 5.8 copy-start.11
  172.4 6.3 copy-start.64
  180.7 97.2 %all-reduce.21.cloned.1.call-start = ((), (), s32[]{:S(2)}) async-start(), calls=%async_computation.15 | async-start | bytes 3145728 | tf_op jit(solution)/shard_map/psum | solution.py:167
  227.3 2.6 copy-start.78
  228.1 1.8 copy-start.65
  228.1 2.5 copy-start.77
  229.9 2.0 copy-start.15
  230.7 2.2 copy-start.69
  234.8 100.1 %all-reduce.23.cloned.1.call-start = ((), (), s32[]{:S(2)}) async-start(), calls=%async_computation.16 | async-start | bytes 3145728 | tf_op jit(solution)/shard_map/psum | solution.py:192
  277.9 3.4 copy-start.12
  281.3 2.6 copy-start.3
  282.0 2.9 copy-start.13
  282.0 2.1 copy-start.48
  291.8 96.3 %all-reduce.25.cloned.1.call-start = ((), (), s32[]{:S(2)}) async-start(), calls=%async_computation.17 | async-start | bytes 3145728 | tf_op jit(solution)/shard_map/psum | solution.py:167
  334.9 3.4 copy-start.5
  334.9 4.1 copy-start.76
  338.3 1.7 copy-start.66
  338.3 2.7 copy-start.75
  339.0 3.2 copy-start.17
  341.0 2.1 copy-start.70
  345.1 105.8 %all-reduce.27.cloned.1.call-start = ((), (), s32[]{:S(2)}) async-start(), calls=%async_computation.18 | async-start | bytes 3145728 | tf_op jit(solution)/shard_map/psum | solution.py:192
  388.2 3.4 copy-start.7
  392.2 2.3 copy-start.9
  398.7 2.1 copy-start.14
  400.8 111.3 %reduce-scatter.38.cloned.1.call-start = ((), (), s32[]{:S(2)}) async-start(), calls=%async_computation.26 | async-start | bytes 1327104
  404.9 3.4 copy-start.16
  408.3 384.7 %all-reduce.29.cloned.1.call-start = ((), (), s32[]{:S(2)}) async-start(), calls=%async_computation.34 | async-start | bytes 17301504
  408.4 2.1 copy-start.34
  408.4 2.1 copy-start.41
  435.1 3.1 copy-start.8
  435.1 456.8 %reduce-scatter.32.cloned.1.call-start = ((), (), s32[]{:S(2)}) async-start(), calls=%async_computation.21 | async-start | bytes 5308416 | tf_op jit(solution)/shard_map/reduce_scatter | solution.py:218
  435.4 2.8 copy-start.74
  441.8 514.8 %reduce-scatter.46.cloned.1.call-start = ((), (), s32[]{:S(2)}) async-start(), calls=%async_computation.30 | async-start | bytes 442368
  443.1 3.4 copy-start.24
  443.1 3.4 copy-start.30
  443.1 3.4 copy-start.32
  444.4 576.3 %reduce-scatter.50.cloned.1.call-start = ((), (), s32[]{:S(2)}) async-start(), calls=%async_computation.32 | async-start | bytes 442368
  445.4 639.1 %reduce-scatter.52.cloned.1.call-start = ((), (), s32[]{:S(2)}) async-start(), calls=%async_computation.33 | async-start | bytes 442368
  446.5 701.6 %reduce-scatter.36.cloned.1.call-start = ((), (), s32[]{:S(2)}) async-start(), calls=%async_computation.25 | async-start | bytes 221184
  447.8 764.2 %reduce-scatter.42.cloned.1.call-start = ((), (), s32[]{:S(2)}) async-start(), calls=%async_computation.28 | async-start | bytes 442368
  448.8 827.1 %reduce-scatter.44.cloned.1.call-start = ((), (), s32[]{:S(2)}) async-start(), calls=%async_computation.29 | async-start | bytes 442368
  449.8 889.9 %reduce-scatter.48.cloned.1.call-start = ((), (), s32[]{:S(2)}) async-start(), calls=%async_computation.31 | async-start | bytes 442368
  450.9 952.9 %reduce-scatter.40.cloned.1.call-start = ((), (), s32[]{:S(2)}) async-start(), calls=%async_computation.27 | async-start | bytes 442368
  450.9 3.8 copy-start.20
  454.7 59.3 %copy-start.71 = (u32[32]{0:T(128)S(1)}, u32[32]{0:T(128)}, u32[]{:S(2)}) copy-start(u32[32]{0:T(128)} %constant.190) | copy-start | bytes 388
  454.7 1013.0 %reduce-scatter.34.cloned.1.call-start = ((), (), s32[]{:S(2)}) async-start(), calls=%async_computation.24 | async-start | bytes 442368
  457.2 1056.6 %all-gather.16.cloned.1.call-start = ((), (), s32[]{:S(2)}) async-start(), calls=%async_computation.20 | async-start | bytes 1769472 | tf_op jit(solution)/shard_map/all_gather | solution.py:229
  513.9 1071.9 %all-gather.14.cloned.1.call-start = ((), (), s32[]{:S(2)}) async-start(), calls=%async_computation.19 | async-start | bytes 4423680 | tf_op jit(solution)/shard_map/all_gather | solution.py:227
  794.9 872.2 %all-gather.20.cloned.1.call-start = ((), (), s32[]{:S(2)}) async-start(), calls=%async_computation.23 | async-start | bytes 5308416 | tf_op jit(solution)/shard_map/all_gather | solution.py:235
  796.9 950.5 %all-gather.18.cloned.1.call-start = ((), (), s32[]{:S(2)}) async-start(), calls=%async_computation.22 | async-start | bytes 5308416 | tf_op jit(solution)/shard_map/all_gather | solution.py:233
  1747.4 4.8 copy-start.1
  (39 other events, 44.0 us)
Sparse Core Ops, SparseCore 0:
  16.8 45.5 all-reduce.12
  73.3 42.8 all-reduce.14
  126.5 42.9 all-reduce.16
  180.8 42.8 all-reduce.18
  235.0 42.8 all-reduce.20
  291.9 42.9 all-reduce.22
  345.2 42.8 all-reduce.24
  400.9 42.8 all-reduce.26
  447.8 64.2 reduce-scatter.37
  516.5 276.3 all-reduce.28
  797.6 94.2 reduce-scatter.31
  895.4 61.1 reduce-scatter.45
  960.2 60.3 reduce-scatter.49
  1024.1 60.3 reduce-scatter.51
  1087.9 60.0 reduce-scatter.35
  1151.5 60.3 reduce-scatter.41
  1215.4 60.3 reduce-scatter.43
  1279.3 60.4 reduce-scatter.47
  1343.4 60.3 reduce-scatter.39
  1407.3 60.4 reduce-scatter.33
  1470.7 42.9 all-gather.15
  1516.7 68.9 all-gather.13
  1588.7 78.2 all-gather.19
  1669.3 78.0 all-gather.17
where the time goes:
time: 1770 us; the launch traced here: 1760 us
  waiting for transfers between devices  1370 us (77%)
  blocking collectives  180 us (10%)
  local copies, waits for them, and re-layouts  96 us (5%)
  matrix products  51.8 us (3%)
  other arithmetic  40.6 us (2%)
    unnamed x35, waiting for transfers between devices  748 us
    reduce_scatter x1, waiting for transfers between devices, sum_every(): lax.psum_scatter(stacked_terms[6], 'dp', scatter_dimension=1, tiled=True)  95 us
    psum x2, waiting for transfers between devices, forward_layer(): lax.psum(jnp.dot(attended_heads, w_out, preferred_element_type=jnp.float3...  88.3 us
    psum x2, waiting for transfers between devices, backward_layer(): lax.psum(contract_cols(grad_hidden_low, w_in), 'tensor')  85.4 us
    psum x2, waiting for transfers between devices, forward_layer(): lax.psum(jnp.dot(active, w_down, preferred_element_type=jnp.float32), 'te...  85.3 us
    unnamed x194, local copies, waits for them, and re-layouts  77.2 us
    all_gather x1, waiting for transfers between devices, sum_every(): lax.all_gather(shared[8], 'dp', axis=2, tiled=True)  73.6 us
    all_gather x1, waiting for transfers between devices, sum_every(): lax.all_gather(shared[6], 'dp', axis=1, tiled=True)  72.2 us
  transfers between devices with their start and end apart: 24, of which 23 were waited for; matrix products, arithmetic and copies ran while one was open for 5% of the time, Pallas kernels for 0%

commit v1 on v0

--- a/solution.py
+++ b/solution.py
@@ -1,7 +1,13 @@
+import functools
+
 import jax
 import jax.numpy as jnp
 from jax import lax
+from jax.experimental import pallas as pl
+from jax.experimental.pallas import tpu as pltpu
 from jax.sharding import PartitionSpec as P
+
+MESH=pl.DeviceIdType.MESH
 
 HEAD_DIM = 64
 LAYERS = 2
@@ -207,37 +213,145 @@
     return (grad_inputs, gradients)
 
 
-def sum_every(stacked_terms, table_term):
-    shared = (
-        lax.psum_scatter(stacked_terms[0], "dp", scatter_dimension=1, tiled=True),
-        lax.psum_scatter(stacked_terms[1], "dp", scatter_dimension=1, tiled=True),
-        lax.psum_scatter(stacked_terms[2], "dp", scatter_dimension=2, tiled=True),
-        lax.psum_scatter(stacked_terms[3], "dp", scatter_dimension=1, tiled=True),
-        lax.psum_scatter(stacked_terms[4], "dp", scatter_dimension=1, tiled=True),
-        lax.psum_scatter(stacked_terms[5], "dp", scatter_dimension=1, tiled=True),
-        lax.psum_scatter(stacked_terms[6], "dp", scatter_dimension=1, tiled=True),
-        lax.psum_scatter(stacked_terms[7], "dp", scatter_dimension=1, tiled=True),
-        lax.psum_scatter(stacked_terms[8], "dp", scatter_dimension=2, tiled=True),
-        lax.psum_scatter(stacked_terms[9], "dp", scatter_dimension=1, tiled=True),
-        lax.psum_scatter(stacked_terms[10], "dp", scatter_dimension=1, tiled=True),
-        lax.psum_scatter(stacked_terms[11], "dp", scatter_dimension=1, tiled=True),
-        lax.psum_scatter(table_term, "dp", scatter_dimension=1, tiled=True),
-    )
-    return (
-        lax.all_gather(shared[0], "dp", axis=1, tiled=True),
-        lax.all_gather(shared[1], "dp", axis=1, tiled=True),
-        lax.all_gather(shared[2], "dp", axis=2, tiled=True),
-        lax.all_gather(shared[3], "dp", axis=1, tiled=True),
-        lax.all_gather(shared[4], "dp", axis=1, tiled=True),
-        lax.all_gather(shared[5], "dp", axis=1, tiled=True),
-        lax.all_gather(shared[6], "dp", axis=1, tiled=True),
-        lax.all_gather(shared[7], "dp", axis=1, tiled=True),
-        lax.all_gather(shared[8], "dp", axis=2, tiled=True),
-        lax.all_gather(shared[9], "dp", axis=1, tiled=True),
-        lax.all_gather(shared[10], "dp", axis=1, tiled=True),
-        lax.all_gather(shared[11], "dp", axis=1, tiled=True),
-        lax.all_gather(shared[12], "dp", axis=1, tiled=True),
-    )
+WIDTH=768
+UNIT=16
+CHUNK=4*UNIT
+LAG=2
+SLOTS=4*LAG
+KINDS=12
+(TX,TNEAR,TFAR,TA1,TA2,TQ1,TQ2,TTA,TTN,TTM,TTF,TG)=range(KINDS)
+
+class Engine:
+    def __init__(self, chunks, part, total, landing, send, recv, local):
+        self.chunks=chunks; self.part=part; self.total=total; self.landing=landing
+        self.send=send; self.recv=recv; self.local=local
+        d=lax.axis_index("dp"); t=lax.axis_index("tensor")
+        x=lax.rem(d,2); z=lax.rem(lax.div(d,2),4)
+        self.x=x; self.z=z
+        self.mid=jnp.logical_or(z==1,z==2)
+        self.upper=lax.div(z,2)
+        self.peer=(d+1-2*x,t)
+        self.line=(d+2-4*lax.rem(z,2),t)
+        self.cross=(jnp.where(z==1,d+2,d-2),t)
+    def neighbours(self):
+        return self.peer,self.line,self.cross
+    def barrier(self, bar):
+        def sig(dev): pl.semaphore_signal(bar,inc=1,device_id=dev,device_id_type=MESH)
+        sig(self.peer); sig(self.line)
+        pl.when(self.mid)(lambda: sig(self.cross))
+        pl.semaphore_wait(bar,jnp.where(self.mid,3,2))
+    def rows(self,j,unit):
+        return pl.ds(pl.multiple_of(j*CHUNK+unit*UNIT,UNIT),UNIT)
+    def copy(self,kind,j,src,dst,dev):
+        slot=lax.rem(j,SLOTS)
+        return pltpu.make_async_remote_copy(src_ref=src,dst_ref=dst,send_sem=self.send.at[kind,slot],recv_sem=self.recv.at[kind,slot],device_id=dev,device_id_type=MESH)
+    def land(self,kind,j):
+        return self.landing.at[kind,lax.rem(j,SLOTS)]
+    def tick(self,t):
+        K=self.chunks; part=self.part; total=self.total; mid=self.mid; end=jnp.logical_not(mid)
+        mine=self.x; other=1-self.x; near=2+self.upper; far=3-self.upper
+        def at(ref,j,u): return ref.at[self.rows(j,u)]
+        def cx(j): return self.copy(TX,j,at(part,j,other),self.land(TX,j),self.peer)
+        def cnear(j): return self.copy(TNEAR,j,at(part,j,near),self.land(TNEAR,j),self.line)
+        def cfar(j): return self.copy(TFAR,j,at(part,j,far),self.land(TFAR,j),self.line)
+        def ca1(j): return self.copy(TA1,j,at(part,j,mine),self.land(TA1,j),self.line)
+        def ca2(j): return self.copy(TA2,j,at(part,j,mine),self.land(TA2,j),self.cross)
+        def cq1(j): return self.copy(TQ1,j,at(part,j,far),self.land(TQ1,j),self.cross)
+        def cq2(j): return self.copy(TQ2,j,at(part,j,near),self.land(TQ2,j),self.peer)
+        def cta(j): return self.copy(TTA,j,at(part,j,mine),at(total,j,mine),self.line)
+        def ctn(j): return self.copy(TTN,j,at(part,j,near),at(total,j,near),self.line)
+        def ctm(j): return self.copy(TTM,j,at(part,j,near),at(total,j,near),self.cross)
+        def ctf(j): return self.copy(TTF,j,at(total,j,far),at(total,j,far),self.line)
+        def cg(j): return self.copy(TG,j,at(total,j,mine),at(total,j,mine),self.peer)
+        def lc(k,j,u): return pltpu.make_async_copy(at(part,j,u),at(total,j,u),self.local.at[k,lax.rem(j,SLOTS)])
+        def add(j,u,kind):
+            r=self.rows(j,u)
+            part[r,:]=part[r,:]+self.landing[kind,lax.rem(j,SLOTS)]
+        def stage(s,f):
+            j=t-s*LAG
+            @pl.when(jnp.logical_and(j>=0,j<K))
+            def _(): f(j)
+        def s0(j):
+            cx(j).start()
+            @pl.when(end)
+            def _():
+                cnear(j).start(); cfar(j).start()
+        def s1(j):
+            cx(j).wait()
+            add(j,mine,TX)
+            @pl.when(end)
+            def _():
+                ca1(j).start()
+                cnear(j).wait_send(); cfar(j).wait_send()
+            @pl.when(mid)
+            def _():
+                cfar(j).wait_recv(); add(j,far,TFAR); cq1(j).start()
+                cnear(j).wait_recv(); add(j,near,TNEAR)
+        def s2(j):
+            @pl.when(end)
+            def _(): ca1(j).wait_send()
+            @pl.when(mid)
+            def _():
+                ca1(j).wait_recv(); add(j,mine,TA1); ca2(j).start()
+                cq1(j).wait(); add(j,near,TQ1); cq2(j).start()
+        def s3(j):
+            @pl.when(mid)
+            def _():
+                ca2(j).wait(); add(j,mine,TA2); cta(j).start(); lc(0,j,mine).start()
+                cq2(j).wait(); add(j,near,TQ2); ctm(j).start(); ctn(j).start(); lc(1,j,near).start()
+        def s4(j):
+            @pl.when(mid)
+            def _():
+                cta(j).wait_send(); ctn(j).wait_send(); lc(0,j,mine).wait(); lc(1,j,near).wait()
+                cg(j).start()
+                ctm(j).wait(); ctf(j).start()
+            @pl.when(end)
+            def _():
+                cta(j).wait_recv(); cg(j).start(); ctn(j).wait_recv()
+        def s5(j):
+            cg(j).wait()
+            pl.when(mid)(lambda: ctf(j).wait_send())
+            pl.when(end)(lambda: ctf(j).wait_recv())
+        for s,f in ((5,s5),(4,s4),(3,s3),(2,s2),(1,s1),(0,s0)): stage(s,f)
+def scratch():
+    return [pltpu.VMEM((KINDS-5,SLOTS,UNIT,WIDTH),jnp.float32),pltpu.SemaphoreType.DMA((KINDS,SLOTS)),pltpu.SemaphoreType.DMA((KINDS,SLOTS)),pltpu.SemaphoreType.DMA((2,SLOTS))]
+def ar_kernel(chunks,x_ref,o_ref,landing,send,recv,local,part=None):
+    e=Engine(chunks,x_ref,o_ref,landing,send,recv,local)
+    e.barrier(pltpu.get_barrier_semaphore())
+    def body(t,c):
+        e.tick(t); return c
+    lax.fori_loop(0,chunks+5*LAG,body,0)
+def allreduce(x,cid=0):
+    chunks=x.shape[0]//CHUNK
+    return pl.pallas_call(functools.partial(ar_kernel,chunks),name="dp_allreduce",
+      out_shape=jax.ShapeDtypeStruct(x.shape,jnp.float32),
+      in_specs=[pl.BlockSpec(memory_space=pltpu.VMEM)],out_specs=pl.BlockSpec(memory_space=pl.ANY),
+      scratch_shapes=scratch(),
+      compiler_params=pltpu.CompilerParams(collective_id=cid,has_side_effects=True,vmem_limit_bytes=60<<20))(x)
+
+
+def sum_every(per_layer, table_term):
+    pieces = []
+    smalls = []
+    for layer_index in reversed(range(LAYERS)):
+        (w_qkv, b_qv, w_out, b_out, gain_one, shift_one, w_in, b_in, w_down, b_down, gain_two, shift_two) = per_layer[layer_index]
+        pieces += [w_down, w_in, w_out, w_qkv.T]
+        padded = jnp.pad(b_qv, (0, WIDTH - b_qv.shape[0]))
+        smalls.append(jnp.stack([padded, b_out, gain_one, shift_one, b_in, b_down, gain_two, shift_two]))
+    flat = jnp.concatenate(pieces + smalls + [table_term, jnp.zeros((16, WIDTH), jnp.float32)], axis=0)
+    every = allreduce(flat)
+    groups = lax.axis_size("dp") // 8
+    if groups > 1:
+        every = lax.psum(every, "dp", axis_index_groups=[[low + 8 * high for high in range(groups)] for low in range(8)])
+    span = 2304
+    def piece(start, rows):
+        return jnp.stack([lax.slice_in_dim(every, start + span * (LAYERS - 1 - layer), start + span * (LAYERS - 1 - layer) + rows) for layer in range(LAYERS)])
+    w_down = piece(0, 768); w_in = piece(768, 768); w_out = piece(1536, 192)
+    w_qkv = jnp.swapaxes(piece(1728, 576), 1, 2)
+    base = span * LAYERS
+    small = jnp.stack([lax.slice_in_dim(every, base + 8 * (LAYERS - 1 - layer), base + 8 * (LAYERS - 1 - layer) + 8) for layer in range(LAYERS)])
+    table = lax.slice_in_dim(every, base + 16, base + 48)
+    return (w_qkv, small[:, 0, :384], w_out, small[:, 1], small[:, 2], small[:, 3], w_in, small[:, 4], w_down, small[:, 5], small[:, 6], small[:, 7], table)
 
 
 def on_device(
@@ -308,13 +422,7 @@
         precision=lax.Precision.HIGHEST,
         preferred_element_type=jnp.float32,
     )
-    stacked_terms = tuple(
-        (
-            jnp.stack([per_layer[layer_index][member] for layer_index in range(LAYERS)])
-            for member in range(12)
-        )
-    )
-    every_result = sum_every(stacked_terms, table_term)
+    every_result = sum_every(per_layer, table_term)
     merged = every_result[:12]
     grad_table = every_result[12]
     return (

time: 1770 us -> 792 us (0.45)
  waiting for transfers between devices: 1370 us -> 314 us
  Pallas kernels: 0 us -> 258 us
  blocking collectives: 180 us -> 0 us
    unnamed x35 -> x8, waiting for transfers between devices: 748 us -> 0.13 us
    pallas_call x0 -> x1, Pallas kernels: none -> 258 us  [allreduce(): pl.pallas_call(functools.partial(ar_kernel, chunks), name='dp_allreduce',...]
    all_gather x4 -> x0, waiting for transfers between devices: 228 us -> none  [the longest x1 73.6 us: sum_every(): lax.all_gather(shared[8], 'dp', axis=2, tiled=True)]
    all_gather x9 -> x0, blocking collectives: 180 us -> none  [the longest x1 30.8 us: sum_every(): lax.all_gather(shared[12], 'dp', axis=1, tiled=True)]
    reduce_scatter x1 -> x0, waiting for transfers between devices: 95 us -> none  [sum_every(): lax.psum_scatter(stacked_terms[6], 'dp', scatter_dimension=1, tiled=True)]
    unnamed x194 -> x242, local copies, waits for them, and re-layouts: 77.2 us -> 23.4 us
    concatenate x0 -> x1, local copies, waits for them, and re-layouts: none -> 44.2 us  [sum_every(): jnp.concatenate(pieces + smalls + [table_term, jnp.zeros((16, WIDTH), jnp...]
    psum x2, waiting for transfers between devices: 43 us -> 69.6 us  [backward_layer(): lax.psum(contract_cols(grad_proj_low, w_qkv), 'tensor')]
  transfers between devices with their start and end apart: 24 -> 8, of which waited for: 23 -> 8; matrix products, arithmetic and copies ran while one was open for 5% -> 4% of each run, Pallas kernels for 0% -> 0%
where the time goes in v1:
time: 792 us; the launch traced here: 783 us
  waiting for transfers between devices  314 us (40%)
  Pallas kernels  258 us (33%)
  local copies, waits for them, and re-layouts  87.5 us (11%)
  matrix products  60.7 us (8%)
  other arithmetic  46.1 us (6%)
  between operations  16 us (2%)
    pallas_call x1, Pallas kernels, allreduce(): pl.pallas_call(functools.partial(ar_kernel, chunks), name='dp_allreduce',...  258 us
    psum x2, waiting for transfers between devices, forward_layer(): lax.psum(jnp.dot(attended_heads, w_out, preferred_element_type=jnp.float3...  88.3 us
    psum x2, waiting for transfers between devices, forward_layer(): lax.psum(jnp.dot(active, w_down, preferred_element_type=jnp.float32), 'te...  85.3 us
    psum x2, waiting for transfers between devices, backward_layer(): lax.psum(contract_cols(grad_hidden_low, w_in), 'tensor')  70.5 us
    psum x2, waiting for transfers between devices, backward_layer(): lax.psum(contract_cols(grad_proj_low, w_qkv), 'tensor')  69.6 us
    concatenate x1, local copies, waits for them, and re-layouts, sum_every(): jnp.concatenate(pieces + smalls + [table_term, jnp.zeros((16, WIDTH), jnp...  44.2 us
    unnamed x242, local copies, waits for them, and re-layouts  23.4 us
    dot_general x8, matrix products, contract_rows(): lax.dot_general(left, right, (((0,), (0,)), ((), ())), preferred_element_...  20.9 us
  transfers between devices with their start and end apart: 8, of which 8 were waited for; matrix products, arithmetic and copies ran while one was open for 4% of the time, Pallas kernels for 0%

profile of v1, /device:TPU:0, one launch (start us, length us, event | category | flops | bytes accessed | tf_op | source)
XLA Modules:
  0.0 782.9 jit_solution(11319790179821613574)
XLA Ops:
  8.2 1.3 broadcast_subtract_fusion
  9.6 2.5 fusion.124
  16.0 1.6 fusion.88
  17.8 45.5 %all-reduce.11.cloned.1.call-done = f32[512,768]{1,0:T(8,128)} async-done(((f32[512,768]{1,0:T(8,128)}), f32[512,768]{1,0:T(8,128)}) %all-reduce.11.cloned.1.call-update) | async-done | bytes 1572880 | tf_op jit(solution)/shard_map/psum | solution.py:125
  63.3 2.0 fusion.123
  65.7 5.4 multiply_convert_fusion.4
  71.2 0.9 copy-done.43
  72.1 1.9 fusion.54
  74.8 42.3 %all-reduce.13.cloned.1.call-done = f32[512,768]{1,0:T(8,128)} async-done(((f32[512,768]{1,0:T(8,128)}), f32[512,768]{1,0:T(8,128)}) %all-reduce.13.cloned.1.call-update) | async-done | bytes 1572880 | tf_op jit(solution)/shard_map/psum | solution.py:135
  117.1 2.5 fusion.121
  123.1 1.2 copy-done.2
  125.7 1.6 fusion.85
  127.5 42.8 %all-reduce.15.cloned.1.call-done = f32[512,768]{1,0:T(8,128)} async-done(((f32[512,768]{1,0:T(8,128)}), f32[512,768]{1,0:T(8,128)}) %all-reduce.15.cloned.1.call-update) | async-done | bytes 1572880 | tf_op jit(solution)/shard_map/psum | solution.py:125
  170.4 2.6 fusion.120
  173.3 5.4 multiply_convert_fusion.3
  178.7 0.9 copy-done.44
  179.6 2.0 fusion.45
  181.7 43.0 %all-reduce.17.cloned.1.call-done = f32[512,768]{1,0:T(8,128)} async-done(((f32[512,768]{1,0:T(8,128)}), f32[512,768]{1,0:T(8,128)}) %all-reduce.17.cloned.1.call-update) | async-done | bytes 1572880 | tf_op jit(solution)/shard_map/psum | solution.py:135
  224.7 2.4 fusion.118
  228.3 1.3 multiply_reduce_fusion.4
  229.6 1.7 fusion.117
  232.0 1.8 fusion.129
  233.8 0.9 copy-done.112
  234.8 2.0 fusion.49
  237.1 4.0 fusion.81
  241.1 38.7 %all-reduce.19.cloned.1.call-done = f32[512,768]{1,0:T(8,128)} async-done(((f32[512,768]{1,0:T(8,128)}), f32[512,768]{1,0:T(8,128)}) %all-reduce.19.cloned.1.call-update) | async-done | bytes 1572880 | tf_op jit(solution)/shard_map/psum | solution.py:173
  279.9 4.0 multiply_reduce_fusion.5
  285.4 1.1 copy-done.3
  288.3 0.9 multiply_convert_fusion.1
  291.7 2.0 fusion.71
  293.9 4.0 fusion.102
  301.4 1.1 pad_maximum_fusion.2
  302.6 1.2 fusion.103
  303.9 1.8 fusion.131
  305.7 31.1 %all-reduce.21.cloned.1.call-done = f32[512,768]{1,0:T(8,128)} async-done(((f32[512,768]{1,0:T(8,128)}), f32[512,768]{1,0:T(8,128)}) %all-reduce.21.cloned.1.call-update) | async-done | bytes 1572880 | tf_op jit(solution)/shard_map/psum | solution.py:198
  336.8 3.4 multiply_reduce_fusion.2
  341.0 1.0 copy-done.105
  342.0 0.9 copy-done.113
  343.0 1.2 fusion.130
  344.2 0.9 copy-done.110
  345.1 2.0 fusion.58
  347.4 1.3 slice_reduce_fusion.1
  351.7 4.3 fusion.104
  356.0 2.4 fusion.78
  358.5 31.7 %all-reduce.23.cloned.1.call-done = f32[512,768]{1,0:T(8,128)} async-done(((f32[512,768]{1,0:T(8,128)}), f32[512,768]{1,0:T(8,128)}) %all-reduce.23.cloned.1.call-update) | async-done | bytes 1572880 | tf_op jit(solution)/shard_map/psum | solution.py:173
  390.2 4.0 multiply_reduce_fusion.3
  397.5 0.8 multiply_convert_fusion
  399.5 1.5 copy-done.36
  401.0 2.0 fusion.73
  404.5 1.2 fusion.105
  405.7 1.8 fusion.132
  407.5 38.5 %all-reduce.25.cloned.1.call-done = f32[512,768]{1,0:T(8,128)} async-done(((f32[512,768]{1,0:T(8,128)}), f32[512,768]{1,0:T(8,128)}) %all-reduce.25.cloned.1.call-update) | async-done | bytes 1572880 | tf_op jit(solution)/shard_map/psum | solution.py:198
  446.1 2.7 add_reduce_fusion
  449.0 0.9 fusion.10
  450.0 44.2 %concatenate.3.x_ref = f32[4672,768]{1,0:T(8,128)} concatenate(f32[768,768]{1,0:T(8,128)} %fusion.102, f32[768,768]{1,0:T(8,128)} %fusion.81, f32[192,768]{1,0:T(8,128)} %fusion.103, f32[576,768]{1,0:T(8,128)} %fusion.131, f32[768,768]{1,0:T(8,128)} %fusion.104, f32[768,768]{1,0:T(8,128)} %fusion.78, f32[192,768]{1,0:T(8,128)} %fusion.105, f32[576,768]{1,0:T(8,128)} %fusion.132, ...), dimensions={0} | concatenate | bytes 28704768 | tf_op jit(solution)/shard_map/concatenate | solution.py:341
  494.2 257.9 %dp_allreduce.1 = f32[4672,768]{1,0:T(8,128)} custom-call(f32[4672,768]{1,0:T(8,128)} %concatenate.3.x_ref), custom_call_target="tpu_custom_call" | custom-call | tf_op jit(solution)/shard_map/dp_allreduce/pallas_call | solution.py:326
  753.0 1.5 slice.261
  754.5 1.3 slice_bitcast_fusion.7
  755.8 2.2 slice_bitcast_fusion.5
  758.1 4.6 slice_bitcast_fusion.1
  767.4 1.1 pad_maximum_fusion.4
  768.6 2.5 pad_maximum_fusion.1
  771.1 2.0 maximum_bitcast_fusion
  773.1 2.5 pad_maximum_fusion
  (338 shorter events, 38.7 us)
Async XLA Ops:
  7.2 5.0 copy-start
  7.2 56.1 %all-reduce.11.cloned.1.call-start = ((), (), s32[]{:S(2)}) async-start(), calls=%async_computation | async-start | bytes 3145728 | tf_op jit(solution)/shard_map/psum | solution.py:125
  9.5 220.1 %copy-start.59 = (f32[512]{0:T(512)}, f32[512]{0:T(512)S(1)}, u32[]{:S(2)}) copy-start(f32[512]{0:T(512)S(1)} %get-tuple-element.145) | copy-start | bytes 6148
  9.5 2.6 copy-start.42
  9.5 2.6 copy-start.99
  17.6 99.5 %all-reduce.13.cloned.1.call-start = ((), (), s32[]{:S(2)}) async-start(), calls=%async_computation.1 | async-start | bytes 3145728 | tf_op jit(solution)/shard_map/psum | solution.py:135
  17.8 99.3 %copy-start.53 = (f32[768]{0:T(1024)}, f32[768]{0:T(1024)S(1)}, u32[]{:S(2)}) copy-start(f32[768]{0:T(1024)S(1)} %get-tuple-element.206) | copy-start | bytes 9220
  17.8 99.3 %copy-start.78 = (f32[768]{0:T(1024)}, f32[768]{0:T(1024)S(1)}, u32[]{:S(2)}) copy-start(f32[768]{0:T(1024)S(1)} %get-tuple-element.126) | copy-start | bytes 9220
  65.4 5.8 copy-start.6
  65.4 51.7 %copy-start.55 = (f32[512]{0:T(512)}, f32[512]{0:T(512)S(1)}, u32[]{:S(2)}) copy-start(f32[512]{0:T(512)S(1)} %broadcast_multiply_fusion.3) | copy-start | bytes 6148
  65.7 5.5 copy-start.67
  65.7 51.4 %copy-start.61 = (f32[512]{0:T(512)}, f32[512]{0:T(512)S(1)}, u32[]{:S(2)}) copy-start(f32[512]{0:T(512)S(1)} %fusion.98) | copy-start | bytes 6148
  65.7 6.3 copy-start.102
  74.0 96.3 %all-reduce.15.cloned.1.call-start = ((), (), s32[]{:S(2)}) async-start(), calls=%async_computation.2 | async-start | bytes 3145728 | tf_op jit(solution)/shard_map/psum | solution.py:125
  74.8 95.6 %copy-start.49 = (f32[768]{0:T(1024)}, f32[768]{0:T(1024)S(1)}, u32[]{:S(2)}) copy-start(f32[768]{0:T(1024)S(1)} %get-tuple-element.208) | copy-start | bytes 9220
  119.6 50.8 %copy-start.51 = (f32[512]{0:T(512)}, f32[512]{0:T(512)S(1)}, u32[]{:S(2)}) copy-start(f32[512]{0:T(512)S(1)} %broadcast_multiply_fusion.2) | copy-start | bytes 6148
  119.9 50.4 %copy-start.57 = (f32[512]{0:T(512)}, f32[512]{0:T(512)S(1)}, u32[]{:S(2)}) copy-start(f32[512]{0:T(512)S(1)} %fusion.99) | copy-start | bytes 6148
  127.3 97.4 %all-reduce.17.cloned.1.call-start = ((), (), s32[]{:S(2)}) async-start(), calls=%async_computation.3 | async-start | bytes 3145728 | tf_op jit(solution)/shard_map/psum | solution.py:135
  170.3 2.9 copy-start.107
  173.0 5.8 copy-start.9
  173.3 6.3 copy-start.103
  181.6 98.2 %all-reduce.19.cloned.1.call-start = ((), (), s32[]{:S(2)}) async-start(), calls=%async_computation.4 | async-start | bytes 3145728 | tf_op jit(solution)/shard_map/psum | solution.py:173
  228.3 3.1 copy-start.116
  231.4 48.5 %copy-start.65 = (f32[512]{0:T(512)}, f32[512]{0:T(512)S(1)}, u32[]{:S(2)}) copy-start(f32[512]{0:T(512)S(1)} %negate_multiply_fusion.5) | copy-start | bytes 6148
  232.0 2.8 copy-start.108
  236.8 100.0 %all-reduce.21.cloned.1.call-start = ((), (), s32[]{:S(2)}) async-start(), calls=%async_computation.5 | async-start | bytes 3145728 | tf_op jit(solution)/shard_map/psum | solution.py:198
  279.9 4.0 copy-start.10
  283.8 2.6 copy-start.3
  284.5 2.6 copy-start.13
  284.5 2.6 copy-start.63
  293.7 4.8 copy-start.71
  293.8 96.4 %all-reduce.23.cloned.1.call-start = ((), (), s32[]{:S(2)}) async-start(), calls=%async_computation.6 | async-start | bytes 3145728 | tf_op jit(solution)/shard_map/psum | solution.py:173
  293.8 4.1 copy-start.72
  293.8 5.3 copy-start.101
  293.8 5.8 copy-start.75
  293.9 6.4 copy-start.74
  293.9 7.0 copy-start.73
  293.9 7.6 copy-start.21
  293.9 7.6 copy-start.23
  297.9 4.7 copy-start.14
  297.9 4.7 copy-start.48
  297.9 4.7 copy-start.64
  303.9 32.9 %copy-start.50 = (f32[768]{0:T(1024)S(1)}, f32[768]{0:T(1024)}, u32[]{:S(2)}) copy-start(f32[768]{0:T(1024)} %copy-done.49) | copy-start | bytes 9220
  303.9 32.9 %copy-start.52 = (f32[512]{0:T(512)S(1)}, f32[512]{0:T(512)}, u32[]{:S(2)}) copy-start(f32[512]{0:T(512)} %copy-done.51) | copy-start | bytes 6148
  303.9 32.9 %copy-start.58 = (f32[512]{0:T(512)S(1)}, f32[512]{0:T(512)}, u32[]{:S(2)}) copy-start(f32[512]{0:T(512)} %copy-done.57) | copy-start | bytes 6148
  305.7 34.5 %copy-start.70 = (f32[512]{0:T(512)S(1)}, f32[512]{0:T(512)}, u32[]{:S(2)}) copy-start(f32[512]{0:T(512)} %copy-done.69) | copy-start | bytes 6148
  336.8 3.4 copy-start.5
  336.8 4.1 copy-start.114
  340.3 2.7 copy-start.113
  340.9 3.2 copy-start.16
  347.1 99.0 %all-reduce.25.cloned.1.call-start = ((), (), s32[]{:S(2)}) async-start(), calls=%async_computation.7 | async-start | bytes 3145728 | tf_op jit(solution)/shard_map/psum | solution.py:198
  351.7 4.3 copy-start.7
  351.7 4.3 copy-start.54
  351.7 4.3 copy-start.56
  351.7 4.3 copy-start.62
  351.7 4.3 copy-start.79
  351.7 4.3 copy-start.111
  358.5 35.7 %copy-start.68 = (f32[512]{0:T(512)S(1)}, f32[512]{0:T(512)}, u32[]{:S(2)}) copy-start(f32[512]{0:T(512)} %copy-done.67) | copy-start | bytes 6148
  390.2 4.0 copy-start.8
  399.5 3.5 copy-start.33
  405.7 40.3 %copy-start.98 = (f32[512]{0:T(512)S(1)}, f32[512]{0:T(512)}, u32[]{:S(2)}) copy-start(f32[512]{0:T(512)} %get-tuple-element.144) | copy-start | bytes 6148
  446.1 2.7 copy-start.19
  446.1 2.7 copy-start.60
  446.1 2.8 copy-start.100
  (61 other events, 78.6 us)
Sparse Core Ops, SparseCore 0:
  17.7 45.5 all-reduce.10
  74.1 42.8 all-reduce.12
  127.4 42.8 all-reduce.14
  181.7 42.8 all-reduce.16
  236.9 42.8 all-reduce.18
  293.9 42.8 all-reduce.20
  347.2 42.9 all-reduce.22
  403.1 42.8 all-reduce.24

commit v2 on v0

v2 whole, which is shorter than its diff:
```python
import functools
import math

import jax
import jax.numpy as jnp
from jax import lax
from jax.experimental import pallas as pl
from jax.experimental.pallas import tpu as pltpu
from jax.sharding import PartitionSpec as P

HEAD_DIM = 64
LAYERS = 2
PAGE_LEN = 512
REPL = 32
EPSILON = 1e-12
SCALE = HEAD_DIM ** (-0.5)
MESH = pl.DeviceIdType.MESH

BLOCK = 128
OWN = BLOCK // 2
BLOCKS = PAGE_LEN // BLOCK

UNIT = 16
CHUNK = 4 * UNIT
LAG = 2
SLOTS = 4 * LAG
KINDS = 12
(TX, TNEAR, TFAR, TA1, TA2, TQ1, TQ2, TTA, TTN, TTM, TTF, TG) = range(KINDS)
LANDINGS = TTA
GROUP = 8


def contract_rows(left, right):
    return lax.dot_general(
        left, right, (((0,), (0,)), ((), ())), preferred_element_type=jnp.float32
    )


def contract_cols(left, right):
    return lax.dot_general(
        left, right, (((1,), (1,)), ((), ())), preferred_element_type=jnp.float32
    )


def matmul(left, right):
    return jnp.dot(left, right, preferred_element_type=jnp.float32)


def repeat(count, body):
    def step(index, carry):
        body(index)
        return carry

    lax.fori_loop(0, count, step, 0)


def normed(values):
    average = jnp.mean(values, axis=-1, keepdims=True)
    centered = values - average
    variance = jnp.mean(centered * centered, axis=-1, keepdims=True)
    scale = lax.rsqrt(variance + EPSILON)
    return centered * scale, scale


def norm_back(grad, zhat, scale, gain):
    scaled = grad * gain
    average = jnp.mean(scaled, axis=-1, keepdims=True)
    along = jnp.mean(scaled * zhat, axis=-1, keepdims=True)
    return scale * (scaled - average - zhat * along)


def normal_cdf(values):
    return 0.5 * (1.0 + lax.erf(values * math.sqrt(0.5)))


def column(row):
    return jnp.transpose(jnp.broadcast_to(row, (128, row.shape[1])))[:, :1]


class Place:
    def __init__(self):
        d = lax.axis_index("dp")
        t = lax.axis_index("tensor")
        self.core = lax.rem(t, 2)
        self.core_peer = (d, t + 1 - 2 * self.core)
        self.y_peer = (d, t + 2 - 4 * lax.div(t, 2))
        pair = lax.rem(d, 2)
        line = lax.rem(lax.div(d, 2), 4)
        self.pair = pair
        self.mid = jnp.logical_or(line == 1, line == 2)
        self.end = jnp.logical_not(self.mid)
        self.upper = lax.div(line, 2)
        self.peer = (d + 1 - 2 * pair, t)
        self.line = (d + 2 - 4 * lax.rem(line, 2), t)
        self.cross = (jnp.where(line == 1, d + 2, d - 2), t)


def greet(place, barrier):
    def signal(device):
        pl.semaphore_signal(barrier, inc=1, device_id=device, device_id_type=MESH)

    for device in (place.core_peer, place.y_peer, place.peer, place.line):
        signal(device)
    pl.when(place.mid)(lambda: signal(place.cross))


def meet(place, barrier):
    pl.semaphore_wait(barrier, jnp.where(place.mid, 5, 4))


class GradientSum:
    def __init__(self, place, chunks, part, total, landing, send, recv, local):
        self.place = place
        self.chunks = chunks
        self.part = part
        self.total = total
        self.landing = landing
        self.send = send
        self.recv = recv
        self.local = local

    def rows(self, j, unit):
        return pl.ds(pl.multiple_of(j * CHUNK + unit * UNIT, UNIT), UNIT)

    def tick(self, t):
        place, part, total, local = self.place, self.part, self.total, self.local
        mine, other = place.pair, 1 - place.pair
        near, far = 2 + place.upper, 3 - place.upper

        def at(ref, j, unit):
            return ref.at[self.rows(j, unit)]

        def copy(kind, j, source, target, device):
            slot = lax.rem(j, SLOTS)
            return pltpu.make_async_remote_copy(
                src_ref=source,
                dst_ref=target,
                send_sem=self.send.at[kind, slot],
                recv_sem=self.recv.at[kind, slot],
                device_id=device,
                device_id_type=MESH,
            )

        def partial(kind, j, unit, device):
            return copy(kind, j, at(part, j, unit), self.landing.at[kind, lax.rem(j, SLOTS)], device)

        def final(kind, j, unit, device, source=part):
            return copy(kind, j, at(source, j, unit), at(total, j, unit), device)

        def keep(index, j, unit):
            return pltpu.make_async_copy(
                at(part, j, unit), at(total, j, unit), local.at[index, lax.rem(j, SLOTS)]
            )

        def add(kind, j, unit):
            rows = self.rows(j, unit)
            part[rows, :] = part[rows, :] + self.landing[kind, lax.rem(j, SLOTS)]

        def pair_first(j):
            return partial(TX, j, other, place.peer)

        def near_in(j):
            return partial(TNEAR, j, near, place.line)

        def far_in(j):
            return partial(TFAR, j, far, place.line)

        def mine_in(j):
            return partial(TA1, j, mine, place.line)

        def mine_across(j):
            return partial(TA2, j, mine, place.cross)

        def far_across(j):
            return partial(TQ1, j, far, place.cross)

        def near_pair(j):
            return partial(TQ2, j, near, place.peer)

        def mine_out(j):
            return final(TTA, j, mine, place.line)

        def near_out(j):
            return final(TTN, j, near, place.line)

        def near_across(j):
            return final(TTM, j, near, place.cross)

        def far_out(j):
            return final(TTF, j, far, place.line, total)

        def pair_last(j):
            return final(TG, j, mine, place.peer, total)

        def stage_0(j):
            pair_first(j).start()

            @pl.when(place.end)
            def _():
                near_in(j).start()
                far_in(j).start()

        def stage_1(j):
            pair_first(j).wait()
            add(TX, j, mine)

            @pl.when(place.end)
            def _():
                mine_in(j).start()
                near_in(j).wait_send()
                far_in(j).wait_send()

            @pl.when(place.mid)
            def _():
                far_in(j).wait_recv()
                add(TFAR, j, far)
                far_across(j).start()
                near_in(j).wait_recv()
                add(TNEAR, j, near)

        def stage_2(j):
            @pl.when(place.end)
            def _():
                mine_in(j).wait_send()

            @pl.when(place.mid)
            def _():
                mine_in(j).wait_recv()
                add(TA1, j, mine)
                mine_across(j).start()
                far_across(j).wait()
                add(TQ1, j, near)
                near_pair(j).start()

        def stage_3(j):
            @pl.when(place.mid)
            def _():
                mine_across(j).wait()
                add(TA2, j, mine)
                mine_out(j).start()
                keep(0, j, mine).start()
                near_pair(j).wait()
                add(TQ2, j, near)
                near_across(j).start()
                near_out(j).start()
                keep(1, j, near).start()

        def stage_4(j):
            @pl.when(place.mid)
            def _():
                mine_out(j).wait_send()
                near_out(j).wait_send()
                keep(0, j, mine).wait()
                keep(1, j, near).wait()
                pair_last(j).start()
                near_across(j).wait()
                far_out(j).start()

            @pl.when(place.end)
            def _():
                mine_out(j).wait_recv()
                pair_last(j).start()
                near_out(j).wait_recv()

        def stage_5(j):
            pair_last(j).wait()
            pl.when(place.mid)(lambda: far_out(j).wait_send())
            pl.when(place.end)(lambda: far_out(j).wait_recv())

        stages = (stage_0, stage_1, stage_2, stage_3, stage_4, stage_5)
        for number in reversed(range(len(stages))):
            j = t - number * LAG
            pl.when(jnp.logical_and(j >= 0, j < self.chunks))(
                functools.partial(stages[number], j)
            )

    def ticks(self):
        return self.chunks + 5 * LAG


def page_kernel(
    sizes,
    embeddings,
    replace_table,
    replace_ids,
    masked,
    padding,
    w_qkv,
    b_qv,
    w_out,
    b_out,
    first_gain,
    first_shift,
    w_in,
    b_in,
    w_down,
    b_down,
    second_gain,
    second_shift,
    cotangent,
    hidden_out,
    grad_embeddings,
    total,
    inputs_low,
    queries,
    keys,
    values,
    log_total,
    heads,
    normed_low,
    hidden,
    active,
    zhat_one,
    scale_one,
    zhat_two,
    scale_two,
    columns,
    own_a,
    own_b,
    part,
    land_core,
    land_y,
    land_back,
    land_small,
    dz_low,
    du_low,
    dheads,
    dkeys,
    dvalues,
    dqkv_low,
    sums,
    local_sums,
    grads,
    landing,
    core_send,
    core_recv,
    y_send,
    y_recv,
    back_send,
    back_recv,
    small_send,
    small_recv,
    dp_send,
    dp_recv,
    dp_local,
):
    width, hidden_width, local_heads, span = sizes
    head_width = local_heads * HEAD_DIM
    place = Place()
    core = place.core
    barrier = pltpu.get_barrier_semaphore()
    greet(place, barrier)
    small_base = LAYERS * span
    chunks = grads.shape[0] // CHUNK
    grad_sum = GradientSum(place, chunks, grads, total, landing, dp_send, dp_recv, dp_local)
    tick = grad_sum.tick

    def vector(ref, layer):
        both = ref[...].astype(jnp.float32)
        return jnp.where(layer == 0, both[0:1], both[1:2])

    def block(b):
        return pl.ds(pl.multiple_of(b * BLOCK, BLOCK), BLOCK)

    def kept(b):
        return pl.ds(pl.multiple_of(b * BLOCK + core * OWN, OWN), OWN)

    def given(b):
        return pl.ds(pl.multiple_of(b * BLOCK + (1 - core) * OWN, OWN), OWN)

    def packed(b):
        return pl.ds(pl.multiple_of(b * OWN, OWN), OWN)

    def lanes(p, size=128):
        return pl.ds(pl.multiple_of(p * size, size), size)

    def remote(source, target, send, recv, device):
        return pltpu.make_async_remote_copy(
            src_ref=source,
            dst_ref=target,
            send_sem=send,
            recv_sem=recv,
            device_id=device,
            device_id_type=MESH,
        )

    def to_core(turn, b):
        return remote(
            part.at[given(b)],
            land_core.at[turn, b],
            core_send.at[turn, b],
            core_recv.at[turn, b],
            place.core_peer,
        )

    def over_y(turn, b):
        return remote(
            part.at[kept(b)],
            land_y.at[turn, b],
            y_send.at[turn, b],
            y_recv.at[turn, b],
            place.y_peer,
        )

    def to_other(turn, b, source):
        return remote(
            source.at[packed(b)],
            land_back.at[turn, b],
            back_send.at[turn, b],
            back_recv.at[turn, b],
            place.core_peer,
        )

    def send_y(turn, b):
        to_core(turn, b).wait()
        part[kept(b), :] = part[kept(b), :] + land_core[turn, b]
        over_y(turn, b).start()

    def summed(turn, b):
        over_y(turn, b).wait()
        return part[kept(b), :] + land_y[turn, b]

    pad_row = padding[...].astype(jnp.float32)
    live_row = masked[...].astype(jnp.float32) * pad_row
    bias_row = (pad_row - 1.0) * 10000.0
    columns[:, 0:1] = column(live_row)
    columns[:, 1:2] = column(replace_ids[...].astype(jnp.float32))
    grads[small_base:, :] = jnp.zeros((CHUNK, width), jnp.float32)

    def chosen(rows, count):
        spots = lax.broadcasted_iota(jnp.int32, (count, REPL), 1).astype(jnp.float32)
        return jnp.where(columns[rows, 1:2] == spots, 1.0, 0.0)

    def first_input(b):
        rows = block(b)
        picked = matmul(chosen(rows, BLOCK).astype(jnp.bfloat16), replace_table[...])
        taken = jnp.where(
            columns[rows, 0:1] > 0.0, picked, embeddings[rows, :].astype(jnp.float32)
        )
        inputs_low[0, rows, :] = taken.astype(jnp.bfloat16)

    repeat(BLOCKS, first_input)

    def scores_of(layer, h, rows):
        return contract_cols(queries[layer, h, rows, :], keys[layer, h]) * SCALE + bias_row

    def forward(layer):
        bias_pair = vector(b_qv, layer)

        def project(b):
            rows = block(b)
            projected = matmul(inputs_low[layer, rows, :], w_qkv[layer])
            for h in range(local_heads):
                base = 3 * HEAD_DIM * h
                bias = 2 * HEAD_DIM * h
                queries[layer, h, rows, :] = (
                    projected[:, base : base + HEAD_DIM] + bias_pair[:, bias : bias + HEAD_DIM]
                ).astype(jnp.bfloat16)
                keys[layer, h, rows, :] = projected[
                    :, base + HEAD_DIM : base + 2 * HEAD_DIM
                ].astype(jnp.bfloat16)
                values[layer, h, rows, :] = (
                    projected[:, base + 2 * HEAD_DIM : base + 3 * HEAD_DIM]
                    + bias_pair[:, bias + HEAD_DIM : bias + 2 * HEAD_DIM]
                ).astype(jnp.bfloat16)

        repeat(BLOCKS, project)
        pl.when(layer == 0)(lambda: meet(place, barrier))

        def attend(b):
            rows = block(b)
            outs = []
            for h in range(local_heads):
                scores = scores_of(layer, h, rows)
                largest = jnp.max(scores, axis=-1, keepdims=True)
                weights = jnp.exp(scores - largest)
                totals = jnp.sum(weights, axis=-1, keepdims=True)
                probs = (weights * (1.0 / totals)).astype(jnp.bfloat16)
                outs.append(matmul(probs, values[layer, h]).astype(jnp.bfloat16))
                log_total[layer, rows, h : h + 1] = largest + jnp.log(totals)
            joined = jnp.concatenate(outs, axis=1)
            heads[layer, rows, :] = joined
            part[rows, :] = matmul(joined, w_out[layer])
            to_core(0, b).start()
            pl.when(b >= 1)(lambda: send_y(0, b - 1))

        repeat(BLOCKS, attend)
        send_y(0, BLOCKS - 1)

        gain, shift, bias_out = vector(first_gain, layer), vector(first_shift, layer), vector(b_out, layer)
        bias_in = vector(b_in, layer)

        def feed(b):
            rows = block(b)
            before = (
                inputs_low[layer, kept(b), :].astype(jnp.float32) + summed(0, b) + bias_out
            )
            zhat, scale = normed(before)
            zhat_one[layer, packed(b), :] = zhat
            scale_one[layer, packed(b), :] = scale
            result = zhat * gain + shift
            own_a[packed(b), :] = result
            to_other(0, b, own_a).start()
            normed_low[layer, kept(b), :] = result.astype(jnp.bfloat16)
            pl.when(b >= 1)(lambda: send_y(1, b - 1))
            to_other(0, b, own_a).wait()
            normed_low[layer, given(b), :] = land_back[0, b].astype(jnp.bfloat16)
            u = matmul(normed_low[layer, rows, :], w_in[layer]) + bias_in
            hidden[layer, rows, :] = u
            g = (u * normal_cdf(u)).astype(jnp.bfloat16)
            active[layer, rows, :] = g
            part[rows, :] = matmul(g, w_down[layer])
            to_core(1, b).start()

        repeat(BLOCKS, feed)
        send_y(1, BLOCKS - 1)

        gain_two, shift_two, bias_down = (
            vector(second_gain, layer),
            vector(second_shift, layer),
            vector(b_down, layer),
        )

        def receive(b):
            to_other(1, b, own_b).wait()
            inputs_low[layer + 1, given(b), :] = land_back[1, b].astype(jnp.bfloat16)

        def finish(b):
            before = own_a[packed(b), :] + summed(1, b) + bias_down
            zhat, scale = normed(before)
            zhat_two[layer, packed(b), :] = zhat
            scale_two[layer, packed(b), :] = scale
            result = zhat * gain_two + shift_two
            own_b[packed(b), :] = result
            to_other(1, b, own_b).start()
            inputs_low[layer + 1, kept(b), :] = result.astype(jnp.bfloat16)
            pl.when(b >= 1)(lambda: receive(b - 1))

        repeat(BLOCKS, finish)
        receive(BLOCKS - 1)

    repeat(LAYERS, forward)
    hidden_out[...] = inputs_low[LAYERS]

    def first_grad(b):
        own_b[packed(b), :] = cotangent[kept(b), :].astype(jnp.float32) * columns[kept(b), 0:1]

    repeat(BLOCKS, first_grad)
    sums[...] = jnp.zeros_like(sums)
    local_sums[...] = jnp.zeros_like(local_sums)

    def backward(turn):
        layer = LAYERS - 1 - turn
        base = turn * span
        start = turn * (span // CHUNK)
        in_base = base + hidden_width
        out_base = in_base + width
        qkv_base = out_base + head_width

        def rows_at(first, count):
            return pl.ds(pl.multiple_of(first, 64), count)

        def total_row(index, amount):
            sums[turn, index : index + 1, :] = sums[turn, index : index + 1, :] + jnp.sum(
                amount, axis=0, keepdims=True
            )

        def receive(back, b, source):
            to_other(back, b, source).wait()
            dz_low[given(b), :] = land_back[back, b].astype(jnp.bfloat16)

        gain_two = vector(second_gain, layer)

        def norm_two(b):
            grad = own_b[packed(b), :]
            zhat = zhat_two[layer, packed(b), :]
            dz = norm_back(grad, zhat, scale_two[layer, packed(b), :], gain_two)
            own_a[packed(b), :] = dz
            to_other(0, b, own_a).start()
            dz_low[kept(b), :] = dz.astype(jnp.bfloat16)
            total_row(0, grad * zhat)
            total_row(1, grad)
            total_row(2, dz)

        repeat(BLOCKS, norm_two)
        repeat(BLOCKS, lambda b: receive(0, b, own_a))

        def down_piece(p):
            grads[rows_at(base + 128 * p, 128), :] = contract_rows(
                active[layer, :, lanes(p)], dz_low[...]
            )

        def in_piece(p):
            grads[rows_at(in_base + 128 * p, 128), :] = contract_rows(
                normed_low[layer, :, lanes(p)], du_low[...]
            )

        down_piece(0)
        tick(start)
        tick(start + 1)

        def feed(b):
            rows = block(b)
            dg = contract_cols(dz_low[rows, :], w_down[layer])
            u = hidden[layer, rows, :]
            density = jnp.exp(u * u * (-0.5)) * (1.0 / math.sqrt(2.0 * math.pi))
            du = dg * (normal_cdf(u) + u * density)
            du_low[rows, :] = du.astype(jnp.bfloat16)
            local_sums[turn, 0:1, :] = local_sums[turn, 0:1, :] + jnp.sum(
                du, axis=0, keepdims=True
            )
            down_piece(b + 1)
            tick(start + 2 + 2 * b)
            tick(start + 3 + 2 * b)

        repeat(BLOCKS, feed)
        down_piece(5)

        def feed_in(b):
            rows = block(b)
            part[rows, :] = contract_cols(du_low[rows, :], w_in[layer])
            to_core(0, b).start()
            in_piece(b)
            tick(start + 10 + 2 * b)
            send_y(0, b)
            tick(start + 11 + 2 * b)

        repeat(BLOCKS, feed_in)
        in_piece(4)
        tick(start + 18)
        in_piece(5)
        tick(start + 19)

        gain = vector(first_gain, layer)

        def norm_one(b):
            grad = own_a[packed(b), :] + summed(0, b)
            zhat = zhat_one[layer, packed(b), :]
            dz = norm_back(grad, zhat, scale_one[layer, packed(b), :], gain)
            own_b[packed(b), :] = dz
            to_other(1, b, own_b).start()
            dz_low[kept(b), :] = dz.astype(jnp.bfloat16)
            total_row(3, grad * zhat)
            total_row(4, grad)
            total_row(5, dz)
            tick(start + 20 + b)
            receive(1, b, own_b)

        repeat(BLOCKS, norm_one)
        grads[rows_at(out_base, head_width), :] = contract_rows(heads[layer], dz_low[...])
        dheads[...] = contract_cols(dz_low[...], w_out[layer]).astype(jnp.bfloat16)
        dkeys[...] = jnp.zeros_like(dkeys)
        dvalues[...] = jnp.zeros_like(dvalues)

        def attend(b):
            rows = block(b)
            for h in range(local_heads):
                side = HEAD_DIM * h
                probs = jnp.exp(scores_of(layer, h, rows) - log_total[layer, rows, h : h + 1])
                dhead = dheads[rows, side : side + HEAD_DIM]
                dprobs = contract_cols(dhead, values[layer, h])
                dvalues[h] = dvalues[h] + contract_rows(probs.astype(jnp.bfloat16), dhead)
                inner = jnp.sum(probs * dprobs, axis=-1, keepdims=True)
                ds = (probs * (dprobs - inner)).astype(jnp.bfloat16)
                dq = matmul(ds, keys[layer, h]) * SCALE
                dkeys[h] = dkeys[h] + contract_rows(ds, queries[layer, h, rows, :])
                dqkv_low[rows, 3 * side : 3 * side + HEAD_DIM] = dq.astype(jnp.bfloat16)
                local_sums[turn, 1:2, 2 * side : 2 * side + HEAD_DIM] = local_sums[
                    turn, 1:2, 2 * side : 2 * side + HEAD_DIM
                ] + jnp.sum(dq, axis=0, keepdims=True)
            pl.when(b < BLOCKS - 1)(lambda: tick(start + 24 + b))

        repeat(BLOCKS, attend)
        for h in range(local_heads):
            side = HEAD_DIM * h
            dqkv_low[:, 3 * side + HEAD_DIM : 3 * side + 2 * HEAD_DIM] = (
                dkeys[h] * SCALE
            ).astype(jnp.bfloat16)
            dv = dvalues[h]
            dqkv_low[:, 3 * side + 2 * HEAD_DIM : 3 * side + 3 * HEAD_DIM] = dv.astype(
                jnp.bfloat16
            )
            local_sums[turn, 1:2, 2 * side + HEAD_DIM : 2 * side + 2 * HEAD_DIM] = jnp.sum(
                dv, axis=0, keepdims=True
            )

        def project(b):
            rows = block(b)
            part[rows, :] = contract_cols(dqkv_low[rows, :], w_qkv[layer])
            to_core(1, b).start()
            pl.when(b >= 1)(lambda: send_y(1, b - 1))

        repeat(BLOCKS, project)
        send_y(1, BLOCKS - 1)

        def qkv_piece(p):
            grads[rows_at(qkv_base + 128 * p, 128), :] = contract_rows(
                dqkv_low[:, lanes(p)], inputs_low[layer]
            )
            tick(start + 27 + 2 * p)
            tick(start + 28 + 2 * p)

        repeat(4, qkv_piece)
        grads[rows_at(qkv_base + 512, 64), :] = contract_rows(
            dqkv_low[:, 512:], inputs_low[layer]
        )
        tick(start + 35)

        def pass_on(b):
            own_b[packed(b), :] = own_b[packed(b), :] + summed(1, b)

        repeat(BLOCKS, pass_on)

    repeat(LAYERS, backward)

    def last_grad(b):
        live = columns[kept(b), 0:1]
        grad = own_b[packed(b), :]
        masked_grad = grad * (1.0 - live)
        own_a[packed(b), :] = masked_grad
        to_other(0, b, own_a).start()
        grad_embeddings[kept(b), :] = masked_grad.astype(jnp.bfloat16)
        grads[small_base : small_base + REPL, :] = grads[
            small_base : small_base + REPL, :
        ] + lax.dot_general(
            chosen(kept(b), OWN),
            grad * live,
            (((0,), (0,)), ((), ())),
            precision=lax.Precision.HIGHEST,
            preferred_element_type=jnp.float32,
        )

    repeat(BLOCKS, last_grad)
    shared = REPL + 8 * LAYERS
    for turn in range(LAYERS):
        first = small_base + REPL + 8 * turn
        grads[first : first + 8, :] = sums[turn]
    grads[small_base + shared : small_base + shared + 8, :] = local_sums[...].reshape(8, width)
    short = remote(
        grads.at[pl.ds(small_base, shared)], land_small, small_send, small_recv, place.core_peer
    )
    short.start()

    def receive(b):
        to_other(0, b, own_a).wait()
        grad_embeddings[given(b), :] = land_back[0, b].astype(jnp.bfloat16)

    repeat(BLOCKS, receive)
    short.wait()
    grads[small_base : small_base + shared, :] = (
        grads[small_base : small_base + shared, :] + land_small[...]
    )
    done = LAYERS * (span // CHUNK)
    repeat(grad_sum.ticks() - done, lambda i: tick(done + i))


def run_pages(args, sizes):
    width, hidden_width, local_heads, span = sizes
    rows = PAGE_LEN
    flat = LAYERS * span + CHUNK
    half = rows // 2
    low, full = jnp.bfloat16, jnp.float32
    vmem, dma = pltpu.VMEM, pltpu.SemaphoreType.DMA
    head_width = local_heads * HEAD_DIM
    return pl.pallas_call(
        functools.partial(page_kernel, sizes),
        name="pages",
        out_shape=(
            jax.ShapeDtypeStruct((rows, width), low),
            jax.ShapeDtypeStruct((rows, width), low),
            jax.ShapeDtypeStruct((flat, width), full),
        ),
        in_specs=[pl.BlockSpec(memory_space=pltpu.VMEM)] * len(args),
        out_specs=(
            pl.BlockSpec(memory_space=pltpu.VMEM),
            pl.BlockSpec(memory_space=pltpu.VMEM),
            pl.BlockSpec(memory_space=pl.ANY),
        ),
        scratch_shapes=[
            vmem((LAYERS + 1, rows, width), low),
            vmem((LAYERS, local_heads, rows, HEAD_DIM), low),
            vmem((LAYERS, local_heads, rows, HEAD_DIM), low),
            vmem((LAYERS, local_heads, rows, HEAD_DIM), low),
            vmem((LAYERS, rows, 128), full),
            vmem((LAYERS, rows, head_width), low),
            vmem((LAYERS, rows, width), low),
            vmem((LAYERS, rows, hidden_width), full),
            vmem((LAYERS, rows, hidden_width), low),
            vmem((LAYERS, half, width), full),
            vmem((LAYERS, half, 1), full),
            vmem((LAYERS, half, width), full),
            vmem((LAYERS, half, 1), full),
            vmem((rows, 128), full),
            vmem((half, width), full),
            vmem((half, width), full),
            vmem((rows, width), full),
            vmem((2, BLOCKS, OWN, width), full),
            vmem((2, BLOCKS, OWN, width), full),
            vmem((2, BLOCKS, OWN, width), full),
            vmem((REPL + 8 * LAYERS, width), full),
            vmem((rows, width), low),
            vmem((rows, hidden_width), low),
            vmem((rows, head_width), low),
            vmem((local_heads, rows, HEAD_DIM), full),
            vmem((local_heads, rows, HEAD_DIM), full),
            vmem((rows, 3 * head_width), low),
            vmem((LAYERS, 8, width), full),
            vmem((LAYERS, 4, width), full),
            vmem((flat, width), full),
            vmem((LANDINGS, SLOTS, UNIT, width), full),
            dma((2, BLOCKS)),
            dma((2, BLOCKS)),
            dma((2, BLOCKS)),
            dma((2, BLOCKS)),
            dma((2, BLOCKS)),
            dma((2, BLOCKS)),
            dma,
            dma,
            dma((KINDS, SLOTS)),
            dma((KINDS, SLOTS)),
            dma((2, SLOTS)),
        ],
        compiler_params=pltpu.CompilerParams(
            collective_id=0, has_side_effects=True, vmem_limit_bytes=62 << 20
        ),
    )(*args)


def on_device(*args):
    (embeddings, replace_table, replace_ids, masked, padding, w_qkv, b_qv, *_) = args
    width = embeddings.shape[1]
    head_width = w_qkv.shape[2] // 3
    hidden_width = args[11].shape[2]
    span = 2 * hidden_width + 4 * head_width
    args = list(args)
    for index in (2, 3, 4):
        args[index] = args[index].reshape(1, PAGE_LEN)
    hidden_out, grad_embeddings, every = run_pages(
        args, (width, hidden_width, head_width // HEAD_DIM, span)
    )
    groups = lax.axis_size("dp") // GROUP
    if groups > 1:
        every = lax.psum(
            every,
            "dp",
            axis_index_groups=[
                [low + GROUP * high for high in range(groups)] for low in range(GROUP)
            ],
        )

    def piece(first, rows):
        return jnp.stack(
            [
                lax.slice_in_dim(every, start, start + rows)
                for start in [first + span * turn for turn in reversed(range(LAYERS))]
            ]
        )

    base = LAYERS * span

    def short(row, step):
        return jnp.stack([every[base + row + step * turn] for turn in reversed(range(LAYERS))])

    grad_w_down = piece(0, hidden_width)
    grad_w_in = piece(hidden_width, width)
    grad_w_out = piece(hidden_width + width, head_width)
    grad_w_qkv = jnp.swapaxes(piece(hidden_width + width + head_width, 3 * head_width), 1, 2)
    local = REPL + 8 * LAYERS
    return (
        hidden_out,
        grad_embeddings,
        lax.slice_in_dim(every, base, base + REPL),
        grad_w_qkv,
        short(local + 1, 4)[:, : 2 * head_width],
        grad_w_out,
        short(REPL + 5, 8),
        short(REPL + 3, 8),
        short(REPL + 4, 8),
        grad_w_in,
        short(local, 4),
        grad_w_down,
        short(REPL + 2, 8),
        short(REPL, 8),
        short(REPL + 1, 8),
    )


def solution(mesh):
    placed = (
        P("dp", None),
        P(),
        P("dp"),
        P("dp"),
        P("dp"),
        P(None, None, "tensor"),
        P(None, "tensor"),
        P(None, "tensor", None),
        P(),
        P(),
        P(),
        P(None, None, "tensor"),
        P(None, "tensor"),
        P(None, "tensor", None),
        P(),
        P(),
        P(),
        P("dp", None),
    )
    return jax.shard_map(
        on_device,
        mesh=mesh,
        in_specs=placed,
        out_specs=(
            P("dp", None),
            P("dp", None),
            P(),
            P(None, None, "tensor"),
            P(None, "tensor"),
            P(None, "tensor", None),
            P(),
            P(),
            P(),
            P(None, None, "tensor"),
            P(None, "tensor"),
            P(None, "tensor", None),
            P(),
            P(),
            P(),
        ),
        check_vma=False,
    )
```

time: 1770 us -> 382 us (0.22)
  waiting for transfers between devices: 1370 us -> 0 us
  Pallas kernels: 0 us -> 354 us
  blocking collectives: 180 us -> 0 us
  local copies, waits for them, and re-layouts: 96 us -> 16.3 us
  matrix products: 51.8 us -> 0 us
  other arithmetic: 40.6 us -> 10.5 us
    unnamed x35 -> x0, waiting for transfers between devices: 748 us -> none
    pallas_call x0 -> x1, Pallas kernels: none -> 354 us  [run_pages(): pl.pallas_call(functools.partial(page_kernel, sizes), name='pages', out_s...]
    psum x8 -> x0, waiting for transfers between devices: 302 us -> none  [the longest x2 88.3 us: forward_layer(): lax.psum(jnp.dot(attended_heads, w_out, preferred_element_type=jnp.float3...]
    all_gather x4 -> x0, waiting for transfers between devices: 228 us -> none  [the longest x1 73.6 us: sum_every(): lax.all_gather(shared[8], 'dp', axis=2, tiled=True)]
    all_gather x9 -> x0, blocking collectives: 180 us -> none  [the longest x1 30.8 us: sum_every(): lax.all_gather(shared[12], 'dp', axis=1, tiled=True)]
    reduce_scatter x1 -> x0, waiting for transfers between devices: 95 us -> none  [sum_every(): lax.psum_scatter(stacked_terms[6], 'dp', scatter_dimension=1, tiled=True)]
    unnamed x194 -> x7, local copies, waits for them, and re-layouts: 77.2 us -> 5.67 us
    dot_general x37 -> x0, matrix products: 49.4 us -> none  [the longest x8 11.3 us: contract_cols(): lax.dot_general(left, right, (((1,), (1,)), ((), ())), preferred_element_...]
  transfers between devices with their start and end apart: 24 -> 0, of which waited for: 23 -> 0; matrix products, arithmetic and copies ran while one was open for 5% -> 0% of each run, Pallas kernels for 0% -> 0%
where the time goes in v2:
time: 382 us
  Pallas kernels  354 us (93%)
  local copies, waits for them, and re-layouts  16.3 us (4%)
  other arithmetic  10.5 us (3%)
    pallas_call x1, Pallas kernels, run_pages(): pl.pallas_call(functools.partial(page_kernel, sizes), name='pages', out_s...  354 us
    another operation x3, local copies, waits for them, and re-layouts, piece(): jnp.stack([lax.slice_in_dim(every, start, start + rows) for start in [fir...  7.93 us

profile of v2, /device:TPU:0, one launch (start us, length us, event | category | flops | bytes accessed | tf_op | source)
XLA Modules:
  0.0 381.9 jit_solution(17577641553312531778)
XLA Ops:
  0.6 3.9 %copy.33.w_qkv = bf16[2,768,576]{2,1,0:T(8,128)(2,1)} copy(bf16[2,768,576]{1,2,0:T(8,128)(2,1)} %param.23) | data formatting | bytes 3538944 | tf_op args[5]
  4.6 354.4 %pages.1 = (bf16[512,768]{1,0:T(8,128)(2,1)}, bf16[512,768]{1,0:T(8,128)(2,1)}, f32[4672,768]{1,0:T(8,128)}) custom-call(bf16[512,768]{1,0:T(8,128)(2,1)} %embeddings.1, bf16[32,768]{1,0:T(8,128)(2,1)} %replace_table.1, s32[1,512]{1,0:T(1,128)} %bitcast.21, s32[1,512]{1,0:T(1,128)} %bitcast.22, s32[1,512]{1,0:T(1,128)} %bitcast.23, ...), custom_call_target="tpu_custom_call" | custom-call | tf_op jit(solution)/shard_map/pages/pallas_call | solution.py:765
  359.0 1.1 fusion
  360.2 0.6 pad_maximum_fusion.9
  360.8 0.6 pad_maximum_fusion.10
  361.3 0.6 pad_maximum_fusion.7
  361.9 0.6 pad_maximum_fusion.5
  362.6 0.6 pad_maximum_fusion.3
  363.2 1.5 slice.78
  364.7 1.3 slice_bitcast_fusion.7
  366.0 1.1 pad_maximum_fusion.2
  367.1 2.2 slice_bitcast_fusion.5
  369.4 4.4 %slice_bitcast_fusion.1 = (f32[1,768,768]{2,1,0:T(8,128)S(1)}, f32[1,768,768]{2,1,0:T(8,128)S(1)}, f32[1,768,768]{2,1,0:T(8,128)S(1)}, f32[1,768,768]{2,1,0:T(8,128)S(1)}) fusion(f32[4672,768]{1,0:T(8,128)} %get-tuple-element.20), kind=kLoop, calls=%fused_computation.4 | loop fusion | bytes 18874368 | tf_op jit(solution)/shard_map/stack | solution.py:852
  373.7 2.0 maximum_bitcast_fusion
  375.8 0.0 copy-start.1
  375.8 0.0 copy-start
  375.8 4.3 %pad_maximum_fusion = (f32[2,768,768]{2,1,0:T(8,128)}, f32[2,768,768]{2,1,0:T(8,128)}) fusion(f32[1,768,768]{2,1,0:T(8,128)S(1)} %get-tuple-element.39, f32[1,768,768]{2,1,0:T(8,128)S(1)} %get-tuple-element.40, f32[1,768,768]{2,1,0:T(8,128)S(1)} %get-tuple-element.38, f32[1,768,768]{2,1,0:T(8,128)S(1)} %get-tuple-element.37), kind=kLoop, calls=%fused_computation | loop fusion | flops 2359296 | bytes 18874368 | tf_op jit(solution)/shard_map/stack | solution.py:852
  380.1 0.0 copy-done.1
  380.1 0.9 copy.36
  381.0 0.0 copy-done
  381.0 0.9 copy.37
Async XLA Ops:
  375.8 4.4 %copy-start.1 = (bf16[512,768]{1,0:T(8,128)(2,1)S(1)}, bf16[512,768]{1,0:T(8,128)(2,1)}, u32[]{:S(2)}) copy-start(bf16[512,768]{1,0:T(8,128)(2,1)} %get-tuple-element.68) | copy-start | bytes 2359300
  375.8 5.2 %copy-start = (bf16[512,768]{1,0:T(8,128)(2,1)S(1)}, bf16[512,768]{1,0:T(8,128)(2,1)}, u32[]{:S(2)}) copy-start(bf16[512,768]{1,0:T(8,128)(2,1)} %get-tuple-element.69) | copy-start | bytes 2359300

commit v3 on v2

--- a/solution.py
+++ b/solution.py
@@ -26,8 +26,9 @@
 SLOTS = 4 * LAG
 KINDS = 12
 (TX, TNEAR, TFAR, TA1, TA2, TQ1, TQ2, TTA, TTN, TTM, TTF, TG) = range(KINDS)
-LANDINGS = TTA
+LANDINGS = TTA + 1
 GROUP = 8
+WEIGHTS = (5, 7, 11, 13)
 
 
 def contract_rows(left, right):
@@ -109,26 +110,24 @@
 
 
 class GradientSum:
-    def __init__(self, place, chunks, part, total, landing, send, recv, local):
+    def __init__(self, place, chunks, part, landing, send, recv):
         self.place = place
         self.chunks = chunks
         self.part = part
-        self.total = total
         self.landing = landing
         self.send = send
         self.recv = recv
-        self.local = local
 
     def rows(self, j, unit):
         return pl.ds(pl.multiple_of(j * CHUNK + unit * UNIT, UNIT), UNIT)
 
     def tick(self, t):
-        place, part, total, local = self.place, self.part, self.total, self.local
+        place, part = self.place, self.part
         mine, other = place.pair, 1 - place.pair
         near, far = 2 + place.upper, 3 - place.upper
 
-        def at(ref, j, unit):
-            return ref.at[self.rows(j, unit)]
+        def at(j, unit):
+            return part.at[self.rows(j, unit)]
 
         def copy(kind, j, source, target, device):
             slot = lax.rem(j, SLOTS)
@@ -142,15 +141,10 @@
             )
 
         def partial(kind, j, unit, device):
-            return copy(kind, j, at(part, j, unit), self.landing.at[kind, lax.rem(j, SLOTS)], device)
-
-        def final(kind, j, unit, device, source=part):
-            return copy(kind, j, at(source, j, unit), at(total, j, unit), device)
-
-        def keep(index, j, unit):
-            return pltpu.make_async_copy(
-                at(part, j, unit), at(total, j, unit), local.at[index, lax.rem(j, SLOTS)]
-            )
+            return copy(kind, j, at(j, unit), self.landing.at[kind, lax.rem(j, SLOTS)], device)
+
+        def final(kind, j, unit, device):
+            return copy(kind, j, at(j, unit), at(j, unit), device)
 
         def add(kind, j, unit):
             rows = self.rows(j, unit)
@@ -178,7 +172,7 @@
             return partial(TQ2, j, near, place.peer)
 
         def mine_out(j):
-            return final(TTA, j, mine, place.line)
+            return partial(TTA, j, mine, place.line)
 
         def near_out(j):
             return final(TTN, j, near, place.line)
@@ -187,10 +181,10 @@
             return final(TTM, j, near, place.cross)
 
         def far_out(j):
-            return final(TTF, j, far, place.line, total)
+            return final(TTF, j, far, place.line)
 
         def pair_last(j):
-            return final(TG, j, mine, place.peer, total)
+            return final(TG, j, mine, place.peer)
 
         def stage_0(j):
             pair_first(j).start()
@@ -206,9 +200,9 @@
 
             @pl.when(place.end)
             def _():
-                mine_in(j).start()
                 near_in(j).wait_send()
                 far_in(j).wait_send()
+                mine_in(j).start()
 
             @pl.when(place.mid)
             def _():
@@ -226,9 +220,9 @@
             @pl.when(place.mid)
             def _():
                 mine_in(j).wait_recv()
+                far_across(j).wait()
                 add(TA1, j, mine)
                 mine_across(j).start()
-                far_across(j).wait()
                 add(TQ1, j, near)
                 near_pair(j).start()
 
@@ -238,20 +232,16 @@
                 mine_across(j).wait()
                 add(TA2, j, mine)
                 mine_out(j).start()
-                keep(0, j, mine).start()
                 near_pair(j).wait()
                 add(TQ2, j, near)
                 near_across(j).start()
                 near_out(j).start()
-                keep(1, j, near).start()
 
         def stage_4(j):
             @pl.when(place.mid)
             def _():
                 mine_out(j).wait_send()
                 near_out(j).wait_send()
-                keep(0, j, mine).wait()
-                keep(1, j, near).wait()
                 pair_last(j).start()
                 near_across(j).wait()
                 far_out(j).start()
@@ -259,8 +249,9 @@
             @pl.when(place.end)
             def _():
                 mine_out(j).wait_recv()
+                near_out(j).wait_recv()
+                part[self.rows(j, mine), :] = self.landing[TTA, lax.rem(j, SLOTS)]
                 pair_last(j).start()
-                near_out(j).wait_recv()
 
         def stage_5(j):
             pair_last(j).wait()
@@ -285,22 +276,22 @@
     replace_ids,
     masked,
     padding,
-    w_qkv,
+    w_qkv_far,
     b_qv,
-    w_out,
+    w_out_far,
     b_out,
     first_gain,
     first_shift,
-    w_in,
+    w_in_far,
     b_in,
-    w_down,
+    w_down_far,
     b_down,
     second_gain,
     second_shift,
     cotangent,
     hidden_out,
     grad_embeddings,
-    total,
+    grads,
     inputs_low,
     queries,
     keys,
@@ -314,6 +305,10 @@
     scale_one,
     zhat_two,
     scale_two,
+    w_qkv,
+    w_out,
+    w_in,
+    w_down,
     columns,
     own_a,
     own_b,
@@ -330,7 +325,6 @@
     dqkv_low,
     sums,
     local_sums,
-    grads,
     landing,
     core_send,
     core_recv,
@@ -342,7 +336,7 @@
     small_recv,
     dp_send,
     dp_recv,
-    dp_local,
+    weight_sem,
 ):
     width, hidden_width, local_heads, span = sizes
     head_width = local_heads * HEAD_DIM
@@ -350,9 +344,20 @@
     core = place.core
     barrier = pltpu.get_barrier_semaphore()
     greet(place, barrier)
+    weights = ((w_qkv_far, w_qkv), (w_out_far, w_out), (w_in_far, w_in), (w_down_far, w_down))
+
+    def weight(index, layer):
+        source, target = weights[index]
+        return pltpu.make_async_copy(
+            source.at[layer], target.at[layer], weight_sem.at[index, layer]
+        )
+
+    for layer in range(LAYERS):
+        for index in range(len(weights)):
+            weight(index, layer).start()
     small_base = LAYERS * span
     chunks = grads.shape[0] // CHUNK
-    grad_sum = GradientSum(place, chunks, grads, total, landing, dp_send, dp_recv, dp_local)
+    grad_sum = GradientSum(place, chunks, grads, landing, dp_send, dp_recv)
     tick = grad_sum.tick
 
     def vector(ref, layer):
@@ -449,7 +454,7 @@
 
         def project(b):
             rows = block(b)
-            projected = matmul(inputs_low[layer, rows, :], w_qkv[layer])
+            projected = contract_cols(inputs_low[layer, rows, :], w_qkv[layer])
             for h in range(local_heads):
                 base = 3 * HEAD_DIM * h
                 bias = 2 * HEAD_DIM * h
@@ -464,8 +469,10 @@
                     + bias_pair[:, bias + HEAD_DIM : bias + 2 * HEAD_DIM]
                 ).astype(jnp.bfloat16)
 
+        weight(0, layer).wait()
         repeat(BLOCKS, project)
         pl.when(layer == 0)(lambda: meet(place, barrier))
+        weight(1, layer).wait()
 
         def attend(b):
             rows = block(b)
@@ -512,6 +519,8 @@
             part[rows, :] = matmul(g, w_down[layer])
             to_core(1, b).start()
 
+        weight(2, layer).wait()
+        weight(3, layer).wait()
         repeat(BLOCKS, feed)
         send_y(1, BLOCKS - 1)
 
@@ -686,7 +695,7 @@
 
         def project(b):
             rows = block(b)
-            part[rows, :] = contract_cols(dqkv_low[rows, :], w_qkv[layer])
+            part[rows, :] = matmul(dqkv_low[rows, :], w_qkv[layer])
             to_core(1, b).start()
             pl.when(b >= 1)(lambda: send_y(1, b - 1))
 
@@ -766,15 +775,18 @@
         functools.partial(page_kernel, sizes),
         name="pages",
         out_shape=(
-            jax.ShapeDtypeStruct((rows, width), low),
-            jax.ShapeDtypeStruct((rows, width), low),
-            jax.ShapeDtypeStruct((flat, width), full),
+            vmem((rows, width), low),
+            vmem((rows, width), low),
+            vmem((flat, width), full),
         ),
-        in_specs=[pl.BlockSpec(memory_space=pltpu.VMEM)] * len(args),
+        in_specs=[
+            pl.BlockSpec(memory_space=pl.ANY if index in WEIGHTS else pltpu.VMEM)
+            for index in range(len(args))
+        ],
         out_specs=(
             pl.BlockSpec(memory_space=pltpu.VMEM),
             pl.BlockSpec(memory_space=pltpu.VMEM),
-            pl.BlockSpec(memory_space=pl.ANY),
+            pl.BlockSpec(memory_space=pltpu.VMEM),
         ),
         scratch_shapes=[
             vmem((LAYERS + 1, rows, width), low),
@@ -790,6 +802,10 @@
             vmem((LAYERS, half, 1), full),
             vmem((LAYERS, half, width), full),
             vmem((LAYERS, half, 1), full),
+            vmem((LAYERS, 3 * head_width, width), low),
+            vmem((LAYERS, head_width, width), low),
+            vmem((LAYERS, width, hidden_width), low),
+            vmem((LAYERS, hidden_width, width), low),
             vmem((rows, 128), full),
             vmem((half, width), full),
             vmem((half, width), full),
@@ -806,7 +822,6 @@
             vmem((rows, 3 * head_width), low),
             vmem((LAYERS, 8, width), full),
             vmem((LAYERS, 4, width), full),
-            vmem((flat, width), full),
             vmem((LANDINGS, SLOTS, UNIT, width), full),
             dma((2, BLOCKS)),
             dma((2, BLOCKS)),
@@ -818,12 +833,128 @@
             dma,
             dma((KINDS, SLOTS)),
             dma((KINDS, SLOTS)),
-            dma((2, SLOTS)),
+            dma((4, LAYERS)),
         ],
         compiler_params=pltpu.CompilerParams(
-            collective_id=0, has_side_effects=True, vmem_limit_bytes=62 << 20
+            collective_id=0, has_side_effects=True, vmem_limit_bytes=46 << 20
         ),
     )(*args)
+
+
+def place_kernel(sizes, hidden_out, grad_embeddings, every, *refs):
+    width, hidden_width, local_heads, span = sizes
+    head_width = local_heads * HEAD_DIM
+    (
+        out_hidden,
+        out_embeddings,
+        out_table,
+        out_w_qkv,
+        out_b_qv,
+        out_w_out,
+        out_b_out,
+        out_first_gain,
+        out_first_shift,
+        out_w_in,
+        out_b_in,
+        out_w_down,
+        out_b_down,
+        out_second_gain,
+        out_second_shift,
+        short,
+        sems,
+    ) = refs
+    base = LAYERS * span
+    pairs = [(every.at[pl.ds(base, CHUNK)], short), (every.at[pl.ds(base, REPL)], out_table)]
+    pairs += [(hidden_out, out_hidden), (grad_embeddings, out_embeddings)]
+    for turn in range(LAYERS):
+        first = span * turn
+        for ref, rows in (
+            (out_w_down, hidden_width),
+            (out_w_in, width),
+            (out_w_out, head_width),
+            (out_w_qkv, 3 * head_width),
+        ):
+            pairs.append((every.at[pl.ds(first, rows)], ref.at[LAYERS - 1 - turn]))
+            first += rows
+    copies = [
+        pltpu.make_async_copy(source, target, sems.at[index])
+        for index, (source, target) in enumerate(pairs)
+    ]
+    for copy in copies:
+        copy.start()
+    copies[0].wait()
+    local = REPL + 8 * LAYERS
+    for ref, row, step in (
+        (out_second_gain, REPL, 8),
+        (out_second_shift, REPL + 1, 8),
+        (out_b_down, REPL + 2, 8),
+        (out_first_gain, REPL + 3, 8),
+        (out_first_shift, REPL + 4, 8),
+        (out_b_out, REPL + 5, 8),
+        (out_b_in, local, 4),
+        (out_b_qv, local + 1, 4),
+    ):
+        for turn in range(LAYERS):
+            layer = LAYERS - 1 - turn
+            ref[layer : layer + 1, :] = short[
+                row + step * turn : row + step * turn + 1, : ref.shape[1]
+            ]
+    for copy in copies[1:]:
+        copy.wait()
+
+
+def place_outputs(hidden_out, grad_embeddings, every, sizes):
+    width, hidden_width, local_heads, span = sizes
+    head_width = local_heads * HEAD_DIM
+    low, full = jnp.bfloat16, jnp.float32
+    rows = hidden_out.shape[0]
+    shapes = (
+        ((rows, width), low),
+        ((rows, width), low),
+        ((REPL, width), full),
+        ((LAYERS, 3 * head_width, width), full),
+        ((LAYERS, 2 * head_width), full),
+        ((LAYERS, head_width, width), full),
+        ((LAYERS, width), full),
+        ((LAYERS, width), full),
+        ((LAYERS, width), full),
+        ((LAYERS, width, hidden_width), full),
+        ((LAYERS, hidden_width), full),
+        ((LAYERS, hidden_width, width), full),
+        ((LAYERS, width), full),
+        ((LAYERS, width), full),
+        ((LAYERS, width), full),
+    )
+    far = pl.BlockSpec(memory_space=pl.ANY)
+    close = pl.BlockSpec(memory_space=pltpu.VMEM)
+    return pl.pallas_call(
+        functools.partial(place_kernel, sizes),
+        name="place_outputs",
+        out_shape=[jax.ShapeDtypeStruct(shape, kind) for shape, kind in shapes],
+        in_specs=[far] * 3,
+        out_specs=[close if shape[0] == LAYERS and len(shape) == 2 else far for shape, _ in shapes],
+        scratch_shapes=[
+            pltpu.VMEM((CHUNK, width), full),
+            pltpu.SemaphoreType.DMA((4 + 4 * LAYERS,)),
+        ],
+    )(hidden_out, grad_embeddings, every)
+
+
+def moved(every):
+    def kernel(source, target, sem):
+        copy = pltpu.make_async_copy(source, target, sem)
+        copy.start()
+        copy.wait()
+
+    far = pl.BlockSpec(memory_space=pl.ANY)
+    return pl.pallas_call(
+        kernel,
+        name="moved",
+        out_shape=jax.ShapeDtypeStruct(every.shape, every.dtype),
+        in_specs=[far],
+        out_specs=far,
+        scratch_shapes=[pltpu.SemaphoreType.DMA],
+    )(every)
 
 
 def on_device(*args):
@@ -833,56 +964,23 @@
     hidden_width = args[11].shape[2]
     span = 2 * hidden_width + 4 * head_width
     args = list(args)
+    args[5] = jnp.swapaxes(args[5], 1, 2)
     for index in (2, 3, 4):
         args[index] = args[index].reshape(1, PAGE_LEN)
-    hidden_out, grad_embeddings, every = run_pages(
-        args, (width, hidden_width, head_width // HEAD_DIM, span)
-    )
+    sizes = (width, hidden_width, head_width // HEAD_DIM, span)
+    hidden_out, grad_embeddings, every = run_pages(args, sizes)
     groups = lax.axis_size("dp") // GROUP
     if groups > 1:
         every = lax.psum(
-            every,
+            moved(every),
             "dp",
             axis_index_groups=[
                 [low + GROUP * high for high in range(groups)] for low in range(GROUP)
             ],
         )
 
-    def piece(first, rows):
-        return jnp.stack(
-            [
-                lax.slice_in_dim(every, start, start + rows)
-                for start in [first + span * turn for turn in reversed(range(LAYERS))]
-            ]
-        )
-
-    base = LAYERS * span
-
-    def short(row, step):
-        return jnp.stack([every[base + row + step * turn] for turn in reversed(range(LAYERS))])
-
-    grad_w_down = piece(0, hidden_width)
-    grad_w_in = piece(hidden_width, width)
-    grad_w_out = piece(hidden_width + width, head_width)
-    grad_w_qkv = jnp.swapaxes(piece(hidden_width + width + head_width, 3 * head_width), 1, 2)
-    local = REPL + 8 * LAYERS
-    return (
-        hidden_out,
-        grad_embeddings,
-        lax.slice_in_dim(every, base, base + REPL),
-        grad_w_qkv,
-        short(local + 1, 4)[:, : 2 * head_width],
-        grad_w_out,
-        short(REPL + 5, 8),
-        short(REPL + 3, 8),
-        short(REPL + 4, 8),
-        grad_w_in,
-        short(local, 4),
-        grad_w_down,
-        short(REPL + 2, 8),
-        short(REPL, 8),
-        short(REPL + 1, 8),
-    )
+    results = place_outputs(hidden_out, grad_embeddings, every, sizes)
+    return (*results[:3], jnp.swapaxes(results[3], 1, 2), *results[4:])
 
 
 def solution(mesh):

time: 382 us -> 841 us (2.20)
  Pallas kernels: 354 us -> 833 us
  other arithmetic: 10.5 us -> 0 us
  local copies, waits for them, and re-layouts: 16.3 us -> 6.92 us
    pallas_call x0 -> x1, Pallas kernels: none -> 481 us  [place_outputs(): pl.pallas_call(functools.partial(place_kernel, sizes), name='place_output...]
    another operation x7 -> x0, other arithmetic: 8.44 us -> none  [the longest x2 5.43 us: piece(): jnp.stack([lax.slice_in_dim(every, start, start + rows) for start in [fir...]
where the time goes in v3:
time: 841 us
  Pallas kernels  833 us (99%)
    pallas_call x1, Pallas kernels, place_outputs(): pl.pallas_call(functools.partial(place_kernel, sizes), name='place_output...  481 us
    pallas_call x1, Pallas kernels, run_pages(): pl.pallas_call(functools.partial(page_kernel, sizes), name='pages', out_s...  352 us

profile of v3, /device:TPU:0, one launch (start us, length us, event | category | flops | bytes accessed | tf_op | source)
XLA Modules:
  0.0 840.8 jit_solution(92462648446281787)
XLA Ops:
  0.7 351.9 %pages.1 = (bf16[512,768]{1,0:T(8,128)(2,1)S(1)}, bf16[512,768]{1,0:T(8,128)(2,1)S(1)}, f32[4672,768]{1,0:T(8,128)S(1)}) custom-call(bf16[512,768]{1,0:T(8,128)(2,1)} %embeddings.1, bf16[32,768]{1,0:T(8,128)(2,1)} %replace_table.1, s32[1,512]{1,0:T(1,128)} %bitcast.6, s32[1,512]{1,0:T(1,128)} %bitcast.7, s32[1,512]{1,0:T(1,128)} %bitcast.8, ...), custom_call_target="tpu_custom_call" | custom-call | tf_op jit(solution)/shard_map/pages/pallas_call | solution.py:774
  352.6 0.0 copy-start
  352.6 5.1 copy-done
  357.7 0.0 copy-start.1
  357.7 0.9 copy-done.1
  358.6 0.0 copy-start.2
  358.6 0.9 copy-done.2
  359.5 481.3 %place_outputs.1 = (bf16[512,768]{1,0:T(8,128)(2,1)}, bf16[512,768]{1,0:T(8,128)(2,1)}, f32[32,768]{1,0:T(8,128)}, f32[2,576,768]{2,1,0:T(8,128)}, f32[2,384]{1,...) custom-call(bf16[512,768]{1,0:T(8,128)(2,1)} %copy-done.1, ...), custom_call_target="tpu_custom_call" | custom-call | tf_op jit(solution)/shard_map/place_outputs/pallas_call | solution.py:930
Async XLA Ops:
  352.6 5.1 copy-start
  357.7 0.9 copy-start.1
  358.6 0.9 copy-start.2

commit v4 on v3

--- a/solution.py
+++ b/solution.py
@@ -937,6 +937,7 @@
             pltpu.VMEM((CHUNK, width), full),
             pltpu.SemaphoreType.DMA((4 + 4 * LAYERS,)),
         ],
+        compiler_params=pltpu.CompilerParams(vmem_limit_bytes=4 << 20),
     )(hidden_out, grad_embeddings, every)
 
 
@@ -954,6 +955,7 @@
         in_specs=[far],
         out_specs=far,
         scratch_shapes=[pltpu.SemaphoreType.DMA],
+        compiler_params=pltpu.CompilerParams(vmem_limit_bytes=4 << 20),
     )(every)
 
 

time: 841 us -> 359 us (0.43)
  Pallas kernels: 833 us -> 358 us
    pallas_call x1, Pallas kernels: 481 us -> 6.6 us  [place_outputs(): pl.pallas_call(functools.partial(place_kernel, sizes), name='place_output...]
where the time goes in v4:
time: 359 us
  Pallas kernels  358 us (100%)
    pallas_call x1, Pallas kernels, run_pages(): pl.pallas_call(functools.partial(page_kernel, sizes), name='pages', out_s...  352 us

profile of v4, /device:TPU:0, one launch (start us, length us, event | category | flops | bytes accessed | tf_op | source)
XLA Modules:
  0.0 359.2 jit_solution(8499933942230454753)
XLA Ops:
  0.7 351.9 %pages.1 = (bf16[512,768]{1,0:T(8,128)(2,1)S(1)}, bf16[512,768]{1,0:T(8,128)(2,1)S(1)}, f32[4672,768]{1,0:T(8,128)S(1)}) custom-call(bf16[512,768]{1,0:T(8,128)(2,1)} %embeddings.1, bf16[32,768]{1,0:T(8,128)(2,1)} %replace_table.1, s32[1,512]{1,0:T(1,128)} %bitcast.6, s32[1,512]{1,0:T(1,128)} %bitcast.7, s32[1,512]{1,0:T(1,128)} %bitcast.8, ...), custom_call_target="tpu_custom_call" | custom-call | tf_op jit(solution)/shard_map/pages/pallas_call | solution.py:774
  352.6 6.6 %place_outputs.1 = (bf16[512,768]{1,0:T(8,128)(2,1)}, bf16[512,768]{1,0:T(8,128)(2,1)}, f32[32,768]{1,0:T(8,128)}, f32[2,576,768]{2,1,0:T(8,128)}, f32[2,384]{1,...) custom-call(bf16[512,768]{1,0:T(8,128)(2,1)S(1)} %get-tuple-element., ...), custom_call_target="tpu_custom_call" | custom-call | tf_op jit(solution)/shard_map/place_outputs/pallas_call | solution.py:930

commit v5 on v4

--- a/solution.py
+++ b/solution.py
@@ -16,9 +16,12 @@
 SCALE = HEAD_DIM ** (-0.5)
 MESH = pl.DeviceIdType.MESH
 
-BLOCK = 128
-OWN = BLOCK // 2
-BLOCKS = PAGE_LEN // BLOCK
+HALF = PAGE_LEN // 2
+SEG = 64
+BLOCKS = HALF // SEG
+BACK_SEG = 64
+BACK_BLOCKS = HALF // BACK_SEG
+BLOCK = 2 * BACK_SEG
 
 UNIT = 16
 CHUNK = 4 * UNIT
@@ -29,6 +32,7 @@
 LANDINGS = TTA + 1
 GROUP = 8
 WEIGHTS = (5, 7, 11, 13)
+DIRECT = (128, 0)
 
 
 def contract_rows(left, right):
@@ -85,6 +89,12 @@
         self.core = lax.rem(t, 2)
         self.core_peer = (d, t + 1 - 2 * self.core)
         self.y_peer = (d, t + 2 - 4 * lax.div(t, 2))
+        self.diagonal = (d, t + 3 - 2 * self.core - 4 * lax.div(t, 2))
+        self.y = lax.div(t, 2)
+        self.low = lax.rem(d, GROUP)
+        self.others = [
+            (d - self.low + lax.rem(self.low + k, GROUP), t) for k in range(1, GROUP)
+        ]
         pair = lax.rem(d, 2)
         line = lax.rem(lax.div(d, 2), 4)
         self.pair = pair
@@ -100,13 +110,12 @@
     def signal(device):
         pl.semaphore_signal(barrier, inc=1, device_id=device, device_id_type=MESH)
 
-    for device in (place.core_peer, place.y_peer, place.peer, place.line):
+    for device in (place.core_peer, place.y_peer, place.diagonal, *place.others):
         signal(device)
-    pl.when(place.mid)(lambda: signal(place.cross))
-
-
-def meet(place, barrier):
-    pl.semaphore_wait(barrier, jnp.where(place.mid, 5, 4))
+
+
+def meet(barrier):
+    pl.semaphore_wait(barrier, 2 + GROUP)
 
 
 class GradientSum:
@@ -309,6 +318,8 @@
     w_out,
     w_in,
     w_down,
+    w_all,
+    shared_heads,
     columns,
     own_a,
     own_b,
@@ -337,6 +348,12 @@
     dp_send,
     dp_recv,
     weight_sem,
+    gather_send,
+    gather_recv,
+    hand_send,
+    hand_recv,
+    heads_send,
+    heads_recv,
 ):
     width, hidden_width, local_heads, span = sizes
     head_width = local_heads * HEAD_DIM
@@ -352,9 +369,8 @@
             source.at[layer], target.at[layer], weight_sem.at[index, layer]
         )
 
-    for layer in range(LAYERS):
-        for index in range(len(weights)):
-            weight(index, layer).start()
+    for index, layer in ((0, 0), (1, 0), (1, 1), (2, 0), (3, 0), (0, 1), (2, 1), (3, 1)):
+        weight(index, layer).start()
     small_base = LAYERS * span
     chunks = grads.shape[0] // CHUNK
     grad_sum = GradientSum(place, chunks, grads, landing, dp_send, dp_recv)
@@ -367,14 +383,20 @@
     def block(b):
         return pl.ds(pl.multiple_of(b * BLOCK, BLOCK), BLOCK)
 
-    def kept(b):
-        return pl.ds(pl.multiple_of(b * BLOCK + core * OWN, OWN), OWN)
-
-    def given(b):
-        return pl.ds(pl.multiple_of(b * BLOCK + (1 - core) * OWN, OWN), OWN)
-
-    def packed(b):
-        return pl.ds(pl.multiple_of(b * OWN, OWN), OWN)
+    def segment(b, size, half):
+        return pl.ds(pl.multiple_of(half * HALF + b * size, size), size)
+
+    def kept(b, size):
+        return segment(b, size, core)
+
+    def given(b, size):
+        return segment(b, size, 1 - core)
+
+    def packed(b, size):
+        return segment(b, size, 0)
+
+    def halves(b, size):
+        return segment(b, size, 0), segment(b, size, 1)
 
     def lanes(p, size=128):
         return pl.ds(pl.multiple_of(p * size, size), size)
@@ -389,41 +411,182 @@
             device_id_type=MESH,
         )
 
-    def to_core(turn, b):
+    def to_core(turn, b, size):
         return remote(
-            part.at[given(b)],
-            land_core.at[turn, b],
+            part.at[given(b, size)],
+            land_core.at[turn, packed(b, size)],
             core_send.at[turn, b],
             core_recv.at[turn, b],
             place.core_peer,
         )
 
-    def over_y(turn, b):
+    def over_y(turn, b, size):
         return remote(
-            part.at[kept(b)],
-            land_y.at[turn, b],
+            part.at[kept(b, size)],
+            land_y.at[turn, packed(b, size)],
             y_send.at[turn, b],
             y_recv.at[turn, b],
             place.y_peer,
         )
 
-    def to_other(turn, b, source):
+    def to_other(turn, b, size, source):
         return remote(
-            source.at[packed(b)],
-            land_back.at[turn, b],
+            source.at[packed(b, size)],
+            land_back.at[turn, packed(b, size)],
             back_send.at[turn, b],
             back_recv.at[turn, b],
             place.core_peer,
         )
 
-    def send_y(turn, b):
-        to_core(turn, b).wait()
-        part[kept(b), :] = part[kept(b), :] + land_core[turn, b]
-        over_y(turn, b).start()
-
-    def summed(turn, b):
-        over_y(turn, b).wait()
-        return part[kept(b), :] + land_y[turn, b]
+    def send_y(turn, b, size):
+        to_core(turn, b, size).wait()
+        rows = kept(b, size)
+        part[rows, :] = part[rows, :] + land_core[turn, packed(b, size), :]
+        over_y(turn, b, size).start()
+
+    def summed(turn, b, size):
+        over_y(turn, b, size).wait()
+        return part[kept(b, size), :] + land_y[turn, packed(b, size), :]
+
+    def received(turn, b, size, source):
+        to_other(turn, b, size, source).wait()
+        return land_back[turn, packed(b, size), :].astype(jnp.bfloat16)
+
+    def shard(which, layer):
+        return (which * LAYERS + layer) * head_width
+
+    def direct(layer):
+        return pl.ds(shard(0, layer), DIRECT[layer]), pl.ds(shard(2, layer), DIRECT[layer])
+
+    def piece_rows(which, layer, owner):
+        size = (head_width - DIRECT[layer]) // GROUP
+        first = shard(which, layer) + DIRECT[layer] + owner * size
+        return pl.ds(pl.multiple_of(first, 8), size)
+
+    def moving(source, target, index, device):
+        return remote(
+            grads.at[source], grads.at[target], gather_send.at[index], gather_recv.at[index], device
+        )
+
+    def whole(which, layer):
+        return pl.ds(shard(which, layer), head_width)
+
+    def own_shard(layer):
+        return moving(whole(0, layer), whole(1, layer), layer, place.core_peer)
+
+    def other_shard(layer):
+        return moving(whole(2, layer), whole(3, layer), LAYERS + layer, place.core_peer)
+
+    def piece_over(layer):
+        return moving(
+            piece_rows(0, layer, place.low),
+            piece_rows(2, layer, place.low),
+            2 * LAYERS + layer,
+            place.y_peer,
+        )
+
+    def rest_over(layer):
+        return moving(*direct(layer), 3 * LAYERS + layer, place.y_peer)
+
+    def handed(layer, k):
+        rows = piece_rows(2, layer, place.low)
+        return pltpu.make_async_remote_copy(
+            src_ref=grads.at[rows],
+            dst_ref=grads.at[rows],
+            send_sem=hand_send.at[layer, k],
+            recv_sem=hand_recv.at[layer, place.low],
+            device_id=place.others[k],
+            device_id_type=MESH,
+        )
+
+    def handed_in(layer, k):
+        owner = lax.rem(place.low + 1 + k, GROUP)
+        rows = piece_rows(2, layer, owner)
+        return pltpu.make_async_remote_copy(
+            src_ref=grads.at[rows],
+            dst_ref=grads.at[rows],
+            send_sem=hand_send.at[layer, k],
+            recv_sem=hand_recv.at[layer, owner],
+            device_id=place.others[k],
+            device_id_type=MESH,
+        )
+
+    def gather_first(layer):
+        weight(1, layer).wait()
+        grads[whole(0, layer), :] = w_out[layer].astype(jnp.float32)
+        piece_over(layer).start()
+        if DIRECT[layer]:
+            rest_over(layer).start()
+        own_shard(layer).start()
+
+    def gather_second(layer):
+        piece_over(layer).wait()
+        for k in range(GROUP - 1):
+            handed(layer, k).start()
+
+    def gather_third(layer):
+        for k in range(GROUP - 1):
+            handed(layer, k).wait_send()
+            handed_in(layer, k).wait_recv()
+        if DIRECT[layer]:
+            rest_over(layer).wait()
+        other_shard(layer).start()
+
+    def gather_last(layer):
+        own_shard(layer).wait()
+        other_shard(layer).wait()
+        pairs_width = 2 * HEAD_DIM
+        for which in range(4):
+            source = which // 2
+            owner = 2 * (place.y + source - 2 * place.y * source) + (
+                core + which % 2 - 2 * core * (which % 2)
+            )
+            low = grads[whole(which, layer), :].astype(jnp.bfloat16)
+            first = pl.multiple_of(owner * pairs_width, pairs_width)
+            w_all[layer, pl.ds(first, pairs_width), :] = low[:pairs_width]
+            first = pl.multiple_of(4 * pairs_width + owner * HEAD_DIM, HEAD_DIM)
+            w_all[layer, pl.ds(first, HEAD_DIM), :] = low[pairs_width:]
+
+    def heads_out(b):
+        mine, theirs = shared_heads.at[core, b], shared_heads.at[1 - core, b]
+        return [
+            remote(
+                source,
+                shared_heads.at[2 + index, b],
+                heads_send.at[index, b],
+                heads_recv.at[index, b],
+                device,
+            )
+            for index, (source, device) in enumerate(
+                (
+                    (theirs, place.core_peer),
+                    (mine, place.y_peer),
+                    (theirs, place.diagonal),
+                )
+            )
+        ]
+
+    def pack_heads(rows):
+        cut = 2 * HEAD_DIM
+        return jnp.concatenate(
+            [
+                rows[:, :cut],
+                jnp.concatenate([rows[: SEG // 2, cut:], rows[SEG // 2 :, cut:]], axis=1),
+            ],
+            axis=0,
+        )
+
+    def all_heads(b):
+        pairs, thirds = [], []
+        for owner in range(4):
+            side, half = owner // 2, owner % 2
+            apart = 2 * (place.y + side - 2 * place.y * side) + (core + half - 2 * core * half)
+            slot = jnp.where(apart == 0, core, apart + 1)
+            low = shared_heads[slot, b].astype(jnp.bfloat16)
+            pairs.append(low[:SEG])
+            tail = low[SEG:]
+            thirds.append(jnp.concatenate([tail[:, :HEAD_DIM], tail[:, HEAD_DIM:]], axis=0))
+        return jnp.concatenate(pairs + thirds, axis=1)
 
     pad_row = padding[...].astype(jnp.float32)
     live_row = masked[...].astype(jnp.float32) * pad_row
@@ -444,119 +607,186 @@
         )
         inputs_low[0, rows, :] = taken.astype(jnp.bfloat16)
 
-    repeat(BLOCKS, first_input)
-
-    def scores_of(layer, h, rows):
-        return contract_cols(queries[layer, h, rows, :], keys[layer, h]) * SCALE + bias_row
+    sums[...] = jnp.zeros_like(sums)
+    local_sums[...] = jnp.zeros_like(local_sums)
+
+    def project(layer, spans):
+        bias_pair = vector(b_qv, layer)
+        inputs = jnp.concatenate([inputs_low[layer, rows, :] for rows in spans], axis=0)
+        projected = contract_cols(inputs, w_qkv[layer])
+
+        def split(ref, h, columns_of):
+            low = columns_of.astype(jnp.bfloat16)
+            first = 0
+            for rows in spans:
+                ref[layer, h, rows, :] = low[first : first + rows.size]
+                first += rows.size
+
+        for h in range(local_heads):
+            base = 3 * HEAD_DIM * h
+            bias = 2 * HEAD_DIM * h
+            split(
+                queries,
+                h,
+                projected[:, base : base + HEAD_DIM] + bias_pair[:, bias : bias + HEAD_DIM],
+            )
+            split(keys, h, projected[:, base + HEAD_DIM : base + 2 * HEAD_DIM])
+            split(
+                values,
+                h,
+                projected[:, base + 2 * HEAD_DIM : base + 3 * HEAD_DIM]
+                + bias_pair[:, bias + HEAD_DIM : bias + 2 * HEAD_DIM],
+            )
+
+    def scores_of(layer, h, query):
+        return contract_cols(query, keys[layer, h]) * SCALE + bias_row
+
+    def total_row(turn, index, amount):
+        sums[turn, index : index + 1, :] = sums[turn, index : index + 1, :] + jnp.sum(
+            amount, axis=0, keepdims=True
+        )
+
+    def norm_two(turn, b, size, grad):
+        layer = LAYERS - 1 - turn
+        rows = packed(b, size)
+        zhat = zhat_two[layer, rows, :]
+        dz = norm_back(grad, zhat, scale_two[layer, rows, :], vector(second_gain, layer))
+        own_a[rows, :] = dz
+        to_other(0, b, size, own_a).start()
+        dz_low[kept(b, size), :] = dz.astype(jnp.bfloat16)
+        total_row(turn, 0, grad * zhat)
+        total_row(turn, 1, grad)
+        total_row(turn, 2, dz)
 
     def forward(layer):
-        bias_pair = vector(b_qv, layer)
-
-        def project(b):
-            rows = block(b)
-            projected = contract_cols(inputs_low[layer, rows, :], w_qkv[layer])
+        last = layer == LAYERS - 1
+
+        def attend(b):
+            spans = halves(b, SEG)
+            outs, logs = [], []
             for h in range(local_heads):
-                base = 3 * HEAD_DIM * h
-                bias = 2 * HEAD_DIM * h
-                queries[layer, h, rows, :] = (
-                    projected[:, base : base + HEAD_DIM] + bias_pair[:, bias : bias + HEAD_DIM]
-                ).astype(jnp.bfloat16)
-                keys[layer, h, rows, :] = projected[
-                    :, base + HEAD_DIM : base + 2 * HEAD_DIM
-                ].astype(jnp.bfloat16)
-                values[layer, h, rows, :] = (
-                    projected[:, base + 2 * HEAD_DIM : base + 3 * HEAD_DIM]
-                    + bias_pair[:, bias + HEAD_DIM : bias + 2 * HEAD_DIM]
-                ).astype(jnp.bfloat16)
-
-        weight(0, layer).wait()
-        repeat(BLOCKS, project)
-        pl.when(layer == 0)(lambda: meet(place, barrier))
-        weight(1, layer).wait()
-
-        def attend(b):
-            rows = block(b)
-            outs = []
-            for h in range(local_heads):
-                scores = scores_of(layer, h, rows)
+                query = jnp.concatenate([queries[layer, h, rows, :] for rows in spans], axis=0)
+                scores = scores_of(layer, h, query)
                 largest = jnp.max(scores, axis=-1, keepdims=True)
-                weights = jnp.exp(scores - largest)
-                totals = jnp.sum(weights, axis=-1, keepdims=True)
-                probs = (weights * (1.0 / totals)).astype(jnp.bfloat16)
+                weights_of = jnp.exp(scores - largest)
+                totals = jnp.sum(weights_of, axis=-1, keepdims=True)
+                probs = (weights_of * (1.0 / totals)).astype(jnp.bfloat16)
                 outs.append(matmul(probs, values[layer, h]).astype(jnp.bfloat16))
-                log_total[layer, rows, h : h + 1] = largest + jnp.log(totals)
+                logs.append(largest + jnp.log(totals))
             joined = jnp.concatenate(outs, axis=1)
-            heads[layer, rows, :] = joined
-            part[rows, :] = matmul(joined, w_out[layer])
-            to_core(0, b).start()
-            pl.when(b >= 1)(lambda: send_y(0, b - 1))
+            full = joined.astype(jnp.float32)
+            for side in range(2):
+                shared_heads[side, b] = pack_heads(full[side * SEG : (side + 1) * SEG])
+            for copy in heads_out(b):
+                copy.start()
+            for side, rows in enumerate(spans):
+                cut = slice(side * SEG, (side + 1) * SEG)
+                heads[layer, rows, :] = joined[cut]
+                for h in range(local_heads):
+                    log_total[layer, rows, h : h + 1] = logs[h][cut]
 
         repeat(BLOCKS, attend)
-        send_y(0, BLOCKS - 1)
-
-        gain, shift, bias_out = vector(first_gain, layer), vector(first_shift, layer), vector(b_out, layer)
+
+        @pl.when(layer == 0)
+        def _():
+            gather_third(0)
+            gather_second(1)
+            gather_last(0)
+
+        gain, shift, bias_out = (
+            vector(first_gain, layer),
+            vector(first_shift, layer),
+            vector(b_out, layer),
+        )
         bias_in = vector(b_in, layer)
-
-        def feed(b):
-            rows = block(b)
-            before = (
-                inputs_low[layer, kept(b), :].astype(jnp.float32) + summed(0, b) + bias_out
-            )
-            zhat, scale = normed(before)
-            zhat_one[layer, packed(b), :] = zhat
-            scale_one[layer, packed(b), :] = scale
-            result = zhat * gain + shift
-            own_a[packed(b), :] = result
-            to_other(0, b, own_a).start()
-            normed_low[layer, kept(b), :] = result.astype(jnp.bfloat16)
-            pl.when(b >= 1)(lambda: send_y(1, b - 1))
-            to_other(0, b, own_a).wait()
-            normed_low[layer, given(b), :] = land_back[0, b].astype(jnp.bfloat16)
-            u = matmul(normed_low[layer, rows, :], w_in[layer]) + bias_in
-            hidden[layer, rows, :] = u
-            g = (u * normal_cdf(u)).astype(jnp.bfloat16)
-            active[layer, rows, :] = g
-            part[rows, :] = matmul(g, w_down[layer])
-            to_core(1, b).start()
-
         weight(2, layer).wait()
         weight(3, layer).wait()
-        repeat(BLOCKS, feed)
-        send_y(1, BLOCKS - 1)
+
+        def feed_norm(b):
+            rows = packed(b, SEG)
+            for copy in heads_out(b):
+                copy.wait()
+            before = (
+                inputs_low[layer, kept(b, SEG), :].astype(jnp.float32)
+                + matmul(all_heads(b), w_all[layer])
+                + bias_out
+            )
+            zhat, scale = normed(before)
+            result = zhat * gain + shift
+            own_a[rows, :] = result
+            to_other(0, b, SEG, own_a).start()
+            zhat_one[layer, rows, :] = zhat
+            scale_one[layer, rows, :] = scale
+            normed_low[layer, kept(b, SEG), :] = result.astype(jnp.bfloat16)
+
+        def feed_main(b):
+            spans = halves(b, SEG)
+            normed_low[layer, given(b, SEG), :] = received(0, b, SEG, own_a)
+            inputs = jnp.concatenate([normed_low[layer, rows, :] for rows in spans], axis=0)
+            u = matmul(inputs, w_in[layer]) + bias_in
+            g = (u * normal_cdf(u)).astype(jnp.bfloat16)
+            lowered = matmul(g, w_down[layer])
+            for side, rows in enumerate(spans):
+                cut = slice(side * SEG, (side + 1) * SEG)
+                part[rows, :] = lowered[cut]
+                hidden[layer, rows, :] = u[cut]
+                active[layer, rows, :] = g[cut]
+            to_core(1, b, SEG).start()
+
+        def feed(b):
+            pl.when(b < BLOCKS)(lambda: feed_norm(b))
+            pl.when(b >= 2)(lambda: send_y(1, b - 2, SEG))
+            pl.when(b >= 1)(lambda: feed_main(b - 1))
+
+        repeat(BLOCKS + 1, feed)
+        pl.when(layer == 0)(lambda: gather_third(1))
+        send_y(1, BLOCKS - 1, SEG)
+        pl.when(layer == 0)(lambda: gather_last(1))
 
         gain_two, shift_two, bias_down = (
             vector(second_gain, layer),
             vector(second_shift, layer),
             vector(b_down, layer),
         )
+        pl.when(jnp.logical_not(last))(lambda: weight(0, layer + 1).wait())
 
         def receive(b):
-            to_other(1, b, own_b).wait()
-            inputs_low[layer + 1, given(b), :] = land_back[1, b].astype(jnp.bfloat16)
+            inputs_low[layer + 1, given(b, SEG), :] = received(1, b, SEG, own_b)
+            pl.when(jnp.logical_not(last))(lambda: project(layer + 1, halves(b, SEG)))
+
+            @pl.when(last)
+            def _():
+                dz_low[given(b, SEG), :] = received(0, b, SEG, own_a)
 
         def finish(b):
-            before = own_a[packed(b), :] + summed(1, b) + bias_down
+            rows = packed(b, SEG)
+            before = own_a[rows, :] + summed(1, b, SEG) + bias_down
             zhat, scale = normed(before)
-            zhat_two[layer, packed(b), :] = zhat
-            scale_two[layer, packed(b), :] = scale
             result = zhat * gain_two + shift_two
-            own_b[packed(b), :] = result
-            to_other(1, b, own_b).start()
-            inputs_low[layer + 1, kept(b), :] = result.astype(jnp.bfloat16)
+            own_b[rows, :] = result
+            to_other(1, b, SEG, own_b).start()
+            zhat_two[layer, rows, :] = zhat
+            scale_two[layer, rows, :] = scale
+            inputs_low[layer + 1, kept(b, SEG), :] = result.astype(jnp.bfloat16)
+
+            @pl.when(last)
+            def _():
+                live = columns[kept(b, SEG), 0:1]
+                norm_two(0, b, SEG, cotangent[kept(b, SEG), :].astype(jnp.float32) * live)
+
             pl.when(b >= 1)(lambda: receive(b - 1))
 
         repeat(BLOCKS, finish)
         receive(BLOCKS - 1)
 
+    meet(barrier)
+    gather_first(0)
+    gather_first(1)
+    repeat(BACK_BLOCKS, first_input)
+    weight(0, 0).wait()
+    repeat(BACK_BLOCKS, lambda b: project(0, (block(b),)))
+    gather_second(0)
     repeat(LAYERS, forward)
-    hidden_out[...] = inputs_low[LAYERS]
-
-    def first_grad(b):
-        own_b[packed(b), :] = cotangent[kept(b), :].astype(jnp.float32) * columns[kept(b), 0:1]
-
-    repeat(BLOCKS, first_grad)
-    sums[...] = jnp.zeros_like(sums)
-    local_sums[...] = jnp.zeros_like(local_sums)
 
     def backward(turn):
         layer = LAYERS - 1 - turn
@@ -568,31 +798,6 @@
 
         def rows_at(first, count):
             return pl.ds(pl.multiple_of(first, 64), count)
-
-        def total_row(index, amount):
-            sums[turn, index : index + 1, :] = sums[turn, index : index + 1, :] + jnp.sum(
-                amount, axis=0, keepdims=True
-            )
-
-        def receive(back, b, source):
-            to_other(back, b, source).wait()
-            dz_low[given(b), :] = land_back[back, b].astype(jnp.bfloat16)
-
-        gain_two = vector(second_gain, layer)
-
-        def norm_two(b):
-            grad = own_b[packed(b), :]
-            zhat = zhat_two[layer, packed(b), :]
-            dz = norm_back(grad, zhat, scale_two[layer, packed(b), :], gain_two)
-            own_a[packed(b), :] = dz
-            to_other(0, b, own_a).start()
-            dz_low[kept(b), :] = dz.astype(jnp.bfloat16)
-            total_row(0, grad * zhat)
-            total_row(1, grad)
-            total_row(2, dz)
-
-        repeat(BLOCKS, norm_two)
-        repeat(BLOCKS, lambda b: receive(0, b, own_a))
 
         def down_piece(p):
             grads[rows_at(base + 128 * p, 128), :] = contract_rows(
@@ -622,19 +827,23 @@
             tick(start + 2 + 2 * b)
             tick(start + 3 + 2 * b)
 
-        repeat(BLOCKS, feed)
+        repeat(BACK_BLOCKS, feed)
         down_piece(5)
 
         def feed_in(b):
-            rows = block(b)
-            part[rows, :] = contract_cols(du_low[rows, :], w_in[layer])
-            to_core(0, b).start()
+            spans = halves(b, BACK_SEG)
+            left = jnp.concatenate([du_low[rows, :] for rows in spans], axis=0)
+            result = contract_cols(left, w_in[layer])
+            for side, rows in enumerate(spans):
+                part[rows, :] = result[side * BACK_SEG : (side + 1) * BACK_SEG]
+            to_core(0, b, BACK_SEG).start()
+            pl.when(b >= 1)(lambda: send_y(0, b - 1, BACK_SEG))
             in_piece(b)
             tick(start + 10 + 2 * b)
-            send_y(0, b)
             tick(start + 11 + 2 * b)
 
-        repeat(BLOCKS, feed_in)
+        repeat(BACK_BLOCKS, feed_in)
+        send_y(0, BACK_BLOCKS - 1, BACK_SEG)
         in_piece(4)
         tick(start + 18)
         in_piece(5)
@@ -643,19 +852,20 @@
         gain = vector(first_gain, layer)
 
         def norm_one(b):
-            grad = own_a[packed(b), :] + summed(0, b)
-            zhat = zhat_one[layer, packed(b), :]
-            dz = norm_back(grad, zhat, scale_one[layer, packed(b), :], gain)
-            own_b[packed(b), :] = dz
-            to_other(1, b, own_b).start()
-            dz_low[kept(b), :] = dz.astype(jnp.bfloat16)
-            total_row(3, grad * zhat)
-            total_row(4, grad)
-            total_row(5, dz)
+            rows = packed(b, BACK_SEG)
+            grad = own_a[rows, :] + summed(0, b, BACK_SEG)
+            zhat = zhat_one[layer, rows, :]
+            dz = norm_back(grad, zhat, scale_one[layer, rows, :], gain)
+            own_b[rows, :] = dz
+            to_other(1, b, BACK_SEG, own_b).start()
+            dz_low[kept(b, BACK_SEG), :] = dz.astype(jnp.bfloat16)
+            total_row(turn, 3, grad * zhat)
+            total_row(turn, 4, grad)
+            total_row(turn, 5, dz)
             tick(start + 20 + b)
-            receive(1, b, own_b)
-
-        repeat(BLOCKS, norm_one)
+            dz_low[given(b, BACK_SEG), :] = received(1, b, BACK_SEG, own_b)
+
+        repeat(BACK_BLOCKS, norm_one)
         grads[rows_at(out_base, head_width), :] = contract_rows(heads[layer], dz_low[...])
         dheads[...] = contract_cols(dz_low[...], w_out[layer]).astype(jnp.bfloat16)
         dkeys[...] = jnp.zeros_like(dkeys)
@@ -665,21 +875,22 @@
             rows = block(b)
             for h in range(local_heads):
                 side = HEAD_DIM * h
-                probs = jnp.exp(scores_of(layer, h, rows) - log_total[layer, rows, h : h + 1])
+                query = queries[layer, h, rows, :]
+                probs = jnp.exp(scores_of(layer, h, query) - log_total[layer, rows, h : h + 1])
                 dhead = dheads[rows, side : side + HEAD_DIM]
                 dprobs = contract_cols(dhead, values[layer, h])
                 dvalues[h] = dvalues[h] + contract_rows(probs.astype(jnp.bfloat16), dhead)
                 inner = jnp.sum(probs * dprobs, axis=-1, keepdims=True)
                 ds = (probs * (dprobs - inner)).astype(jnp.bfloat16)
                 dq = matmul(ds, keys[layer, h]) * SCALE
-                dkeys[h] = dkeys[h] + contract_rows(ds, queries[layer, h, rows, :])
+                dkeys[h] = dkeys[h] + contract_rows(ds, query)
                 dqkv_low[rows, 3 * side : 3 * side + HEAD_DIM] = dq.astype(jnp.bfloat16)
                 local_sums[turn, 1:2, 2 * side : 2 * side + HEAD_DIM] = local_sums[
                     turn, 1:2, 2 * side : 2 * side + HEAD_DIM
                 ] + jnp.sum(dq, axis=0, keepdims=True)
-            pl.when(b < BLOCKS - 1)(lambda: tick(start + 24 + b))
-
-        repeat(BLOCKS, attend)
+            pl.when(b < BACK_BLOCKS - 1)(lambda: tick(start + 24 + b))
+
+        repeat(BACK_BLOCKS, attend)
         for h in range(local_heads):
             side = HEAD_DIM * h
             dqkv_low[:, 3 * side + HEAD_DIM : 3 * side + 2 * HEAD_DIM] = (
@@ -693,14 +904,17 @@
                 dv, axis=0, keepdims=True
             )
 
-        def project(b):
-            rows = block(b)
-            part[rows, :] = matmul(dqkv_low[rows, :], w_qkv[layer])
-            to_core(1, b).start()
-            pl.when(b >= 1)(lambda: send_y(1, b - 1))
-
-        repeat(BLOCKS, project)
-        send_y(1, BLOCKS - 1)
+        def back_project(b):
+            spans = halves(b, BACK_SEG)
+            left = jnp.concatenate([dqkv_low[rows, :] for rows in spans], axis=0)
+            result = matmul(left, w_qkv[layer])
+            for side, rows in enumerate(spans):
+                part[rows, :] = result[side * BACK_SEG : (side + 1) * BACK_SEG]
+            to_core(1, b, BACK_SEG).start()
+            pl.when(b >= 1)(lambda: send_y(1, b - 1, BACK_SEG))
+
+        repeat(BACK_BLOCKS, back_project)
+        send_y(1, BACK_BLOCKS - 1, BACK_SEG)
 
         def qkv_piece(p):
             grads[rows_at(qkv_base + 128 * p, 128), :] = contract_rows(
@@ -716,30 +930,40 @@
         tick(start + 35)
 
         def pass_on(b):
-            own_b[packed(b), :] = own_b[packed(b), :] + summed(1, b)
-
-        repeat(BLOCKS, pass_on)
+            rows = packed(b, BACK_SEG)
+            grad = own_b[rows, :] + summed(1, b, BACK_SEG)
+            own_b[rows, :] = grad
+            pl.when(turn < LAYERS - 1)(lambda: norm_two(turn + 1, b, BACK_SEG, grad))
+
+        repeat(BACK_BLOCKS, pass_on)
+
+        def receive(b):
+            dz_low[given(b, BACK_SEG), :] = received(0, b, BACK_SEG, own_a)
+
+        pl.when(turn < LAYERS - 1)(lambda: repeat(BACK_BLOCKS, receive))
 
     repeat(LAYERS, backward)
+    hidden_out[...] = inputs_low[LAYERS]
 
     def last_grad(b):
-        live = columns[kept(b), 0:1]
-        grad = own_b[packed(b), :]
+        rows = kept(b, BACK_SEG)
+        live = columns[rows, 0:1]
+        grad = own_b[packed(b, BACK_SEG), :]
         masked_grad = grad * (1.0 - live)
-        own_a[packed(b), :] = masked_grad
-        to_other(0, b, own_a).start()
-        grad_embeddings[kept(b), :] = masked_grad.astype(jnp.bfloat16)
+        own_a[packed(b, BACK_SEG), :] = masked_grad
+        to_other(0, b, BACK_SEG, own_a).start()
+        grad_embeddings[rows, :] = masked_grad.astype(jnp.bfloat16)
         grads[small_base : small_base + REPL, :] = grads[
             small_base : small_base + REPL, :
         ] + lax.dot_general(
-            chosen(kept(b), OWN),
+            chosen(rows, BACK_SEG),
             grad * live,
             (((0,), (0,)), ((), ())),
             precision=lax.Precision.HIGHEST,
             preferred_element_type=jnp.float32,
         )
 
-    repeat(BLOCKS, last_grad)
+    repeat(BACK_BLOCKS, last_grad)
     shared = REPL + 8 * LAYERS
     for turn in range(LAYERS):
         first = small_base + REPL + 8 * turn
@@ -750,11 +974,10 @@
     )
     short.start()
 
-    def receive(b):
-        to_other(0, b, own_a).wait()
-        grad_embeddings[given(b), :] = land_back[0, b].astype(jnp.bfloat16)
-
-    repeat(BLOCKS, receive)
+    def receive_grad(b):
+        grad_embeddings[given(b, BACK_SEG), :] = received(0, b, BACK_SEG, own_a)
+
+    repeat(BACK_BLOCKS, receive_grad)
     short.wait()
     grads[small_base : small_base + shared, :] = (
         grads[small_base : small_base + shared, :] + land_small[...]
@@ -806,13 +1029,15 @@
             vmem((LAYERS, head_width, width), low),
             vmem((LAYERS, width, hidden_width), low),
             vmem((LAYERS, hidden_width, width), low),
+            vmem((LAYERS, 4 * head_width, width), low),
+            vmem((5, BLOCKS, 3 * SEG // 2, 2 * HEAD_DIM), full),
             vmem((rows, 128), full),
             vmem((half, width), full),
             vmem((half, width), full),
             vmem((rows, width), full),
-            vmem((2, BLOCKS, OWN, width), full),
-            vmem((2, BLOCKS, OWN, width), full),
-            vmem((2, BLOCKS, OWN, width), full),
+            vmem((2, half, width), full),
+            vmem((2, half, width), full),
+            vmem((2, half, width), full),
             vmem((REPL + 8 * LAYERS, width), full),
             vmem((rows, width), low),
             vmem((rows, hidden_width), low),
@@ -834,6 +1059,12 @@
             dma((KINDS, SLOTS)),
             dma((KINDS, SLOTS)),
             dma((4, LAYERS)),
+            dma((4 * LAYERS,)),
+            dma((4 * LAYERS,)),
+            dma((LAYERS, GROUP)),
+            dma((LAYERS, GROUP)),
+            dma((3, BLOCKS)),
+            dma((3, BLOCKS)),
         ],
         compiler_params=pltpu.CompilerParams(
             collective_id=0, has_side_effects=True, vmem_limit_bytes=46 << 20

time: 359 us -> 346 us (0.964)
  Pallas kernels: 358 us -> 345 us
    pallas_call x1, Pallas kernels: 352 us -> 339 us  [run_pages(): pl.pallas_call(functools.partial(page_kernel, sizes), name='pages', out_s...]
where the time goes in v5:
time: 346 us
  Pallas kernels  345 us (100%)
    pallas_call x1, Pallas kernels, run_pages(): pl.pallas_call(functools.partial(page_kernel, sizes), name='pages', out_s...  339 us

profile of v5, /device:TPU:0, one launch (start us, length us, event | category | flops | bytes accessed | tf_op | source)
XLA Modules:
  0.0 345.9 jit_solution(3600457555677218972)
XLA Ops:
  0.7 338.7 %pages.1 = (bf16[512,768]{1,0:T(8,128)(2,1)S(1)}, bf16[512,768]{1,0:T(8,128)(2,1)S(1)}, f32[4672,768]{1,0:T(8,128)S(1)}) custom-call(bf16[512,768]{1,0:T(8,128)(2,1)} %embeddings.1, bf16[32,768]{1,0:T(8,128)(2,1)} %replace_table.1, s32[1,512]{1,0:T(1,128)} %bitcast.6, s32[1,512]{1,0:T(1,128)} %bitcast.7, s32[1,512]{1,0:T(1,128)} %bitcast.8, ...), custom_call_target="tpu_custom_call" | custom-call | tf_op jit(solution)/shard_map/pages/pallas_call | solution.py:997
  339.3 6.6 %place_outputs.1 = (bf16[512,768]{1,0:T(8,128)(2,1)}, bf16[512,768]{1,0:T(8,128)(2,1)}, f32[32,768]{1,0:T(8,128)}, f32[2,576,768]{2,1,0:T(8,128)}, f32[2,384]{1,...) custom-call(bf16[512,768]{1,0:T(8,128)(2,1)S(1)} %get-tuple-element., ...), custom_call_target="tpu_custom_call" | custom-call | tf_op jit(solution)/shard_map/place_outputs/pallas_call | solution.py:1161

commit v6 on v5

--- a/solution.py
+++ b/solution.py
@@ -32,7 +32,7 @@
 LANDINGS = TTA + 1
 GROUP = 8
 WEIGHTS = (5, 7, 11, 13)
-DIRECT = (128, 0)
+DIRECT = (64, 0)
 
 
 def contract_rows(left, right):
@@ -689,9 +689,11 @@
 
         @pl.when(layer == 0)
         def _():
+            gather_first(1)
             gather_third(0)
-            gather_second(1)
             gather_last(0)
+
+        pl.when(layer == 1)(lambda: gather_last(1))
 
         gain, shift, bias_out = (
             vector(first_gain, layer),
@@ -737,11 +739,10 @@
             pl.when(b < BLOCKS)(lambda: feed_norm(b))
             pl.when(b >= 2)(lambda: send_y(1, b - 2, SEG))
             pl.when(b >= 1)(lambda: feed_main(b - 1))
+            pl.when(jnp.logical_and(layer == 0, b == 1))(lambda: gather_second(1))
 
         repeat(BLOCKS + 1, feed)
-        pl.when(layer == 0)(lambda: gather_third(1))
         send_y(1, BLOCKS - 1, SEG)
-        pl.when(layer == 0)(lambda: gather_last(1))
 
         gain_two, shift_two, bias_down = (
             vector(second_gain, layer),
@@ -778,15 +779,33 @@
 
         repeat(BLOCKS, finish)
         receive(BLOCKS - 1)
+        pl.when(layer == 0)(lambda: gather_third(1))
 
     meet(barrier)
     gather_first(0)
-    gather_first(1)
     repeat(BACK_BLOCKS, first_input)
     weight(0, 0).wait()
-    repeat(BACK_BLOCKS, lambda b: project(0, (block(b),)))
+    project(0, (block(0),))
     gather_second(0)
+    repeat(BACK_BLOCKS - 1, lambda b: project(0, (block(b + 1),)))
     repeat(LAYERS, forward)
+
+    def last_grad(b, grad):
+        rows = kept(b, BACK_SEG)
+        live = columns[rows, 0:1]
+        masked_grad = grad * (1.0 - live)
+        own_a[packed(b, BACK_SEG), :] = masked_grad
+        to_other(0, b, BACK_SEG, own_a).start()
+        grad_embeddings[rows, :] = masked_grad.astype(jnp.bfloat16)
+        grads[small_base : small_base + REPL, :] = grads[
+            small_base : small_base + REPL, :
+        ] + lax.dot_general(
+            chosen(rows, BACK_SEG),
+            grad * live,
+            (((0,), (0,)), ((), ())),
+            precision=lax.Precision.HIGHEST,
+            preferred_element_type=jnp.float32,
+        )
 
     def backward(turn):
         layer = LAYERS - 1 - turn
@@ -824,8 +843,7 @@
                 du, axis=0, keepdims=True
             )
             down_piece(b + 1)
-            tick(start + 2 + 2 * b)
-            tick(start + 3 + 2 * b)
+            tick(start + 2 + b)
 
         repeat(BACK_BLOCKS, feed)
         down_piece(5)
@@ -838,16 +856,16 @@
                 part[rows, :] = result[side * BACK_SEG : (side + 1) * BACK_SEG]
             to_core(0, b, BACK_SEG).start()
             pl.when(b >= 1)(lambda: send_y(0, b - 1, BACK_SEG))
-            in_piece(b)
-            tick(start + 10 + 2 * b)
-            tick(start + 11 + 2 * b)
+            tick(start + 6 + b)
 
         repeat(BACK_BLOCKS, feed_in)
         send_y(0, BACK_BLOCKS - 1, BACK_SEG)
-        in_piece(4)
-        tick(start + 18)
-        in_piece(5)
-        tick(start + 19)
+
+        def early_piece(p):
+            in_piece(p)
+            tick(start + 10 + p)
+
+        repeat(4, early_piece)
 
         gain = vector(first_gain, layer)
 
@@ -862,12 +880,15 @@
             total_row(turn, 3, grad * zhat)
             total_row(turn, 4, grad)
             total_row(turn, 5, dz)
-            tick(start + 20 + b)
+            tick(start + 14 + b)
             dz_low[given(b, BACK_SEG), :] = received(1, b, BACK_SEG, own_b)
 
         repeat(BACK_BLOCKS, norm_one)
         grads[rows_at(out_base, head_width), :] = contract_rows(heads[layer], dz_low[...])
         dheads[...] = contract_cols(dz_low[...], w_out[layer]).astype(jnp.bfloat16)
+        tick(start + 18)
+        in_piece(4)
+        in_piece(5)
         dkeys[...] = jnp.zeros_like(dkeys)
         dvalues[...] = jnp.zeros_like(dvalues)
 
@@ -888,7 +909,7 @@
                 local_sums[turn, 1:2, 2 * side : 2 * side + HEAD_DIM] = local_sums[
                     turn, 1:2, 2 * side : 2 * side + HEAD_DIM
                 ] + jnp.sum(dq, axis=0, keepdims=True)
-            pl.when(b < BACK_BLOCKS - 1)(lambda: tick(start + 24 + b))
+            tick(start + 19 + b)
 
         repeat(BACK_BLOCKS, attend)
         for h in range(local_heads):
@@ -912,6 +933,7 @@
                 part[rows, :] = result[side * BACK_SEG : (side + 1) * BACK_SEG]
             to_core(1, b, BACK_SEG).start()
             pl.when(b >= 1)(lambda: send_y(1, b - 1, BACK_SEG))
+            tick(start + 23 + b)
 
         repeat(BACK_BLOCKS, back_project)
         send_y(1, BACK_BLOCKS - 1, BACK_SEG)
@@ -920,20 +942,20 @@
             grads[rows_at(qkv_base + 128 * p, 128), :] = contract_rows(
                 dqkv_low[:, lanes(p)], inputs_low[layer]
             )
-            tick(start + 27 + 2 * p)
-            tick(start + 28 + 2 * p)
+            tick(start + 27 + p)
 
         repeat(4, qkv_piece)
         grads[rows_at(qkv_base + 512, 64), :] = contract_rows(
             dqkv_low[:, 512:], inputs_low[layer]
         )
-        tick(start + 35)
+        tick(start + 31)
 
         def pass_on(b):
             rows = packed(b, BACK_SEG)
             grad = own_b[rows, :] + summed(1, b, BACK_SEG)
-            own_b[rows, :] = grad
             pl.when(turn < LAYERS - 1)(lambda: norm_two(turn + 1, b, BACK_SEG, grad))
+            pl.when(turn == LAYERS - 1)(lambda: last_grad(b, grad))
+            tick(start + 32 + b)
 
         repeat(BACK_BLOCKS, pass_on)
 
@@ -945,25 +967,6 @@
     repeat(LAYERS, backward)
     hidden_out[...] = inputs_low[LAYERS]
 
-    def last_grad(b):
-        rows = kept(b, BACK_SEG)
-        live = columns[rows, 0:1]
-        grad = own_b[packed(b, BACK_SEG), :]
-        masked_grad = grad * (1.0 - live)
-        own_a[packed(b, BACK_SEG), :] = masked_grad
-        to_other(0, b, BACK_SEG, own_a).start()
-        grad_embeddings[rows, :] = masked_grad.astype(jnp.bfloat16)
-        grads[small_base : small_base + REPL, :] = grads[
-            small_base : small_base + REPL, :
-        ] + lax.dot_general(
-            chosen(rows, BACK_SEG),
-            grad * live,
-            (((0,), (0,)), ((), ())),
-            precision=lax.Precision.HIGHEST,
-            preferred_element_type=jnp.float32,
-        )
-
-    repeat(BACK_BLOCKS, last_grad)
     shared = REPL + 8 * LAYERS
     for turn in range(LAYERS):
         first = small_base + REPL + 8 * turn

time: 346 us -> 337 us (0.974)
  Pallas kernels: 345 us -> 336 us
    pallas_call x1, Pallas kernels: 339 us -> 329 us  [run_pages(): pl.pallas_call(functools.partial(page_kernel, sizes), name='pages', out_s...]
where the time goes in v6:
time: 337 us
  Pallas kernels  336 us (100%)
    pallas_call x1, Pallas kernels, run_pages(): pl.pallas_call(functools.partial(page_kernel, sizes), name='pages', out_s...  329 us

profile of v6, /device:TPU:0, one launch (start us, length us, event | category | flops | bytes accessed | tf_op | source)
XLA Modules:
  0.0 336.6 jit_solution(10794819029679859390)
XLA Ops:
  0.7 329.4 %pages.1 = (bf16[512,768]{1,0:T(8,128)(2,1)S(1)}, bf16[512,768]{1,0:T(8,128)(2,1)S(1)}, f32[4672,768]{1,0:T(8,128)S(1)}) custom-call(bf16[512,768]{1,0:T(8,128)(2,1)} %embeddings.1, bf16[32,768]{1,0:T(8,128)(2,1)} %replace_table.1, s32[1,512]{1,0:T(1,128)} %bitcast.6, s32[1,512]{1,0:T(1,128)} %bitcast.7, s32[1,512]{1,0:T(1,128)} %bitcast.8, ...), custom_call_target="tpu_custom_call" | custom-call | tf_op jit(solution)/shard_map/pages/pallas_call | solution.py:1000
  330.0 6.6 %place_outputs.1 = (bf16[512,768]{1,0:T(8,128)(2,1)}, bf16[512,768]{1,0:T(8,128)(2,1)}, f32[32,768]{1,0:T(8,128)}, f32[2,576,768]{2,1,0:T(8,128)}, f32[2,384]{1,...) custom-call(bf16[512,768]{1,0:T(8,128)(2,1)S(1)} %get-tuple-element., ...), custom_call_target="tpu_custom_call" | custom-call | tf_op jit(solution)/shard_map/place_outputs/pallas_call | solution.py:1164

commit v7 on v6

--- a/solution.py
+++ b/solution.py
@@ -23,13 +23,19 @@
 BACK_BLOCKS = HALF // BACK_SEG
 BLOCK = 2 * BACK_SEG
 
-UNIT = 16
-CHUNK = 4 * UNIT
+WIDE = 24
+NARROW = 8
+CHUNK = 2 * WIDE + 4 * NARROW
+HOLE = 2 * NARROW
+SHORT_CHUNKS = 3
 LAG = 2
 SLOTS = 4 * LAG
-KINDS = 12
-(TX, TNEAR, TFAR, TA1, TA2, TQ1, TQ2, TTA, TTN, TTM, TTF, TG) = range(KINDS)
-LANDINGS = TTA + 1
+KINDS = 18
+(TX, TA1, TA2, TTA, TQ0, TQ1, TQ2, TR0, TR1, TR2, TR3, TTN, TTM, TTF, TG, TR4, TR5, TR6) = range(
+    KINDS
+)
+WIDE_LANDINGS = (TX, TA1, TA2, TTA)
+NARROW_LANDINGS = (TQ1, TQ2, TR0, TR1, TR2, TR3)
 GROUP = 8
 WEIGHTS = (5, 7, 11, 13)
 DIRECT = (64, 0)
@@ -119,29 +125,33 @@
 
 
 class GradientSum:
-    def __init__(self, place, chunks, part, landing, send, recv):
+    def __init__(self, place, chunks, part, wide, both, narrow, send, recv):
         self.place = place
         self.chunks = chunks
         self.part = part
-        self.landing = landing
+        self.wide = wide
+        self.both = both
+        self.narrow = narrow
         self.send = send
         self.recv = recv
 
-    def rows(self, j, unit):
-        return pl.ds(pl.multiple_of(j * CHUNK + unit * UNIT, UNIT), UNIT)
+    def wide_rows(self, j, unit):
+        return pl.ds(pl.multiple_of(j * CHUNK + unit * WIDE, NARROW), WIDE)
+
+    def narrow_rows(self, j, unit, count=1):
+        first = j * CHUNK + 2 * WIDE + unit * NARROW
+        return pl.ds(pl.multiple_of(first, NARROW), count * NARROW)
 
     def tick(self, t):
         place, part = self.place, self.part
         mine, other = place.pair, 1 - place.pair
-        near, far = 2 + place.upper, 3 - place.upper
-
-        def at(j, unit):
-            return part.at[self.rows(j, unit)]
-
-        def copy(kind, j, source, target, device):
+        near, far = place.upper, 1 - place.upper
+        near_end, far_end = 2 + place.upper, 3 - place.upper
+
+        def copy(kind, j, rows, target, device):
             slot = lax.rem(j, SLOTS)
             return pltpu.make_async_remote_copy(
-                src_ref=source,
+                src_ref=part.at[rows],
                 dst_ref=target,
                 send_sem=self.send.at[kind, slot],
                 recv_sem=self.recv.at[kind, slot],
@@ -149,77 +159,122 @@
                 device_id_type=MESH,
             )
 
-        def partial(kind, j, unit, device):
-            return copy(kind, j, at(j, unit), self.landing.at[kind, lax.rem(j, SLOTS)], device)
-
-        def final(kind, j, unit, device):
-            return copy(kind, j, at(j, unit), at(j, unit), device)
-
-        def add(kind, j, unit):
-            rows = self.rows(j, unit)
-            part[rows, :] = part[rows, :] + self.landing[kind, lax.rem(j, SLOTS)]
+        def wide_slot(kind, j):
+            return WIDE_LANDINGS.index(kind), lax.rem(j, SLOTS)
+
+        def narrow_slot(kind, j):
+            return NARROW_LANDINGS.index(kind), lax.rem(j, SLOTS)
+
+        def wide_part(kind, j, unit, device):
+            return copy(
+                kind, j, self.wide_rows(j, unit), self.wide.at[wide_slot(kind, j)], device
+            )
+
+        def narrow_part(kind, j, unit, device):
+            return copy(
+                kind, j, self.narrow_rows(j, unit), self.narrow.at[narrow_slot(kind, j)], device
+            )
+
+        def final(kind, j, rows, device):
+            return copy(kind, j, rows, part.at[rows], device)
+
+        def add_wide(kind, j, unit):
+            rows = self.wide_rows(j, unit)
+            part[rows, :] = part[rows, :] + self.wide[wide_slot(kind, j)]
+
+        def add_narrow(kind, j, unit):
+            rows = self.narrow_rows(j, unit)
+            part[rows, :] = part[rows, :] + self.narrow[narrow_slot(kind, j)]
 
         def pair_first(j):
-            return partial(TX, j, other, place.peer)
-
-        def near_in(j):
-            return partial(TNEAR, j, near, place.line)
-
-        def far_in(j):
-            return partial(TFAR, j, far, place.line)
+            return wide_part(TX, j, other, place.peer)
 
         def mine_in(j):
-            return partial(TA1, j, mine, place.line)
+            return wide_part(TA1, j, mine, place.line)
 
         def mine_across(j):
-            return partial(TA2, j, mine, place.cross)
+            return wide_part(TA2, j, mine, place.cross)
+
+        def mine_out(j):
+            return wide_part(TTA, j, mine, place.line)
+
+        def pair_last(j):
+            return final(TG, j, self.wide_rows(j, mine), place.peer)
+
+        def both_in(j):
+            rows = self.narrow_rows(j, 0, 2)
+            return copy(TQ0, j, rows, self.both.at[lax.rem(j, SLOTS)], place.line)
 
         def far_across(j):
-            return partial(TQ1, j, far, place.cross)
+            return narrow_part(TQ1, j, far, place.cross)
 
         def near_pair(j):
-            return partial(TQ2, j, near, place.peer)
-
-        def mine_out(j):
-            return partial(TTA, j, mine, place.line)
+            return narrow_part(TQ2, j, near, place.peer)
 
         def near_out(j):
-            return final(TTN, j, near, place.line)
+            return final(TTN, j, self.narrow_rows(j, near), place.line)
 
         def near_across(j):
-            return final(TTM, j, near, place.cross)
+            return final(TTM, j, self.narrow_rows(j, near), place.cross)
 
         def far_out(j):
-            return final(TTF, j, far, place.line)
-
-        def pair_last(j):
-            return final(TG, j, mine, place.peer)
+            return final(TTF, j, self.narrow_rows(j, far), place.line)
+
+        def end_in(j):
+            return narrow_part(TR0, j, far_end, place.line)
+
+        def end_across(j):
+            return narrow_part(TR1, j, far_end, place.cross)
+
+        def end_up(j):
+            return narrow_part(TR2, j, near_end, place.line)
+
+        def end_pair(j):
+            return narrow_part(TR3, j, near_end, place.peer)
+
+        def end_down(j):
+            return final(TR4, j, self.narrow_rows(j, near_end), place.line)
+
+        def end_back(j):
+            return final(TR5, j, self.narrow_rows(j, near_end), place.cross)
+
+        def end_out(j):
+            return final(TR6, j, self.narrow_rows(j, far_end), place.line)
+
+        def ended(j, body):
+            pl.when(j < self.chunks - SHORT_CHUNKS)(body)
 
         def stage_0(j):
             pair_first(j).start()
 
             @pl.when(place.end)
             def _():
-                near_in(j).start()
-                far_in(j).start()
+                ended(j, lambda: end_in(j).start())
+                both_in(j).start()
 
         def stage_1(j):
             pair_first(j).wait()
-            add(TX, j, mine)
 
             @pl.when(place.end)
             def _():
-                near_in(j).wait_send()
-                far_in(j).wait_send()
+                both_in(j).wait_send()
+                ended(j, lambda: end_in(j).wait_send())
+                add_wide(TX, j, mine)
                 mine_in(j).start()
 
             @pl.when(place.mid)
             def _():
-                far_in(j).wait_recv()
-                add(TFAR, j, far)
+                def onward():
+                    end_in(j).wait_recv()
+                    add_narrow(TR0, j, far_end)
+                    end_across(j).start()
+
+                ended(j, onward)
+                both_in(j).wait_recv()
+                rows = self.narrow_rows(j, 0, 2)
+                part[rows, :] = part[rows, :] + self.both[lax.rem(j, SLOTS)]
                 far_across(j).start()
-                near_in(j).wait_recv()
-                add(TNEAR, j, near)
+                add_wide(TX, j, mine)
 
         def stage_2(j):
             @pl.when(place.end)
@@ -230,44 +285,93 @@
             def _():
                 mine_in(j).wait_recv()
                 far_across(j).wait()
-                add(TA1, j, mine)
+
+                def onward():
+                    end_across(j).wait()
+                    add_narrow(TR1, j, near_end)
+                    end_up(j).start()
+
+                ended(j, onward)
+                add_narrow(TQ1, j, near)
+                near_pair(j).start()
+                add_wide(TA1, j, mine)
                 mine_across(j).start()
-                add(TQ1, j, near)
-                near_pair(j).start()
 
         def stage_3(j):
+            @pl.when(place.end)
+            def _():
+                def onward():
+                    end_up(j).wait_recv()
+                    add_narrow(TR2, j, near_end)
+                    end_pair(j).start()
+
+                ended(j, onward)
+
             @pl.when(place.mid)
             def _():
+                ended(j, lambda: end_up(j).wait_send())
                 mine_across(j).wait()
-                add(TA2, j, mine)
-                mine_out(j).start()
                 near_pair(j).wait()
-                add(TQ2, j, near)
+                add_narrow(TQ2, j, near)
                 near_across(j).start()
                 near_out(j).start()
+                add_wide(TA2, j, mine)
+                mine_out(j).start()
 
         def stage_4(j):
             @pl.when(place.mid)
             def _():
-                mine_out(j).wait_send()
-                near_out(j).wait_send()
-                pair_last(j).start()
                 near_across(j).wait()
                 far_out(j).start()
+                near_out(j).wait_send()
+                mine_out(j).wait_send()
+                pair_last(j).start()
 
             @pl.when(place.end)
             def _():
                 mine_out(j).wait_recv()
                 near_out(j).wait_recv()
-                part[self.rows(j, mine), :] = self.landing[TTA, lax.rem(j, SLOTS)]
+
+                def onward():
+                    end_pair(j).wait()
+                    add_narrow(TR3, j, near_end)
+                    end_down(j).start()
+
+                ended(j, onward)
+                part[self.wide_rows(j, mine), :] = self.wide[wide_slot(TTA, j)]
                 pair_last(j).start()
 
         def stage_5(j):
+            @pl.when(place.mid)
+            def _():
+                def onward():
+                    end_down(j).wait_recv()
+                    end_back(j).start()
+
+                ended(j, onward)
+                far_out(j).wait_send()
+
+            @pl.when(place.end)
+            def _():
+                ended(j, lambda: end_down(j).wait_send())
+                far_out(j).wait_recv()
+
             pair_last(j).wait()
-            pl.when(place.mid)(lambda: far_out(j).wait_send())
-            pl.when(place.end)(lambda: far_out(j).wait_recv())
-
-        stages = (stage_0, stage_1, stage_2, stage_3, stage_4, stage_5)
+
+        def stage_6(j):
+            @pl.when(place.mid)
+            def _():
+                def onward():
+                    end_back(j).wait()
+                    end_out(j).start()
+
+                ended(j, onward)
+
+        def stage_7(j):
+            pl.when(place.mid)(lambda: ended(j, lambda: end_out(j).wait_send()))
+            pl.when(place.end)(lambda: ended(j, lambda: end_out(j).wait_recv()))
+
+        stages = (stage_0, stage_1, stage_2, stage_3, stage_4, stage_5, stage_6, stage_7)
         for number in reversed(range(len(stages))):
             j = t - number * LAG
             pl.when(jnp.logical_and(j >= 0, j < self.chunks))(
@@ -275,7 +379,7 @@
             )
 
     def ticks(self):
-        return self.chunks + 5 * LAG
+        return self.chunks + max(5 * LAG, 7 * LAG - SHORT_CHUNKS)
 
 
 def page_kernel(
@@ -336,7 +440,9 @@
     dqkv_low,
     sums,
     local_sums,
-    landing,
+    land_wide,
+    land_both,
+    land_narrow,
     core_send,
     core_recv,
     y_send,
@@ -371,9 +477,11 @@
 
     for index, layer in ((0, 0), (1, 0), (1, 1), (2, 0), (3, 0), (0, 1), (2, 1), (3, 1)):
         weight(index, layer).start()
-    small_base = LAYERS * span
+    tail_base = LAYERS * span - HEAD_DIM + HOLE
+    small_base = tail_base + CHUNK
+    assert tail_base % CHUNK == 0 and span % HEAD_DIM == 0
     chunks = grads.shape[0] // CHUNK
-    grad_sum = GradientSum(place, chunks, grads, landing, dp_send, dp_recv)
+    grad_sum = GradientSum(place, chunks, grads, land_wide, land_both, land_narrow, dp_send, dp_recv)
     tick = grad_sum.tick
 
     def vector(ref, layer):
@@ -811,12 +919,13 @@
         layer = LAYERS - 1 - turn
         base = turn * span
         start = turn * (span // CHUNK)
+        last = turn == LAYERS - 1
         in_base = base + hidden_width
         out_base = in_base + width
         qkv_base = out_base + head_width
 
         def rows_at(first, count):
-            return pl.ds(pl.multiple_of(first, 64), count)
+            return pl.ds(pl.multiple_of(first, 16), count)
 
         def down_piece(p):
             grads[rows_at(base + 128 * p, 128), :] = contract_rows(
@@ -830,7 +939,6 @@
 
         down_piece(0)
         tick(start)
-        tick(start + 1)
 
         def feed(b):
             rows = block(b)
@@ -843,7 +951,7 @@
                 du, axis=0, keepdims=True
             )
             down_piece(b + 1)
-            tick(start + 2 + b)
+            tick(start + 1 + b)
 
         repeat(BACK_BLOCKS, feed)
         down_piece(5)
@@ -856,16 +964,17 @@
                 part[rows, :] = result[side * BACK_SEG : (side + 1) * BACK_SEG]
             to_core(0, b, BACK_SEG).start()
             pl.when(b >= 1)(lambda: send_y(0, b - 1, BACK_SEG))
-            tick(start + 6 + b)
+            tick(start + 5 + b)
 
         repeat(BACK_BLOCKS, feed_in)
         send_y(0, BACK_BLOCKS - 1, BACK_SEG)
 
         def early_piece(p):
             in_piece(p)
-            tick(start + 10 + p)
+            tick(start + 9 + p)
 
         repeat(4, early_piece)
+        in_piece(4)
 
         gain = vector(first_gain, layer)
 
@@ -880,15 +989,14 @@
             total_row(turn, 3, grad * zhat)
             total_row(turn, 4, grad)
             total_row(turn, 5, dz)
-            tick(start + 14 + b)
+            tick(start + 13 + b)
             dz_low[given(b, BACK_SEG), :] = received(1, b, BACK_SEG, own_b)
 
         repeat(BACK_BLOCKS, norm_one)
         grads[rows_at(out_base, head_width), :] = contract_rows(heads[layer], dz_low[...])
         dheads[...] = contract_cols(dz_low[...], w_out[layer]).astype(jnp.bfloat16)
-        tick(start + 18)
-        in_piece(4)
         in_piece(5)
+        tick(start + 17)
         dkeys[...] = jnp.zeros_like(dkeys)
         dvalues[...] = jnp.zeros_like(dvalues)
 
@@ -909,7 +1017,7 @@
                 local_sums[turn, 1:2, 2 * side : 2 * side + HEAD_DIM] = local_sums[
                     turn, 1:2, 2 * side : 2 * side + HEAD_DIM
                 ] + jnp.sum(dq, axis=0, keepdims=True)
-            tick(start + 19 + b)
+            pl.when(b < BACK_BLOCKS - 1)(lambda: tick(start + 18 + b))
 
         repeat(BACK_BLOCKS, attend)
         for h in range(local_heads):
@@ -926,6 +1034,9 @@
             )
 
         def back_project(b):
+            grads[rows_at(qkv_base + 128 * b, 128), :] = contract_rows(
+                dqkv_low[:, lanes(b)], inputs_low[layer]
+            )
             spans = halves(b, BACK_SEG)
             left = jnp.concatenate([dqkv_low[rows, :] for rows in spans], axis=0)
             result = matmul(left, w_qkv[layer])
@@ -933,36 +1044,30 @@
                 part[rows, :] = result[side * BACK_SEG : (side + 1) * BACK_SEG]
             to_core(1, b, BACK_SEG).start()
             pl.when(b >= 1)(lambda: send_y(1, b - 1, BACK_SEG))
-            tick(start + 23 + b)
+            tick(start + 21 + b)
 
         repeat(BACK_BLOCKS, back_project)
         send_y(1, BACK_BLOCKS - 1, BACK_SEG)
 
-        def qkv_piece(p):
-            grads[rows_at(qkv_base + 128 * p, 128), :] = contract_rows(
-                dqkv_low[:, lanes(p)], inputs_low[layer]
-            )
-            tick(start + 27 + p)
-
-        repeat(4, qkv_piece)
-        grads[rows_at(qkv_base + 512, 64), :] = contract_rows(
+        tail = jnp.where(last, HOLE, 0)
+        grads[rows_at(qkv_base + 512 + tail, HEAD_DIM), :] = contract_rows(
             dqkv_low[:, 512:], inputs_low[layer]
         )
-        tick(start + 31)
+        tick(start + 25)
 
         def pass_on(b):
             rows = packed(b, BACK_SEG)
             grad = own_b[rows, :] + summed(1, b, BACK_SEG)
-            pl.when(turn < LAYERS - 1)(lambda: norm_two(turn + 1, b, BACK_SEG, grad))
-            pl.when(turn == LAYERS - 1)(lambda: last_grad(b, grad))
-            tick(start + 32 + b)
+            pl.when(jnp.logical_not(last))(lambda: norm_two(turn + 1, b, BACK_SEG, grad))
+            pl.when(last)(lambda: last_grad(b, grad))
+            pl.when(jnp.logical_or(last, b < 2))(lambda: tick(start + 26 + b))
 
         repeat(BACK_BLOCKS, pass_on)
 
         def receive(b):
             dz_low[given(b, BACK_SEG), :] = received(0, b, BACK_SEG, own_a)
 
-        pl.when(turn < LAYERS - 1)(lambda: repeat(BACK_BLOCKS, receive))
+        pl.when(jnp.logical_not(last))(lambda: repeat(BACK_BLOCKS, receive))
 
     repeat(LAYERS, backward)
     hidden_out[...] = inputs_low[LAYERS]
@@ -985,14 +1090,14 @@
     grads[small_base : small_base + shared, :] = (
         grads[small_base : small_base + shared, :] + land_small[...]
     )
-    done = LAYERS * (span // CHUNK)
+    done = chunks - 1
     repeat(grad_sum.ticks() - done, lambda i: tick(done + i))
 
 
 def run_pages(args, sizes):
     width, hidden_width, local_heads, span = sizes
     rows = PAGE_LEN
-    flat = LAYERS * span + CHUNK
+    flat = LAYERS * span - HEAD_DIM + HOLE + 2 * CHUNK
     half = rows // 2
     low, full = jnp.bfloat16, jnp.float32
     vmem, dma = pltpu.VMEM, pltpu.SemaphoreType.DMA
@@ -1050,7 +1155,9 @@
             vmem((rows, 3 * head_width), low),
             vmem((LAYERS, 8, width), full),
             vmem((LAYERS, 4, width), full),
-            vmem((LANDINGS, SLOTS, UNIT, width), full),
+            vmem((len(WIDE_LANDINGS), SLOTS, WIDE, width), full),
+            vmem((SLOTS, 2 * NARROW, width), full),
+            vmem((len(NARROW_LANDINGS), SLOTS, NARROW, width), full),
             dma((2, BLOCKS)),
             dma((2, BLOCKS)),
             dma((2, BLOCKS)),
@@ -1097,7 +1204,8 @@
         short,
         sems,
     ) = refs
-    base = LAYERS * span
+    tail = LAYERS * span - HEAD_DIM
+    base = tail + HOLE + CHUNK
     pairs = [(every.at[pl.ds(base, CHUNK)], short), (every.at[pl.ds(base, REPL)], out_table)]
     pairs += [(hidden_out, out_hidden), (grad_embeddings, out_embeddings)]
     for turn in range(LAYERS):
@@ -1108,7 +1216,16 @@
             (out_w_out, head_width),
             (out_w_qkv, 3 * head_width),
         ):
-            pairs.append((every.at[pl.ds(first, rows)], ref.at[LAYERS - 1 - turn]))
+            target = ref.at[LAYERS - 1 - turn]
+            direct = min(rows, tail - first)
+            pairs.append((every.at[pl.ds(first, direct)], target.at[pl.ds(0, direct)]))
+            if direct < rows:
+                pairs.append(
+                    (
+                        every.at[pl.ds(tail + HOLE, rows - direct)],
+                        target.at[pl.ds(direct, rows - direct)],
+                    )
+                )
             first += rows
     copies = [
         pltpu.make_async_copy(source, target, sems.at[index])
@@ -1169,7 +1286,7 @@
         out_specs=[close if shape[0] == LAYERS and len(shape) == 2 else far for shape, _ in shapes],
         scratch_shapes=[
             pltpu.VMEM((CHUNK, width), full),
-            pltpu.SemaphoreType.DMA((4 + 4 * LAYERS,)),
+            pltpu.SemaphoreType.DMA((5 + 4 * LAYERS,)),
         ],
         compiler_params=pltpu.CompilerParams(vmem_limit_bytes=4 << 20),
     )(hidden_out, grad_embeddings, every)

time: 337 us -> 321 us (0.953)
  Pallas kernels: 336 us -> 321 us
    pallas_call x1, Pallas kernels: 329 us -> 314 us  [run_pages(): pl.pallas_call(functools.partial(page_kernel, sizes), name='pages', out_s...]
where the time goes in v7:
time: 321 us
  Pallas kernels  321 us (100%)
    pallas_call x1, Pallas kernels, run_pages(): pl.pallas_call(functools.partial(page_kernel, sizes), name='pages', out_s...  314 us
    pallas_call x1, Pallas kernels, place_outputs(): pl.pallas_call(functools.partial(place_kernel, sizes), name='place_output...  6.62 us

profile of v7, /device:TPU:0, one launch (start us, length us, event | category | flops | bytes accessed | tf_op | source)
XLA Modules:
  0.0 321.3 jit_solution(13625088112016730956)
XLA Ops:
  0.7 314.1 %pages.1 = (bf16[512,768]{1,0:T(8,128)(2,1)S(1)}, bf16[512,768]{1,0:T(8,128)(2,1)S(1)}, f32[4720,768]{1,0:T(8,128)S(1)}) custom-call(bf16[512,768]{1,0:T(8,128)(2,1)} %embeddings.1, bf16[32,768]{1,0:T(8,128)(2,1)} %replace_table.1, s32[1,512]{1,0:T(1,128)} %bitcast.6, s32[1,512]{1,0:T(1,128)} %bitcast.7, s32[1,512]{1,0:T(1,128)} %bitcast.8, ...), custom_call_target="tpu_custom_call" | custom-call | tf_op jit(solution)/shard_map/pages/pallas_call | solution.py:1105
  314.7 6.6 %place_outputs.1 = (bf16[512,768]{1,0:T(8,128)(2,1)}, bf16[512,768]{1,0:T(8,128)(2,1)}, f32[32,768]{1,0:T(8,128)}, f32[2,576,768]{2,1,0:T(8,128)}, f32[2,384]{1,...) custom-call(bf16[512,768]{1,0:T(8,128)(2,1)S(1)} %get-tuple-element., ...), custom_call_target="tpu_custom_call" | custom-call | tf_op jit(solution)/shard_map/place_outputs/pallas_call | solution.py:1281

commit v8 on v7

--- a/solution.py
+++ b/solution.py
@@ -30,14 +30,15 @@
 SHORT_CHUNKS = 3
 LAG = 2
 SLOTS = 4 * LAG
-KINDS = 18
-(TX, TA1, TA2, TTA, TQ0, TQ1, TQ2, TR0, TR1, TR2, TR3, TTN, TTM, TTF, TG, TR4, TR5, TR6) = range(
-    KINDS
-)
+EQUAL_SLOTS = 2 * LAG
+EQUALS = (TX, TA2, TQ1, TQ2, TR1, TR3, TTM, TG, TR5) = range(9)
+ONE_WAY = (TA1, TTA, TQ0, TR0, TR2, TTN, TTF, TR4, TR6) = range(9, 18)
 WIDE_LANDINGS = (TX, TA1, TA2, TTA)
 NARROW_LANDINGS = (TQ1, TQ2, TR0, TR1, TR2, TR3)
 GROUP = 8
+ARGS = 18
 WEIGHTS = (5, 7, 11, 13)
+SHORT_ARGS = tuple(index for index in range(1, ARGS - 1) if index not in WEIGHTS)
 DIRECT = (64, 0)
 
 
@@ -125,7 +126,7 @@
 
 
 class GradientSum:
-    def __init__(self, place, chunks, part, wide, both, narrow, send, recv):
+    def __init__(self, place, chunks, part, wide, both, narrow, send, recv, one_way):
         self.place = place
         self.chunks = chunks
         self.part = part
@@ -134,6 +135,7 @@
         self.narrow = narrow
         self.send = send
         self.recv = recv
+        self.one_way = one_way
 
     def wide_rows(self, j, unit):
         return pl.ds(pl.multiple_of(j * CHUNK + unit * WIDE, NARROW), WIDE)
@@ -149,12 +151,16 @@
         near_end, far_end = 2 + place.upper, 3 - place.upper
 
         def copy(kind, j, rows, target, device):
-            slot = lax.rem(j, SLOTS)
+            if kind in EQUALS:
+                slot = lax.rem(j, EQUAL_SLOTS)
+                send, recv = self.send.at[kind, slot], self.recv.at[kind, slot]
+            else:
+                send = recv = self.one_way.at[kind - len(EQUALS), lax.rem(j, SLOTS)]
             return pltpu.make_async_remote_copy(
                 src_ref=part.at[rows],
                 dst_ref=target,
-                send_sem=self.send.at[kind, slot],
-                recv_sem=self.recv.at[kind, slot],
+                send_sem=send,
+                recv_sem=recv,
                 device_id=device,
                 device_id_type=MESH,
             )
@@ -382,106 +388,110 @@
         return self.chunks + max(5 * LAG, 7 * LAG - SHORT_CHUNKS)
 
 
-def page_kernel(
-    sizes,
-    embeddings,
-    replace_table,
-    replace_ids,
-    masked,
-    padding,
-    w_qkv_far,
-    b_qv,
-    w_out_far,
-    b_out,
-    first_gain,
-    first_shift,
-    w_in_far,
-    b_in,
-    w_down_far,
-    b_down,
-    second_gain,
-    second_shift,
-    cotangent,
-    hidden_out,
-    grad_embeddings,
-    grads,
-    inputs_low,
-    queries,
-    keys,
-    values,
-    log_total,
-    heads,
-    normed_low,
-    hidden,
-    active,
-    zhat_one,
-    scale_one,
-    zhat_two,
-    scale_two,
-    w_qkv,
-    w_out,
-    w_in,
-    w_down,
-    w_all,
-    shared_heads,
-    columns,
-    own_a,
-    own_b,
-    part,
-    land_core,
-    land_y,
-    land_back,
-    land_small,
-    dz_low,
-    du_low,
-    dheads,
-    dkeys,
-    dvalues,
-    dqkv_low,
-    sums,
-    local_sums,
-    land_wide,
-    land_both,
-    land_narrow,
-    core_send,
-    core_recv,
-    y_send,
-    y_recv,
-    back_send,
-    back_recv,
-    small_send,
-    small_recv,
-    dp_send,
-    dp_recv,
-    weight_sem,
-    gather_send,
-    gather_recv,
-    hand_send,
-    hand_recv,
-    heads_send,
-    heads_recv,
-):
+def page_kernel(sizes, *refs):
+    far, refs = refs[:ARGS], refs[ARGS:]
+    (hidden_out, grad_embeddings, grads), refs = refs[:3], refs[3:]
+    close, refs = refs[:ARGS], refs[ARGS:]
+    (
+        embeddings,
+        replace_table,
+        replace_ids,
+        masked,
+        padding,
+        w_qkv,
+        b_qv,
+        w_out,
+        b_out,
+        first_gain,
+        first_shift,
+        w_in,
+        b_in,
+        w_down,
+        b_down,
+        second_gain,
+        second_shift,
+        cotangent,
+    ) = close
+    (
+        inputs_low,
+        queries,
+        keys,
+        values,
+        log_total,
+        heads,
+        normed_low,
+        hidden,
+        active,
+        zhat_one,
+        scale_one,
+        zhat_two,
+        scale_two,
+        w_all,
+        shared_heads,
+        columns,
+        own_a,
+        own_b,
+        part,
+        land_core,
+        land_y,
+        land_back,
+        land_small,
+        dz_low,
+        du_low,
+        dheads,
+        dkeys,
+        dvalues,
+        dqkv_low,
+        sums,
+        local_sums,
+        land_wide,
+        land_both,
+        land_narrow,
+        core_send,
+        core_recv,
+        y_send,
+        y_recv,
+        back_send,
+        back_recv,
+        small_send,
+        small_recv,
+        dp_send,
+        dp_recv,
+        dp_one_way,
+        gather_send,
+        gather_recv,
+        hand_send,
+        hand_recv,
+        heads_send,
+        heads_recv,
+        close_sem,
+    ) = refs
     width, hidden_width, local_heads, span = sizes
     head_width = local_heads * HEAD_DIM
     place = Place()
     core = place.core
     barrier = pltpu.get_barrier_semaphore()
     greet(place, barrier)
-    weights = ((w_qkv_far, w_qkv), (w_out_far, w_out), (w_in_far, w_in), (w_down_far, w_down))
-
-    def weight(index, layer):
-        source, target = weights[index]
+
+    def fetch(index):
+        return pltpu.make_async_copy(far[index], close[index], close_sem.at[index, 0])
+
+    def weight(which, layer):
+        index = WEIGHTS[which]
         return pltpu.make_async_copy(
-            source.at[layer], target.at[layer], weight_sem.at[index, layer]
-        )
-
-    for index, layer in ((0, 0), (1, 0), (1, 1), (2, 0), (3, 0), (0, 1), (2, 1), (3, 1)):
-        weight(index, layer).start()
+            far[index].at[layer], close[index].at[layer], close_sem.at[index, layer]
+        )
+
+    weight(1, 0).start()
+    fetch(0).start()
+    weight(0, 0).start()
+    for index in SHORT_ARGS:
+        fetch(index).start()
     tail_base = LAYERS * span - HEAD_DIM + HOLE
     small_base = tail_base + CHUNK
     assert tail_base % CHUNK == 0 and span % HEAD_DIM == 0
     chunks = grads.shape[0] // CHUNK
-    grad_sum = GradientSum(place, chunks, grads, land_wide, land_both, land_narrow, dp_send, dp_recv)
+    grad_sum = GradientSum(place, chunks, grads, land_wide, land_both, land_narrow, dp_send, dp_recv, dp_one_way)
     tick = grad_sum.tick
 
     def vector(ref, layer):
@@ -696,6 +706,11 @@
             thirds.append(jnp.concatenate([tail[:, :HEAD_DIM], tail[:, HEAD_DIM:]], axis=0))
         return jnp.concatenate(pairs + thirds, axis=1)
 
+    meet(barrier)
+    gather_first(0)
+
+    for index in SHORT_ARGS:
+        fetch(index).wait()
     pad_row = padding[...].astype(jnp.float32)
     live_row = masked[...].astype(jnp.float32) * pad_row
     bias_row = (pad_row - 1.0) * 10000.0
@@ -770,6 +785,7 @@
         last = layer == LAYERS - 1
 
         def attend(b):
+            pl.when(jnp.logical_and(layer == 0, b == BLOCKS - 1))(lambda: gather_third(0))
             spans = halves(b, SEG)
             outs, logs = [], []
             for h in range(local_heads):
@@ -798,7 +814,6 @@
         @pl.when(layer == 0)
         def _():
             gather_first(1)
-            gather_third(0)
             gather_last(0)
 
         pl.when(layer == 1)(lambda: gather_last(1))
@@ -844,12 +859,12 @@
             to_core(1, b, SEG).start()
 
         def feed(b):
-            pl.when(b < BLOCKS)(lambda: feed_norm(b))
-            pl.when(b >= 2)(lambda: send_y(1, b - 2, SEG))
-            pl.when(b >= 1)(lambda: feed_main(b - 1))
-            pl.when(jnp.logical_and(layer == 0, b == 1))(lambda: gather_second(1))
-
-        repeat(BLOCKS + 1, feed)
+            feed_norm(b)
+            pl.when(b >= 1)(lambda: send_y(1, b - 1, SEG))
+            feed_main(b)
+            pl.when(jnp.logical_and(layer == 0, b == 0))(lambda: gather_second(1))
+
+        repeat(BLOCKS, feed)
         send_y(1, BLOCKS - 1, SEG)
 
         gain_two, shift_two, bias_down = (
@@ -889,13 +904,16 @@
         receive(BLOCKS - 1)
         pl.when(layer == 0)(lambda: gather_third(1))
 
-    meet(barrier)
-    gather_first(0)
+    fetch(0).wait()
     repeat(BACK_BLOCKS, first_input)
+    fetch(ARGS - 1).start()
+    for index, layer in ((1, 1), (2, 0), (3, 0), (0, 1), (2, 1), (3, 1)):
+        weight(index, layer).start()
     weight(0, 0).wait()
     project(0, (block(0),))
     gather_second(0)
     repeat(BACK_BLOCKS - 1, lambda b: project(0, (block(b + 1),)))
+    fetch(ARGS - 1).wait()
     repeat(LAYERS, forward)
 
     def last_grad(b, grad):
@@ -1110,16 +1128,14 @@
             vmem((rows, width), low),
             vmem((flat, width), full),
         ),
-        in_specs=[
-            pl.BlockSpec(memory_space=pl.ANY if index in WEIGHTS else pltpu.VMEM)
-            for index in range(len(args))
-        ],
+        in_specs=[pl.BlockSpec(memory_space=pl.ANY)] * ARGS,
         out_specs=(
             pl.BlockSpec(memory_space=pltpu.VMEM),
             pl.BlockSpec(memory_space=pltpu.VMEM),
             pl.BlockSpec(memory_space=pltpu.VMEM),
         ),
         scratch_shapes=[
+            *[vmem(arg.shape, arg.dtype) for arg in args],
             vmem((LAYERS + 1, rows, width), low),
             vmem((LAYERS, local_heads, rows, HEAD_DIM), low),
             vmem((LAYERS, local_heads, rows, HEAD_DIM), low),
@@ -1133,10 +1149,6 @@
             vmem((LAYERS, half, 1), full),
             vmem((LAYERS, half, width), full),
             vmem((LAYERS, half, 1), full),
-            vmem((LAYERS, 3 * head_width, width), low),
-            vmem((LAYERS, head_width, width), low),
-            vmem((LAYERS, width, hidden_width), low),
-            vmem((LAYERS, hidden_width, width), low),
             vmem((LAYERS, 4 * head_width, width), low),
             vmem((5, BLOCKS, 3 * SEG // 2, 2 * HEAD_DIM), full),
             vmem((rows, 128), full),
@@ -1166,15 +1178,16 @@
             dma((2, BLOCKS)),
             dma,
             dma,
-            dma((KINDS, SLOTS)),
-            dma((KINDS, SLOTS)),
-            dma((4, LAYERS)),
+            dma((len(EQUALS), EQUAL_SLOTS)),
+            dma((len(EQUALS), EQUAL_SLOTS)),
+            dma((len(ONE_WAY), SLOTS)),
             dma((4 * LAYERS,)),
             dma((4 * LAYERS,)),
             dma((LAYERS, GROUP)),
             dma((LAYERS, GROUP)),
             dma((3, BLOCKS)),
             dma((3, BLOCKS)),
+            dma((ARGS, LAYERS)),
         ],
         compiler_params=pltpu.CompilerParams(
             collective_id=0, has_side_effects=True, vmem_limit_bytes=46 << 20
@@ -1202,6 +1215,7 @@
         out_second_gain,
         out_second_shift,
         short,
+        shorts,
         sems,
     ) = refs
     tail = LAYERS * span - HEAD_DIM
@@ -1234,8 +1248,9 @@
     for copy in copies:
         copy.start()
     copies[0].wait()
+    pieces = []
     local = REPL + 8 * LAYERS
-    for ref, row, step in (
+    for index, (ref, row, step) in enumerate((
         (out_second_gain, REPL, 8),
         (out_second_shift, REPL + 1, 8),
         (out_b_down, REPL + 2, 8),
@@ -1244,13 +1259,18 @@
         (out_b_out, REPL + 5, 8),
         (out_b_in, local, 4),
         (out_b_qv, local + 1, 4),
-    ):
+    )):
         for turn in range(LAYERS):
             layer = LAYERS - 1 - turn
-            ref[layer : layer + 1, :] = short[
-                row + step * turn : row + step * turn + 1, : ref.shape[1]
+            shorts[index, layer : layer + 1, :] = short[
+                row + step * turn : row + step * turn + 1, :
             ]
-    for copy in copies[1:]:
+        piece = pltpu.make_async_copy(
+            shorts.at[index, :, pl.ds(0, ref.shape[1])], ref, sems.at[len(copies) + index]
+        )
+        piece.start()
+        pieces.append(piece)
+    for copy in copies[1:] + pieces:
         copy.wait()
 
 
@@ -1277,16 +1297,16 @@
         ((LAYERS, width), full),
     )
     far = pl.BlockSpec(memory_space=pl.ANY)
-    close = pl.BlockSpec(memory_space=pltpu.VMEM)
     return pl.pallas_call(
         functools.partial(place_kernel, sizes),
         name="place_outputs",
         out_shape=[jax.ShapeDtypeStruct(shape, kind) for shape, kind in shapes],
         in_specs=[far] * 3,
-        out_specs=[close if shape[0] == LAYERS and len(shape) == 2 else far for shape, _ in shapes],
+        out_specs=[far] * len(shapes),
         scratch_shapes=[
             pltpu.VMEM((CHUNK, width), full),
-            pltpu.SemaphoreType.DMA((5 + 4 * LAYERS,)),
+            pltpu.VMEM((8, LAYERS, width), full),
+            pltpu.SemaphoreType.DMA((13 + 4 * LAYERS,)),
         ],
         compiler_params=pltpu.CompilerParams(vmem_limit_bytes=4 << 20),
     )(hidden_out, grad_embeddings, every)

time: 321 us -> 318 us (level)
  Pallas kernels: 321 us -> 317 us
where the time goes in v8:
time: 318 us
  Pallas kernels  317 us (100%)
    pallas_call x1, Pallas kernels, run_pages(): pl.pallas_call(functools.partial(page_kernel, sizes), name='pages', out_s...  311 us

profile of v8, /device:TPU:0, one launch (start us, length us, event | category | flops | bytes accessed | tf_op | source)
XLA Modules:
  0.0 317.7 jit_solution(10545959597984220460)
XLA Ops:
  0.7 311.0 %pages.1 = (bf16[512,768]{1,0:T(8,128)(2,1)S(1)}, bf16[512,768]{1,0:T(8,128)(2,1)S(1)}, f32[4720,768]{1,0:T(8,128)S(1)}) custom-call(bf16[512,768]{1,0:T(8,128)(2,1)} %refs_0_.1, bf16[32,768]{1,0:T(8,128)(2,1)} %refs_1_.1, s32[1,512]{1,0:T(1,128)} %bitcast.6, s32[1,512]{1,0:T(1,128)} %bitcast.7, s32[1,512]{1,0:T(1,128)} %bitcast.8, ...), custom_call_target="tpu_custom_call" | custom-call | tf_op jit(solution)/shard_map/pages/pallas_call | solution.py:1123
  311.6 6.1 %place_outputs.1 = (bf16[512,768]{1,0:T(8,128)(2,1)}, bf16[512,768]{1,0:T(8,128)(2,1)}, f32[32,768]{1,0:T(8,128)}, f32[2,576,768]{2,1,0:T(8,128)}, f32[2,384]{1,...) custom-call(bf16[512,768]{1,0:T(8,128)(2,1)S(1)} %get-tuple-element., ...), custom_call_target="tpu_custom_call" | custom-call | tf_op jit(solution)/shard_map/place_outputs/pallas_call | solution.py:1300

commit v9 on v8

--- a/solution.py
+++ b/solution.py
@@ -30,9 +30,11 @@
 SHORT_CHUNKS = 3
 LAG = 2
 SLOTS = 4 * LAG
-EQUAL_SLOTS = 2 * LAG
-EQUALS = (TX, TA2, TQ1, TQ2, TR1, TR3, TTM, TG, TR5) = range(9)
-ONE_WAY = (TA1, TTA, TQ0, TR0, TR2, TTN, TTF, TR4, TR6) = range(9, 18)
+EQUAL_SLOTS = 3 * LAG
+EQUALS = (TA2, TQ1, TQ2, TR1, TR3, TTM, TG, TR5) = range(8)
+ONE_WAY = (TA1, TTA, TQ0, TR0, TTN, TR6) = range(8, 14)
+SHORT_WAY = (TR2, TTF, TR4) = range(14, 17)
+TX = 17
 WIDE_LANDINGS = (TX, TA1, TA2, TTA)
 NARROW_LANDINGS = (TQ1, TQ2, TR0, TR1, TR2, TR3)
 GROUP = 8
@@ -126,7 +128,7 @@
 
 
 class GradientSum:
-    def __init__(self, place, chunks, part, wide, both, narrow, send, recv, one_way):
+    def __init__(self, place, chunks, part, wide, both, narrow, send, recv, one_way, short_way, first_send, first_recv):
         self.place = place
         self.chunks = chunks
         self.part = part
@@ -136,6 +138,9 @@
         self.send = send
         self.recv = recv
         self.one_way = one_way
+        self.short_way = short_way
+        self.first_send = first_send
+        self.first_recv = first_recv
 
     def wide_rows(self, j, unit):
         return pl.ds(pl.multiple_of(j * CHUNK + unit * WIDE, NARROW), WIDE)
@@ -151,11 +156,17 @@
         near_end, far_end = 2 + place.upper, 3 - place.upper
 
         def copy(kind, j, rows, target, device):
-            if kind in EQUALS:
+            if kind == TX:
+                slot = lax.rem(j, SLOTS)
+                send, recv = self.first_send.at[slot], self.first_recv.at[slot]
+            elif kind in EQUALS:
                 slot = lax.rem(j, EQUAL_SLOTS)
                 send, recv = self.send.at[kind, slot], self.recv.at[kind, slot]
+            elif kind in ONE_WAY:
+                send = recv = self.one_way.at[kind - len(EQUALS), lax.rem(j, SLOTS)]
             else:
-                send = recv = self.one_way.at[kind - len(EQUALS), lax.rem(j, SLOTS)]
+                index = kind - len(EQUALS) - len(ONE_WAY)
+                send = recv = self.short_way.at[index, lax.rem(j, EQUAL_SLOTS)]
             return pltpu.make_async_remote_copy(
                 src_ref=part.at[rows],
                 dst_ref=target,
@@ -378,7 +389,7 @@
             pl.when(place.end)(lambda: ended(j, lambda: end_out(j).wait_recv()))
 
         stages = (stage_0, stage_1, stage_2, stage_3, stage_4, stage_5, stage_6, stage_7)
-        for number in reversed(range(len(stages))):
+        for number in range(len(stages)):
             j = t - number * LAG
             pl.when(jnp.logical_and(j >= 0, j < self.chunks))(
                 functools.partial(stages[number], j)
@@ -458,6 +469,9 @@
         dp_send,
         dp_recv,
         dp_one_way,
+        dp_short_way,
+        dp_first_send,
+        dp_first_recv,
         gather_send,
         gather_recv,
         hand_send,
@@ -474,12 +488,14 @@
     greet(place, barrier)
 
     def fetch(index):
-        return pltpu.make_async_copy(far[index], close[index], close_sem.at[index, 0])
+        return pltpu.make_async_copy(far[index], close[index], close_sem.at[index])
 
     def weight(which, layer):
         index = WEIGHTS[which]
         return pltpu.make_async_copy(
-            far[index].at[layer], close[index].at[layer], close_sem.at[index, layer]
+            far[index].at[layer],
+            close[index].at[layer],
+            close_sem.at[index + layer * (ARGS - index) + layer * which],
         )
 
     weight(1, 0).start()
@@ -491,7 +507,7 @@
     small_base = tail_base + CHUNK
     assert tail_base % CHUNK == 0 and span % HEAD_DIM == 0
     chunks = grads.shape[0] // CHUNK
-    grad_sum = GradientSum(place, chunks, grads, land_wide, land_both, land_narrow, dp_send, dp_recv, dp_one_way)
+    grad_sum = GradientSum(place, chunks, grads, land_wide, land_both, land_narrow, dp_send, dp_recv, dp_one_way, dp_short_way, dp_first_send, dp_first_recv)
     tick = grad_sum.tick
 
     def vector(ref, layer):
@@ -1181,13 +1197,16 @@
             dma((len(EQUALS), EQUAL_SLOTS)),
             dma((len(EQUALS), EQUAL_SLOTS)),
             dma((len(ONE_WAY), SLOTS)),
+            dma((len(SHORT_WAY), EQUAL_SLOTS)),
+            dma((SLOTS,)),
+            dma((SLOTS,)),
             dma((4 * LAYERS,)),
             dma((4 * LAYERS,)),
             dma((LAYERS, GROUP)),
             dma((LAYERS, GROUP)),
             dma((3, BLOCKS)),
             dma((3, BLOCKS)),
-            dma((ARGS, LAYERS)),
+            dma((ARGS + (LAYERS - 1) * len(WEIGHTS),)),
         ],
         compiler_params=pltpu.CompilerParams(
             collective_id=0, has_side_effects=True, vmem_limit_bytes=46 << 20

time: 318 us -> 316 us (level)
  no operation moved by 1% of the time
where the time goes in v9:
time: 316 us
  Pallas kernels  315 us (100%)
    pallas_call x1, Pallas kernels, run_pages(): pl.pallas_call(functools.partial(page_kernel, sizes), name='pages', out_s...  309 us

profile of v9, /device:TPU:0, one launch (start us, length us, event | category | flops | bytes accessed | tf_op | source)
XLA Modules:
  0.0 316.1 jit_solution(1069981662504837410)
XLA Ops:
  0.7 309.4 %pages.1 = (bf16[512,768]{1,0:T(8,128)(2,1)S(1)}, bf16[512,768]{1,0:T(8,128)(2,1)S(1)}, f32[4720,768]{1,0:T(8,128)S(1)}) custom-call(bf16[512,768]{1,0:T(8,128)(2,1)} %refs_0_.1, bf16[32,768]{1,0:T(8,128)(2,1)} %refs_1_.1, s32[1,512]{1,0:T(1,128)} %bitcast.6, s32[1,512]{1,0:T(1,128)} %bitcast.7, s32[1,512]{1,0:T(1,128)} %bitcast.8, ...), custom_call_target="tpu_custom_call" | custom-call | tf_op jit(solution)/shard_map/pages/pallas_call | solution.py:1139
  310.1 6.1 %place_outputs.1 = (bf16[512,768]{1,0:T(8,128)(2,1)}, bf16[512,768]{1,0:T(8,128)(2,1)}, f32[32,768]{1,0:T(8,128)}, f32[2,576,768]{2,1,0:T(8,128)}, f32[2,384]{1,...) custom-call(bf16[512,768]{1,0:T(8,128)(2,1)S(1)} %get-tuple-element., ...), custom_call_target="tpu_custom_call" | custom-call | tf_op jit(solution)/shard_map/place_outputs/pallas_call | solution.py:1319

commit v10 on v9

--- a/solution.py
+++ b/solution.py
@@ -31,10 +31,10 @@
 LAG = 2
 SLOTS = 4 * LAG
 EQUAL_SLOTS = 3 * LAG
-EQUALS = (TA2, TQ1, TQ2, TR1, TR3, TTM, TG, TR5) = range(8)
-ONE_WAY = (TA1, TTA, TQ0, TR0, TTN, TR6) = range(8, 14)
-SHORT_WAY = (TR2, TTF, TR4) = range(14, 17)
-TX = 17
+EQUALS = (TA2, TQ1, TQ2, TR1, TTM, TG, TR5) = range(7)
+ONE_WAY = (TA1, TTA, TQ0, TR0, TTN, TR6) = range(7, 13)
+SHORT_WAY = (TR2, TTF, TR4) = range(13, 16)
+TX, TR3 = 16, 17
 WIDE_LANDINGS = (TX, TA1, TA2, TTA)
 NARROW_LANDINGS = (TQ1, TQ2, TR0, TR1, TR2, TR3)
 GROUP = 8
@@ -159,9 +159,9 @@
             if kind == TX:
                 slot = lax.rem(j, SLOTS)
                 send, recv = self.first_send.at[slot], self.first_recv.at[slot]
-            elif kind in EQUALS:
-                slot = lax.rem(j, EQUAL_SLOTS)
-                send, recv = self.send.at[kind, slot], self.recv.at[kind, slot]
+            elif kind in EQUALS or kind == TR3:
+                slot, index = lax.rem(j, EQUAL_SLOTS), TQ2 if kind == TR3 else kind
+                send, recv = self.send.at[index, slot], self.recv.at[index, slot]
             elif kind in ONE_WAY:
                 send = recv = self.one_way.at[kind - len(EQUALS), lax.rem(j, SLOTS)]
             else:
@@ -804,15 +804,23 @@
             pl.when(jnp.logical_and(layer == 0, b == BLOCKS - 1))(lambda: gather_third(0))
             spans = halves(b, SEG)
             outs, logs = [], []
-            for h in range(local_heads):
-                query = jnp.concatenate([queries[layer, h, rows, :] for rows in spans], axis=0)
-                scores = scores_of(layer, h, query)
+            all_scores = [
+                scores_of(
+                    layer,
+                    h,
+                    jnp.concatenate([queries[layer, h, rows, :] for rows in spans], axis=0),
+                )
+                for h in range(local_heads)
+            ]
+            all_probs = []
+            for scores in all_scores:
                 largest = jnp.max(scores, axis=-1, keepdims=True)
                 weights_of = jnp.exp(scores - largest)
                 totals = jnp.sum(weights_of, axis=-1, keepdims=True)
-                probs = (weights_of * (1.0 / totals)).astype(jnp.bfloat16)
+                all_probs.append((weights_of * (1.0 / totals)).astype(jnp.bfloat16))
+                logs.append(largest + jnp.log(totals))
+            for h, probs in enumerate(all_probs):
                 outs.append(matmul(probs, values[layer, h]).astype(jnp.bfloat16))
-                logs.append(largest + jnp.log(totals))
             joined = jnp.concatenate(outs, axis=1)
             full = joined.astype(jnp.float32)
             for side in range(2):

time: 316 us -> 316 us (level)
  no operation moved by 1% of the time
where the time goes in v10:
time: 316 us
  Pallas kernels  315 us (100%)
    pallas_call x1, Pallas kernels, run_pages(): pl.pallas_call(functools.partial(page_kernel, sizes), name='pages', out_s...  309 us

profile of v10, /device:TPU:0, one launch (start us, length us, event | category | flops | bytes accessed | tf_op | source)
XLA Modules:
  0.0 315.5 jit_solution(7999767358054481797)
XLA Ops:
  0.7 308.8 %pages.1 = (bf16[512,768]{1,0:T(8,128)(2,1)S(1)}, bf16[512,768]{1,0:T(8,128)(2,1)S(1)}, f32[4720,768]{1,0:T(8,128)S(1)}) custom-call(bf16[512,768]{1,0:T(8,128)(2,1)} %refs_0_.1, bf16[32,768]{1,0:T(8,128)(2,1)} %refs_1_.1, s32[1,512]{1,0:T(1,128)} %bitcast.6, s32[1,512]{1,0:T(1,128)} %bitcast.7, s32[1,512]{1,0:T(1,128)} %bitcast.8, ...), custom_call_target="tpu_custom_call" | custom-call | tf_op jit(solution)/shard_map/pages/pallas_call | solution.py:1147
  309.4 6.1 %place_outputs.1 = (bf16[512,768]{1,0:T(8,128)(2,1)}, bf16[512,768]{1,0:T(8,128)(2,1)}, f32[32,768]{1,0:T(8,128)}, f32[2,576,768]{2,1,0:T(8,128)}, f32[2,384]{1,...) custom-call(bf16[512,768]{1,0:T(8,128)(2,1)S(1)} %get-tuple-element., ...), custom_call_target="tpu_custom_call" | custom-call | tf_op jit(solution)/shard_map/place_outputs/pallas_call | solution.py:1327

commit v11 on v10

--- a/solution.py
+++ b/solution.py
@@ -328,12 +328,12 @@
             def _():
                 ended(j, lambda: end_up(j).wait_send())
                 mine_across(j).wait()
+                add_wide(TA2, j, mine)
+                mine_out(j).start()
                 near_pair(j).wait()
                 add_narrow(TQ2, j, near)
                 near_across(j).start()
                 near_out(j).start()
-                add_wide(TA2, j, mine)
-                mine_out(j).start()
 
         def stage_4(j):
             @pl.when(place.mid)

time: 316 us -> 316 us (level)
  no operation moved by 1% of the time
where the time goes in v11:
time: 316 us
  Pallas kernels  315 us (100%)
    pallas_call x1, Pallas kernels, run_pages(): pl.pallas_call(functools.partial(page_kernel, sizes), name='pages', out_s...  309 us

profile of v11, /device:TPU:0, one launch (start us, length us, event | category | flops | bytes accessed | tf_op | source)
XLA Modules:
  0.0 315.5 jit_solution(10486250116034580455)
XLA Ops:
  0.7 308.8 %pages.1 = (bf16[512,768]{1,0:T(8,128)(2,1)S(1)}, bf16[512,768]{1,0:T(8,128)(2,1)S(1)}, f32[4720,768]{1,0:T(8,128)S(1)}) custom-call(bf16[512,768]{1,0:T(8,128)(2,1)} %refs_0_.1, bf16[32,768]{1,0:T(8,128)(2,1)} %refs_1_.1, s32[1,512]{1,0:T(1,128)} %bitcast.6, s32[1,512]{1,0:T(1,128)} %bitcast.7, s32[1,512]{1,0:T(1,128)} %bitcast.8, ...), custom_call_target="tpu_custom_call" | custom-call | tf_op jit(solution)/shard_map/pages/pallas_call | solution.py:1147
  309.4 6.1 %place_outputs.1 = (bf16[512,768]{1,0:T(8,128)(2,1)}, bf16[512,768]{1,0:T(8,128)(2,1)}, f32[32,768]{1,0:T(8,128)}, f32[2,576,768]{2,1,0:T(8,128)}, f32[2,384]{1,...) custom-call(bf16[512,768]{1,0:T(8,128)(2,1)S(1)} %get-tuple-element., ...), custom_call_target="tpu_custom_call" | custom-call | tf_op jit(solution)/shard_map/place_outputs/pallas_call | solution.py:1327
